TPU v7x, 32 devices: a whole 2x2x4 slice. The times are simulated.
32 devices in a mesh: seq: 2 (over y), dp: 16 (over z, x, core).
Axes of the slice: x: 2, y: 2, z: 4, core: 2. Of those that a mesh axis runs over, the one named last changes fastest.
Arguments:
- tokens: bfloat16 [16, 2560, 768], P('dp', 'seq'), may hold values from -6 to 6
- cotangent: bfloat16 [16, 2560, 768], P('dp', 'seq'), may hold values from -6 to 6
- lengths: int32 [16, 5], P('dp'), may hold values from 0 to 2048, as said below
- threshold: int32 [1], replicated, may hold values from 0 to 1023
- attn_gain: float32 [768], replicated, may hold values from 0.25 to 1.75
- qkv_weight: bfloat16 [768, 2304], replicated, may hold values from -0.21875 to 0.21875
- out_weight: bfloat16 [768, 768], replicated, may hold values from -1 to 1
- mlp_gain: float32 [768], replicated, may hold values from 0.25 to 1.75
- up_weight: bfloat16 [768, 3072], replicated, may hold values from -0.21875 to 0.21875
- down_weight: bfloat16 [3072, 768], replicated, may hold values from -0.109375 to 0.109375
Outputs:
- output: bfloat16 [16, 2560, 768], P('dp', 'seq')
- input_grad: bfloat16 [16, 2560, 768], P('dp', 'seq')
- attn_gain_grad: float32 [768], P('dp')
- qkv_weight_grad: float32 [768, 2304], P('dp')
- out_weight_grad: float32 [768, 768], P('dp')
- mlp_gain_grad: float32 [768], P('dp')
- up_weight_grad: float32 [768, 3072], P('dp')
- down_weight_grad: float32 [3072, 768], P('dp')
- excess: float32 [1], replicated
Inputs may be any that keep to these rules, and one draw needn't show every extreme that they name: `lengths`: each row is either 2048 and 512 in some order followed by three zeros, or 512 five times; every row sums to 2560; row 0 holds a sequence of 2048.
All inputs are finite; a program needn't handle non-finite values.
Results may differ from a plain program's by a relative error of at most 0.014.
Values may be sent and summed in bfloat16 or wider, within the bound.
No kernel may reach another device: no remote copies, remote signals or barrier semaphores. Data moves between devices by JAX's collectives and lax.ppermute only.
A program may use at most 448 MiB of HBM per device.

v0:
```python
import jax
import jax.numpy as jnp
from jax import lax
from jax.sharding import PartitionSpec as P

HEADS = 12
HEAD_DIM = 64


LN_EPS = 1e-05
GELU_C = 0.7978845608028654


def from_behind(block, axis, distance):
    devices = range(lax.axis_size(axis))
    route = [(i - distance, i) for i in devices if i - distance in devices]
    return lax.ppermute(block, axis, route)


def shifted_2(array, axis, by):
    size = lax.axis_size(axis)
    return lax.ppermute(array, axis, [(i, (i + by) % size) for i in range(size)])


def for_sending(array):

    def short(part):
        return part.astype(jnp.bfloat16) if part.dtype == jnp.float32 else part

    return jax.tree.map(short, array)


def layer_norm(values, gain):
    centre = jnp.mean(values, axis=-1, keepdims=True)
    shifted = values - centre
    spread = jnp.mean(shifted * shifted, axis=-1, keepdims=True)
    return shifted * lax.rsqrt(spread + LN_EPS) * gain


def gelu_tanh(values):
    return 0.5 * values * (1.0 + jnp.tanh(GELU_C * (values + 0.044715 * values * values * values)))


def seg_info(lengths, positions):
    seg_ends = jnp.cumsum(lengths, axis=1)
    segment = jnp.sum((positions[None, :, None] >= seg_ends[:, None, :]).astype(jnp.int32), axis=2)
    slot_ids = jnp.arange(lengths.shape[1], dtype=jnp.int32)
    seg_len = jnp.sum(
        jnp.where(segment[:, :, None] == slot_ids[None, None, :], lengths[:, None, :], 0), axis=2
    )
    return (segment, 4.0 / seg_len.astype(jnp.float32))


def pair_terms(queries, key_vals, q_seg, q_pos, k_seg, k_pos, q_rate, carried):
    packs, block_len, heads, head_dim = queries.shape
    width = heads * head_dim
    key_rows = key_vals[:, :, :width].reshape(packs, block_len, heads, head_dim)
    values = key_vals[:, :, width:].reshape(packs, block_len, heads, head_dim)
    scores = jnp.einsum(
        "sqhe,skhe->shqk", queries, key_rows, preferred_element_type=jnp.float32
    ) * head_dim ** (-0.5)
    same_seg = q_seg[:, :, None] == k_seg[:, None, :]
    allowed = same_seg & (k_pos[None, None, :] <= q_pos[None, :, None])
    strict = same_seg & (k_pos[None, None, :] < q_pos[None, :, None])
    chosen = jnp.where(strict, jnp.maximum(scores[:, 0], 0.0), 0.0)
    earlier_sum = jnp.cumsum(chosen, axis=1) - chosen
    penalty = q_rate[:, :, None] * (carried[:, None, :] + earlier_sum)
    numerators = jnp.where(allowed[:, None], jnp.exp(scores - penalty[:, None]), 0.0)
    return (key_rows, values, scores, strict, chosen, numerators)


def on_device(
    tokens,
    cotangent,
    lengths,
    threshold,
    attn_gain,
    qkv_weight,
    out_weight,
    mlp_gain,
    up_weight,
    down_weight,
):
    packs, block_len, model_width = tokens.shape
    seq_count = lax.axis_size("seq")
    seq_pos = lax.axis_index("seq")
    score_scale = HEAD_DIM ** (-0.5)
    row_ids = jnp.arange(block_len, dtype=jnp.int32)
    q_pos = seq_pos * block_len + row_ids
    q_seg, q_rate = seg_info(lengths, q_pos)
    token_vals = tokens.astype(jnp.float32)
    normed = layer_norm(token_vals, attn_gain)
    normed_low = normed.astype(jnp.bfloat16)
    qkv = jnp.einsum(
        "sbd,dc->sbc", normed_low, qkv_weight, preferred_element_type=jnp.float32
    ).astype(jnp.bfloat16)
    queries = qkv[:, :, :model_width].reshape(packs, block_len, HEADS, HEAD_DIM)
    own_kv = qkv[:, :, model_width:]

    def block_info(key_block):
        k_pos = key_block * block_len + row_ids
        k_seg, k_rate = seg_info(lengths, k_pos)
        active = (key_block == seq_pos) | (key_block < seq_pos) & jnp.any(
            q_seg[:, 0] == k_seg[:, block_len - 1]
        )
        return (k_pos, k_seg, k_rate, active)

    def visit(visit_step, key_vals, carried, numer_sum, totals, kept_sums):
        key_block = (seq_pos - visit_step) % seq_count
        k_pos, k_seg, k_rate, active = block_info(key_block)
        kept_sums = lax.dynamic_update_index_in_dim(kept_sums, carried, key_block, 0)

        def attend(loop_state):
            carried_in, numer_in, totals_in = loop_state
            key_rows, values, scores, strict, chosen, numerators = pair_terms(
                queries, key_vals, q_seg, q_pos, k_seg, k_pos, q_rate, carried_in
            )
            numer_out = numer_in + jnp.einsum(
                "shqk,skhe->sqhe",
                numerators.astype(jnp.bfloat16),
                values,
                preferred_element_type=jnp.float32,
            )
            totals_out = totals_in + jnp.sum(numerators, axis=3)
            return (carried_in + jnp.sum(chosen, axis=1), numer_out, totals_out)

        carried, numer_sum, totals = lax.cond(
            active, attend, lambda loop_state: loop_state, (carried, numer_sum, totals)
        )
        return (carried, numer_sum, totals, kept_sums)

    def forward_turn(visit_step, loop_state):
        key_vals, carried, numer_sum, totals, kept_sums = loop_state
        carried, numer_sum, totals, kept_sums = visit(
            visit_step, key_vals, carried, numer_sum, totals, kept_sums
        )
        key_vals = from_behind(key_vals, "seq", 1)
        carried = shifted_2(carried, "seq", 1)
        return (key_vals, carried, numer_sum, totals, kept_sums)

    start = (
        own_kv,
        jnp.zeros((packs, block_len), jnp.float32),
        jnp.zeros((packs, block_len, HEADS, HEAD_DIM), jnp.float32),
        jnp.zeros((packs, HEADS, block_len), jnp.float32),
        jnp.zeros((seq_count, packs, block_len), jnp.float32),
    )
    loop_state = lax.fori_loop(0, seq_count - 1, forward_turn, start)
    carried, numer_sum, totals, kept_sums = visit(seq_count - 1, *loop_state)
    last_pos, last_seg, last_rate, last_active = block_info((seq_pos + 1) % seq_count)
    limit = threshold[0].astype(jnp.float32) / 1024.0
    excess_part = jnp.sum(jnp.maximum(last_rate * carried - limit, 0.0))
    row_totals = jnp.transpose(totals, (0, 2, 1))[..., None]
    attended4 = numer_sum / row_totals
    attended_low = attended4.reshape(packs, block_len, model_width).astype(jnp.bfloat16)
    residual = token_vals + jnp.einsum(
        "sbd,de->sbe", attended_low, out_weight, preferred_element_type=jnp.float32
    )
    normed_mlp = layer_norm(residual, mlp_gain).astype(jnp.bfloat16)
    pre = jnp.einsum("sbd,df->sbf", normed_mlp, up_weight, preferred_element_type=jnp.float32)
    hidden = gelu_tanh(pre).astype(jnp.bfloat16)
    output = (
        residual
        + jnp.einsum("sbf,fd->sbd", hidden, down_weight, preferred_element_type=jnp.float32)
    ).astype(jnp.bfloat16)
    down_grad = jnp.einsum("sbf,sbd->fd", hidden, cotangent, preferred_element_type=jnp.float32)
    d_hidden = jnp.einsum("sbd,fd->sbf", cotangent, down_weight, preferred_element_type=jnp.float32)
    gelu_out, gelu_pull = jax.vjp(gelu_tanh, pre)
    d_pre = gelu_pull(d_hidden)[0].astype(jnp.bfloat16)
    up_grad = jnp.einsum("sbd,sbf->df", normed_mlp, d_pre, preferred_element_type=jnp.float32)
    d_normed_mlp = jnp.einsum("sbf,df->sbd", d_pre, up_weight, preferred_element_type=jnp.float32)
    norm_out, mlp_pull = jax.vjp(layer_norm, residual, mlp_gain)
    d_res_norm, mlp_gain_grad = mlp_pull(d_normed_mlp)
    d_residual = cotangent.astype(jnp.float32) + d_res_norm
    d_branch = d_residual.astype(jnp.bfloat16)
    out_grad = jnp.einsum("sbd,sbe->de", attended_low, d_branch, preferred_element_type=jnp.float32)
    d_attended = jnp.einsum(
        "sbe,de->sbd", d_branch, out_weight, preferred_element_type=jnp.float32
    ).astype(jnp.bfloat16)
    d_att4 = d_attended.reshape(packs, block_len, HEADS, HEAD_DIM)
    d_att_vals = d_att4.astype(jnp.float32)
    row_dots = jnp.transpose(jnp.sum(d_att_vals * attended4, axis=3), (0, 2, 1))
    scaled_grad = d_att_vals / row_totals
    scaled_hi = scaled_grad.astype(jnp.bfloat16)
    scaled_lo = (scaled_grad - scaled_hi.astype(jnp.float32)).astype(jnp.bfloat16)

    def back_turn(visit_step, loop_state):
        key_vals, grad_kv, grad_sel, grad_query = loop_state
        key_vals = shifted_2(key_vals, "seq", -1)
        grad_kv, grad_sel = (
            from_behind(grad_kv.astype(jnp.bfloat16), "seq", -1).astype(grad_kv.dtype),
            from_behind(grad_sel.astype(jnp.bfloat16), "seq", -1).astype(grad_sel.dtype),
        )
        key_block = (seq_pos + 1 + visit_step) % seq_count
        k_pos, k_seg, k_rate, active = block_info(key_block)
        carried_in = lax.dynamic_index_in_dim(kept_sums, key_block, 0, keepdims=False)

        def revisit(acc_state):
            kv_grad_in, sel_in, query_in = acc_state
            key_rows, values, scores, strict, chosen, numerators = pair_terms(
                queries, key_vals, q_seg, q_pos, k_seg, k_pos, q_rate, carried_in
            )
            softmax_w = numerators / totals[:, :, :, None]
            d_probs = jnp.einsum(
                "sqhe,skhe->shqk", d_att4, values, preferred_element_type=jnp.float32
            )
            d_logit = softmax_w * (d_probs - row_dots[:, :, :, None])
            d_penalty = -jnp.sum(d_logit, axis=1)
            later_sum = lax.cumsum(d_penalty, axis=1, reverse=True) - d_penalty
            d_chosen = jnp.where(
                strict & (scores[:, 0] > 0.0),
                q_rate[:, :, None] * (sel_in[:, None, :] + later_sum),
                0.0,
            )
            d_scores = jnp.concatenate(
                [d_logit[:, :1] + d_chosen[:, None], d_logit[:, 1:]], axis=1
            ).astype(jnp.bfloat16)
            query_out = (
                query_in
                + jnp.einsum(
                    "shqk,skhe->sqhe", d_scores, key_rows, preferred_element_type=jnp.float32
                )
                * score_scale
            )
            d_keys = (
                jnp.einsum("shqk,sqhe->skhe", d_scores, queries, preferred_element_type=jnp.float32)
                * score_scale
            )
            numer_low = numerators.astype(jnp.bfloat16)
            d_values = jnp.einsum(
                "shqk,sqhe->skhe", numer_low, scaled_hi, preferred_element_type=jnp.float32
            ) + jnp.einsum(
                "shqk,sqhe->skhe", numer_low, scaled_lo, preferred_element_type=jnp.float32
            )
            kv_grad_out = kv_grad_in + jnp.concatenate(
                [
                    d_keys.reshape(packs, block_len, model_width),
                    d_values.reshape(packs, block_len, model_width),
                ],
                axis=2,
            )
            return (kv_grad_out, sel_in + jnp.sum(d_penalty, axis=1), query_out)

        grad_kv, grad_sel, grad_query = lax.cond(
            active, revisit, lambda acc_state: acc_state, (grad_kv, grad_sel, grad_query)
        )
        return (key_vals, grad_kv, grad_sel, grad_query)

    back_start = (
        own_kv,
        jnp.zeros((packs, block_len, 2 * model_width), jnp.float32),
        jnp.zeros((packs, block_len), jnp.float32),
        jnp.zeros((packs, block_len, HEADS, HEAD_DIM), jnp.float32),
    )
    final_kv, grad_kv, grad_sel, grad_query = lax.fori_loop(0, seq_count, back_turn, back_start)
    d_qkv = jnp.concatenate(
        [grad_query.reshape(packs, block_len, model_width), grad_kv], axis=2
    ).astype(jnp.bfloat16)
    qkv_grad = jnp.einsum("sbd,sbc->dc", normed_low, d_qkv, preferred_element_type=jnp.float32)
    d_normed = jnp.einsum("sbc,dc->sbd", d_qkv, qkv_weight, preferred_element_type=jnp.float32)
    attn_out, attn_pull = jax.vjp(layer_norm, token_vals, attn_gain)
    d_tok_norm, attn_gain_grad = attn_pull(d_normed)
    input_grad = (d_residual + d_tok_norm).astype(jnp.bfloat16)
    dp_count = lax.axis_size("dp")
    local_grads = (attn_gain_grad, qkv_grad, out_grad, mlp_gain_grad, up_grad, down_grad)
    arranged = tuple(
        (
            jnp.transpose(grad.reshape(dp_count, seq_count, -1), (1, 0, 2)).reshape(-1)
            for grad in local_grads
        )
    )
    pieces = lax.psum_scatter(arranged, ("seq", "dp"), scatter_dimension=0, tiled=True)
    joined = jax.tree.map(
        lambda part, own: part.astype(own.dtype),
        lax.all_gather(for_sending(pieces), "seq", axis=0, tiled=True),
        pieces,
    )
    summed = tuple(
        (
            part.reshape((grad.shape[0] // dp_count,) + grad.shape[1:])
            for part, grad in zip(joined, local_grads)
        )
    )
    excess_sum = lax.psum(excess_part, ("seq", "dp"))
    excess = (excess_sum / (packs * dp_count * block_len * seq_count)).reshape(1)
    return (
        output,
        input_grad,
        summed[0],
        summed[1],
        summed[2],
        summed[3],
        summed[4],
        summed[5],
        excess,
    )


def solution(mesh):
    return jax.shard_map(
        on_device,
        mesh=mesh,
        in_specs=(
            P("dp", "seq", None),
            P("dp", "seq", None),
            P("dp", None),
            P(),
            P(),
            P(),
            P(),
            P(),
            P(),
            P(),
        ),
        out_specs=(
            P("dp", "seq", None),
            P("dp", "seq", None),
            P("dp"),
            P("dp", None),
            P("dp", None),
            P("dp"),
            P("dp", None),
            P("dp", None),
            P(),
        ),
        check_vma=False,
    )
```

profile of v0, /device:TPU:0, one launch (start us, length us, event | category | flops | bytes accessed | tf_op | source)
XLA Modules:
  0.0 2206.6 jit_solution(7601092934014917244)
XLA Ops:
  9.4 7.3 fusion.73
  21.4 6.8 collective-permute-start.4
  44.3 150.1 %conditional.3 = (f32[1,1280]{1,0:T(1,128)}, f32[1,1280,12,64]{1,3,2,0:T(8,128)}, f32[1,12,1280]{2,1,0:T(8,128)}) conditional(s32[]{:T(128)} %convert_element_type.311, (f32[1,1280]{1,0:T(1,128)}, f32[1,1280,12,64]{1,3,2,0:T(8,128)}, f32[1,12,1280]{2,1,0:T(8,128)}) %tuple.58, (s32[1,1280]{1,0:T(1,128)S(1)}, s32[1,1280]{1,0:T(1,128)}, s32[]{:T(128)}, ...), branch_computations={%region_7.8_spmd, %region_8.13_spmd} | conditional | flops 5401277440 | bytes 343152672 | solution.py:127
  50.8 6.3 copy.115
  61.5 29.8 %convolution_multiply_fusion = f32[12,1280,1280]{2,1,0:T(8,128)} fusion(bf16[1280,12,64]{0,2,1:T(8,128)(2,1)} %bitcast.315, bf16[1,1280,12,64]{1,3,2,0:T(8,128)(2,1)} %get-tuple-element.628), kind=kOutput, calls=%fused_computation.2 | convolution fusion | flops 2536243200 | bytes 82575360 | tf_op jit(solution)/shard_map/while/body/eval_jaxpr/cond/branch_1_fun/sqhe,skhe->shqk/dot_general | solution.py:59
  98.8 10.7 fusion.9
  111.0 10.6 copy.106
  124.0 8.6 fusion.15
  132.6 32.2 %bitcast_add_fusion.1 = f32[1,1280,12,64]{1,3,2,0:T(8,128)} fusion(f32[1,1280,12,64]{1,3,2,0:T(8,128)} %get-tuple-element.630, bf16[1280,12,64]{0,2,1:T(8,128)(2,1)} %bitcast.320, f32[12,1280,1280]{2,1,0:T(8,128)} %convolution_multiply_fusion, f32[1280,1280]{1,0:T(8,128)} %fusion.15, pred[1280,1280]{1,0:T(8,128)(4,1)} %compare_and_fusion), kind=kOutput, calls=%fused_computation.19 | convolution fusion | flops 2576547840 | bytes 96665600 | tf_op jit(solution)/shard_map/while/body/eval_jaxpr/cond/branch_1_fun/shqk,skhe->sqhe/dot_general | solution.py:118
  164.8 27.7 %fusion.4 = f32[12,1280]{1,0:T(8,128)} fusion(f32[12,1280,1280]{2,1,0:T(8,128)} %convolution_multiply_fusion, f32[1280,1280]{1,0:T(8,128)} %fusion.15, pred[1280,1280]{1,0:T(8,128)(4,1)} %compare_and_fusion), kind=kLoop, calls=%fused_computation.4 | loop fusion | flops 58967040 | bytes 86896640 | tf_op jit(solution)/shard_map/while/body/eval_jaxpr/cond/branch_1_fun/reduce_sum | solution.py:124
  197.0 6.3 copy.119
  223.1 12.8 fusion.114
  235.8 13.8 fusion.87
  249.7 20.2 fusion.70
  269.9 14.1 fusion.95
  284.0 9.6 fusion.85
  293.6 9.0 fusion.112
  309.6 6.5 subtract_convert_fusion
  319.7 1249.1 %while.15 = (s32[]{:T(128)}, bf16[1,1280,1536]{1,2,0:T(8,128)(2,1)}, f32[1,1280,1536]{1,2,0:T(8,128)}, f32[1,1280]{1,0:T(1,128)}, f32[1,1280,12,64]{1,3,2,0:T(8,...) while((s32[]{:T(128)}, ...), condition=%wide.region_34.35_spmd.clone.clone, body=%wide.region_24.34_spmd.clone.clone.sunk | while | flops 15950430208 | bytes 860509056 | solution.py:255
  326.8 151.6 %collective-permute-start = (bf16[1,1280,1536]{1,2,0:T(8,128)(2,1)}, bf16[1,1280,1536]{1,2,0:T(8,128)(2,1)}, u32[]{:S(2)}, u32[]{:S(2)}) collective-permute-start(bf16[1,1280,1536]{1,2,0:T(8,128)(2,1)} %get-tuple-element.1291), channel_id=1, source_target_pairs={{0,16},{16,0},{1,17},{17,1},{2,18},{18,2},{3,19},{19,3},{4,20},{20... | collective-permute-start | bytes 11796488 | tf_op jit(solution)/shard_map/while/body/eval_jaxpr/ppermute | solution.py:22
  484.8 160.8 %collective-permute-done.2 = bf16[1,1280]{1,0:T(2,128)(2,1)} collective-permute-done((bf16[1,1280]{1,0:T(2,128)(2,1)}, bf16[1,1280]{1,0:T(2,128)(2,1)}, u32[]{:S(2)}, u32[]{:S(2)}) %collective-permute-start.2) | collective-permute-done | bytes 2592 | tf_op jit(solution)/shard_map/while/body/eval_jaxpr/ppermute | solution.py:17
  665.9 359.5 %collective-permute-start = (bf16[1,1280,1536]{1,2,0:T(8,128)(2,1)}, bf16[1,1280,1536]{1,2,0:T(8,128)(2,1)}, u32[]{:S(2)}, u32[]{:S(2)}) collective-permute-start(bf16[1,1280,1536]{1,2,0:T(8,128)(2,1)} %get-tuple-element.1291), channel_id=1, source_target_pairs={{0,16},{16,0},{1,17},{17,1},{2,18},{18,2},{3,19},{19,3},{4,20},{20... | collective-permute-start | bytes 11796488 | tf_op jit(solution)/shard_map/while/body/eval_jaxpr/ppermute | solution.py:22
  1031.9 160.1 %collective-permute-done.2 = bf16[1,1280]{1,0:T(2,128)(2,1)} collective-permute-done((bf16[1,1280]{1,0:T(2,128)(2,1)}, bf16[1,1280]{1,0:T(2,128)(2,1)}, u32[]{:S(2)}, u32[]{:S(2)}) %collective-permute-start.2) | collective-permute-done | bytes 2592 | tf_op jit(solution)/shard_map/while/body/eval_jaxpr/ppermute | solution.py:17
  1199.7 358.4 %conditional.8 = ((f32[1,1280,1536]{1,2,0:T(8,128)}, f32[1,1280]{1,0:T(1,128)}, f32[1,1280,12,64]{1,3,2,0:T(8,128)})) conditional(s32[]{:T(128)} %convert_element_type.473, (f32[1,1280,1536]{1,2,0:T(8,128)}, f32[1,1280]{1,0:T(1,128)}, f32[1,1280,12,64]{1,3,2,0:T(8,128)}) %tuple.128, (s32[1,1280]{1,0:T(1,128)S(1)}, s32[1,1280]{1,0:T(1,128)}, ...), branch_computations={%region_26.26_spmd, %region_27.33_spmd} | conditional | flops 15946476544 | bytes 797435008 | solution.py:244
  1211.3 29.8 %convolution_multiply_fusion.2 = f32[12,1280,1280]{2,1,0:T(8,128)} fusion(bf16[1280,12,64]{0,2,1:T(8,128)(2,1)} %bitcast.304, bf16[1,1280,12,64]{1,3,2,0:T(8,128)(2,1)} %get-tuple-element.650), kind=kOutput, calls=%fused_computation.53 | convolution fusion | flops 2536243200 | bytes 82575360 | tf_op jit(solution)/shard_map/while/body/eval_jaxpr/cond/branch_1_fun/sqhe,skhe->shqk/dot_general | solution.py:59
  1247.0 10.7 fusion.43
  1259.2 10.5 copy.110
  1272.1 11.2 fusion.51
  1283.3 31.2 %fusion.55 = f32[12,1280,64]{1,2,0:T(8,128)} fusion(bf16[1,1280,12,64]{1,3,2,0:T(8,128)(2,1)} %get-tuple-element.659, f32[12,1280,1280]{2,1,0:T(8,128)} %convolution_multiply_fusion.2, f32[1280,1280]{1,0:T(8,128)} %fusion.51, pred[1280,1280]{1,0:T(8,128)(4,1)} %compare_and_fusion.3), kind=kOutput, calls=%fused_computation.88 | convolution fusion | flops 2575564800 | bytes 92733440 | tf_op jit(solution)/shard_map/while/body/eval_jaxpr/cond/branch_1_fun/shqk,sqhe->skhe/dot_general | solution.py:230
  1314.5 32.6 %convolution_add_fusion = f32[12,1280,64]{1,2,0:T(8,128)} fusion(f32[12,1280,64]{1,2,0:T(8,128)} %fusion.55, bf16[1,1280,12,64]{1,3,2,0:T(8,128)(2,1)} %get-tuple-element.660, f32[12,1280,1280]{2,1,0:T(8,128)} %convolution_multiply_fusion.2, f32[1280,1280]{1,0:T(8,128)} %fusion.51, pred[1280,1280]{1,0:T(8,128)(4,1)} %compare_and_fusion.3), kind=kOutput, calls=%fused_computation.85 | convolution fusion | flops 2576547840 | bytes 96665600 | tf_op jit(solution)/shard_map/while/body/eval_jaxpr/cond/branch_1_fun/shqk,sqhe->skhe/dot_general | solution.py:232
  1347.1 68.9 %fusion.116 = (f32[1280]{0:T(1024)S(1)}, f32[1280,1280]{1,0:T(8,128)}, f32[12,1280,1280]{2,1,0:T(8,128)}) fusion(f32[12,1280]{1,0:T(8,128)} %bitcast.328, bf16[1280,12,64]{0,2,1:T(8,128)(2,1)} %bitcast.308, bf16[1,1280,12,64]{1,3,2,0:T(8,128)(2,1)} %get-tuple-element.656, f32[12,1280]{1,0:T(8,128)} %bitcast.46, ...), kind=kOutput, calls=%fused_computation.207 | convolution fusion | flops 2652568320 | bytes 176092160 | tf_op jit(solution)/shard_map/while/body/eval_jaxpr/cond/branch_1_fun/sqhe,skhe->shqk/dot_general | solution.py:204
  1421.2 28.7 %fusion.41 = f32[1,1280,10,128]{1,2,3,0:T(8,128)} fusion(f32[1,1280,10,128]{1,3,2,0:T(8,128)S(1)} %bitcast.300), kind=kOutput, calls=%fused_computation.62 | output fusion | flops 208076800 | bytes 13107200 | tf_op jit(solution)/shard_map/reduce-window.10
  1451.5 10.6 copy.112
  1464.5 12.0 fusion.45
  1476.5 34.7 %fusion.38 = bf16[11,1280,1280]{2,1,0:T(8,128)(2,1)} fusion(f32[1,12,1280,1280]{3,2,1,0:T(8,128)} %bitcast.50), kind=kLoop, calls=%fused_computation.59 | loop fusion | bytes 72089600 | tf_op jit(solution)/shard_map/while/body/eval_jaxpr/cond/branch_1_fun/concatenate | solution.py:215
  1511.2 20.8 bitcast_add_fusion.8
  1532.1 16.2 fusion.52
  1548.3 9.6 maximum_add_fusion
  1575.2 7.2 fusion.84
  1582.5 8.7 fusion.88
  1595.1 15.5 reshape.1912
  1610.6 9.1 copy.125
  1625.0 15.9 reshape.1908
  1640.9 9.1 copy.124
  1674.0 13.3 reshape.1898
  1687.3 7.1 copy.121
  1706.0 457.3 %all-reduce.11 = (bf16[1769472]{0:T(1024)(128)(2,1)}, bf16[589824]{0:T(1024)(128)(2,1)}, bf16[2359296]{0:T(1024)(128)(2,1)}, bf16[2359296]{0:T(1024)(128)(2,1)},...) all-reduce(f32[1769472]{0:T(1024)} %bitcast.313, ...), channel_id=3, replica_groups=mesh['seq'=2,'dp'=16] {'seq','dp'}, use_global_device_ids=true, to_apply=%region_39.40.clone | all-reduce | flops 7079425 | bytes 42476552
  2185.2 7.4 all_gather.23
  (255 shorter events, 247.0 us)
Async XLA Ops:
  0.6 8.7 copy-start
  0.7 8.7 copy-start.37
  6.7 10.0 copy-start.26
  9.4 7.3 copy-start.28
  16.7 2.5 copy-start.11
  19.2 11.9 copy-start.42
  21.4 192.9 %collective-permute-start.4 = (bf16[1,1280,1536]{2,1,0:T(8,128)(2,1)}, bf16[1,1280,1536]{2,1,0:T(8,128)(2,1)}, u32[]{:S(2)}, u32[]{:S(2)}) collective-permute-start(bf16[1,1280,1536]{2,1,0:T(8,128)(2,1)} %slice.137), channel_id=1, source_target_pairs={{0,16},{1,17},{2,18},{3,19},{4,20},{5,21},{6,22},{7,23},{8,24},{9,... | collective-permute-start | bytes 11796488 | tf_op jit(solution)/shard_map/while/body/eval_jaxpr/ppermute | solution.py:17
  194.4 18.6 collective-permute-start.3
  217.6 2.8 copy-start.3
  217.6 3.1 copy-start.43
  217.6 5.4 slice-start
  235.8 13.8 copy-start.19
  303.8 4.1 copy-start.6
  303.8 4.1 copy-start.32
  304.7 3.2 copy-start.44
  309.6 6.5 copy-start.18
  320.0 5.5 copy-start.23
  320.0 333.3 %copy-start.21 = (s32[1,1280]{1,0:T(1,128)}, s32[1,1280]{1,0:T(1,128)S(1)}, u32[]{:S(2)}) copy-start(s32[1,1280]{1,0:T(1,128)S(1)} %get-tuple-element.1319) | copy-start | bytes 15364 | tf_op jit(solution)/shard_map/while
  325.5 321.4 %collective-permute-start.1 = (bf16[1,1280,1536]{1,2,0:T(8,128)(2,1)}, bf16[1,1280,1536]{1,2,0:T(8,128)(2,1)}, u32[]{:S(2)}, u32[]{:S(2)}) collective-permute-start(bf16[1,1280,1536]{1,2,0:T(8,128)(2,1)} %convert_element_type.474), channel_id=1, source_target_pairs={{16,0},{17,1},{18,2},{19,3},{20,4},{21,5},{22,6},{23,7},{24,8},{25... | collective-permute-start | bytes 11796488 | tf_op jit(solution)/shard_map/while/body/eval_jaxpr/ppermute | solution.py:17
  326.8 326.0 %collective-permute-start = (bf16[1,1280,1536]{1,2,0:T(8,128)(2,1)}, bf16[1,1280,1536]{1,2,0:T(8,128)(2,1)}, u32[]{:S(2)}, u32[]{:S(2)}) collective-permute-start(bf16[1,1280,1536]{1,2,0:T(8,128)(2,1)} %get-tuple-element.1291), channel_id=1, source_target_pairs={{0,16},{16,0},{1,17},{17,1},{2,18},{18,2},{3,19},{19,3},{4,20},{20... | collective-permute-start | bytes 11796488 | tf_op jit(solution)/shard_map/while/body/eval_jaxpr/ppermute | solution.py:22
  479.7 165.9 %collective-permute-start.2 = (bf16[1,1280]{1,0:T(2,128)(2,1)}, bf16[1,1280]{1,0:T(2,128)(2,1)}, u32[]{:S(2)}, u32[]{:S(2)}) collective-permute-start(bf16[1,1280]{1,0:T(2,128)(2,1)} %convert_element_type.476), channel_id=1, source_target_pairs={{16,0},{17,1},{18,2},{19,3},{20,4},{21,5},{22,6},{23,7},{24,8},{25... | collective-permute-start | bytes 7688 | tf_op jit(solution)/shard_map/while/body/eval_jaxpr/ppermute | solution.py:17
  654.7 4.4 copy-start.22
  654.7 4.4 copy-start.24
  659.1 5.5 copy-start.23
  659.1 540.5 %copy-start.21 = (s32[1,1280]{1,0:T(1,128)}, s32[1,1280]{1,0:T(1,128)S(1)}, u32[]{:S(2)}) copy-start(s32[1,1280]{1,0:T(1,128)S(1)} %get-tuple-element.1319) | copy-start | bytes 15364 | tf_op jit(solution)/shard_map/while
  664.6 528.6 %collective-permute-start.1 = (bf16[1,1280,1536]{1,2,0:T(8,128)(2,1)}, bf16[1,1280,1536]{1,2,0:T(8,128)(2,1)}, u32[]{:S(2)}, u32[]{:S(2)}) collective-permute-start(bf16[1,1280,1536]{1,2,0:T(8,128)(2,1)} %convert_element_type.474), channel_id=1, source_target_pairs={{16,0},{17,1},{18,2},{19,3},{20,4},{21,5},{22,6},{23,7},{24,8},{25... | collective-permute-start | bytes 11796488 | tf_op jit(solution)/shard_map/while/body/eval_jaxpr/ppermute | solution.py:17
  665.9 533.1 %collective-permute-start = (bf16[1,1280,1536]{1,2,0:T(8,128)(2,1)}, bf16[1,1280,1536]{1,2,0:T(8,128)(2,1)}, u32[]{:S(2)}, u32[]{:S(2)}) collective-permute-start(bf16[1,1280,1536]{1,2,0:T(8,128)(2,1)} %get-tuple-element.1291), channel_id=1, source_target_pairs={{0,16},{16,0},{1,17},{17,1},{2,18},{18,2},{3,19},{19,3},{4,20},{20... | collective-permute-start | bytes 11796488 | tf_op jit(solution)/shard_map/while/body/eval_jaxpr/ppermute | solution.py:22
  1026.7 165.2 %collective-permute-start.2 = (bf16[1,1280]{1,0:T(2,128)(2,1)}, bf16[1,1280]{1,0:T(2,128)(2,1)}, u32[]{:S(2)}, u32[]{:S(2)}) collective-permute-start(bf16[1,1280]{1,0:T(2,128)(2,1)} %convert_element_type.476), channel_id=1, source_target_pairs={{16,0},{17,1},{18,2},{19,3},{20,4},{21,5},{22,6},{23,7},{24,8},{25... | collective-permute-start | bytes 7688 | tf_op jit(solution)/shard_map/while/body/eval_jaxpr/ppermute | solution.py:17
  1201.0 71.1 %copy-start.12 = (s32[1280]{0:T(1024)}, s32[1280]{0:T(1024)S(1)}, u32[]{:S(2)}) copy-start(s32[1280]{0:T(1024)S(1)} %reduce.44) | copy-start | bytes 15364 | tf_op jit(solution)/shard_map/while/body/eval_jaxpr/cond
  1201.7 70.4 %copy-start.14 = (s32[1280]{0:T(1024)}, s32[1280]{0:T(1024)S(1)}, u32[]{:S(2)}) copy-start(s32[1280]{0:T(1024)S(1)} %reduce.45) | copy-start | bytes 15364 | tf_op jit(solution)/shard_map/while/body/eval_jaxpr/cond
  1451.4 13.1 copy-start.13
  1451.4 13.1 copy-start.15
  1511.2 20.8 copy-start.1
  1511.2 20.8 copy-start.2
  1558.1 4.4 copy-start.22
  1558.1 4.4 copy-start.24
  1572.5 2.7 copy-start.4
  1572.5 2.7 copy-start.27
  1572.5 2.7 copy-start.38
  1575.2 7.2 copy-start.29
  1663.7 5.1 copy-start.31
  1663.7 5.1 copy-start.40
  1663.7 5.1 copy-start.5
  1663.8 5.1 copy-start.10
  1663.8 5.1 copy-start.39
  1667.0 4.0 copy-start.7
  1667.0 4.0 copy-start.9
  1667.0 4.0 copy-start.33
  (12 other events, 12.2 us)
where the time goes:
time: 2220 us; the launch traced here: 2210 us
  starting transfers between devices  523 us (24%)
  blocking collectives  486 us (22%)
  matrix products  371 us (17%)
  waiting for transfers between devices  321 us (14%)
  local copies, waits for them, and re-layouts  267 us (12%)
  other arithmetic  218 us (10%)
    ppermute x3, starting transfers between devices, shifted_2(): lax.ppermute(array, axis, [(i, (i + by) % size) for i in range(size)])  511 us
    unnamed x2, blocking collectives  462 us
    ppermute x5, waiting for transfers between devices, from_behind(): return lax.ppermute(block, axis, route)  321 us
    reshape x10, local copies, waits for them, and re-layouts, on_device(): grad.reshape(dp_count, seq_count, -1)  79.6 us
    another operation x16, other arithmetic  76.3 us
    dot_general x1, matrix products, revisit(): jnp.einsum('sqhe,skhe->shqk', d_att4, values, preferred_element_type=jnp....  68.9 us
    dot_general x2, matrix products, pair_terms(): jnp.einsum('sqhe,skhe->shqk', queries, key_rows, preferred_element_type=j...  59.5 us
    unnamed x88, local copies, waits for them, and re-layouts  49.6 us
  transfers between devices with their start and end apart: 8, of which 2 were waited for; matrix products, arithmetic and copies ran while one was open for 9% of the time, Pallas kernels for 0%

commit v1 on v0

v1 whole, which is shorter than its diff:
```python
import functools

import jax
import jax.numpy as jnp
from jax import lax
from jax.experimental import pallas as pl
from jax.experimental.pallas import tpu as pltpu
from jax.sharding import PartitionSpec as P

HEADS = 12
HEAD_DIM = 64
PAIRS = HEADS // 2
PAIR = 2 * HEAD_DIM

LN_EPS = 1e-05
GELU_C = 0.7978845608028654
LOG2E = 1.4426950408889634
FAR = 1e30
VMEM_LIMIT = 56 * 2**20

BF16 = jnp.bfloat16
F32 = jnp.float32
NN = (((1,), (0,)), ((), ()))
NT = (((1,), (1,)), ((), ()))
TN = (((0,), (0,)), ((), ()))


def mm(left, right, dims):
    return lax.dot_general(left, right, dims, preferred_element_type=F32)


def pick_tile(block_len):
    return 256 if block_len % 256 == 0 else block_len


def layer_norm(values, gain):
    centre = jnp.mean(values, axis=-1, keepdims=True)
    shifted = values - centre
    spread = jnp.mean(shifted * shifted, axis=-1, keepdims=True)
    return shifted * lax.rsqrt(spread + LN_EPS) * gain


def gelu_tanh(values):
    return 0.5 * values * (1.0 + jnp.tanh(GELU_C * (values + 0.044715 * values * values * values)))


def split2(values):
    high = values.astype(BF16)
    return high, (values - high.astype(F32)).astype(BF16)


def half_masks(rows):
    lane = lax.broadcasted_iota(jnp.int32, (rows, PAIR), 1)
    return (lane < HEAD_DIM, lane >= HEAD_DIM)


def tile_marks(tile, row_tile, key_tile, start):
    rows = row_tile * tile + lax.broadcasted_iota(jnp.int32, (tile, tile), 0)
    keys = key_tile * tile + lax.broadcasted_iota(jnp.int32, (tile, tile), 1)
    inside = keys >= start
    return inside & (keys < rows), inside & (keys <= rows)


def head0_scores(q_pair, k_pair, tile):
    first, _ = half_masks(tile)
    return mm(jnp.where(first, q_pair, 0), k_pair, NT) * HEAD_DIM**-0.5


def before_sum(chosen, tile):
    rows = lax.broadcasted_iota(jnp.int32, (tile, tile), 0)
    cols = lax.broadcasted_iota(jnp.int32, (tile, tile), 1)
    lower = (cols < rows).astype(F32).astype(BF16)
    high, low = split2(chosen)
    above = mm(lower, high, NN) + mm(lower, low, NN)
    return above, above[tile - 1 :, :] + chosen[tile - 1 :, :]


def after_sum(values, tile):
    rows = lax.broadcasted_iota(jnp.int32, (tile, tile), 0)
    cols = lax.broadcasted_iota(jnp.int32, (tile, tile), 1)
    upper = (cols > rows).astype(F32).astype(BF16)
    high, low = split2(values)
    below = mm(upper, high, NN) + mm(upper, low, NN)
    return below, below[:1, :] + values[:1, :]


def forward_kernel(
    tile, tiles,
    slot_ref, low_ref, q_ref, q0_ref, k_ref, v_ref, start_ref, rate_ref,
    att_ref, den_ref, kept_ref, sums_ref,
    acc, pen,
):
    halves = half_masks(tile)
    sums_ref[...] = jnp.zeros_like(sums_ref)

    def row_step(i, carry):
        slot = slot_ref[i]
        start = start_ref[i]
        rate = rate_ref[i]

        @pl.when(slot < 0)
        def _():
            def key_step(j, c):
                strict, _ = tile_marks(tile, i, j, start)
                scores = head0_scores(q0_ref[i], k_ref[j, :, :PAIR], tile)
                chosen = jnp.where(strict, jnp.maximum(scores, 0.0), 0.0)
                sums_ref[j] += jnp.sum(chosen, axis=0, keepdims=True)
                return c

            lax.fori_loop(low_ref[i], i + 1, key_step, 0)

        @pl.when(slot >= 0)
        def _():
            acc[...] = jnp.zeros_like(acc)

            def key_step(j, c):
                kept = sums_ref[j]
                kept_ref[slot, j] = kept
                strict, allowed = tile_marks(tile, i, j, start)
                scores = head0_scores(q0_ref[i], k_ref[j, :, :PAIR], tile)
                chosen = jnp.where(strict, jnp.maximum(scores, 0.0), 0.0)
                above, total = before_sum(chosen, tile)
                pen[...] = jnp.where(allowed, (rate * LOG2E) * (kept + above), FAR)
                sums_ref[j] = kept + total
                for pair in range(PAIRS):
                    at = slice(pair * PAIR, (pair + 1) * PAIR)
                    for half in range(2):
                        q_one = jnp.where(halves[half], q_ref[slot, :, at], 0)
                        logits = mm(q_one, k_ref[j, :, at], NT) * (HEAD_DIM**-0.5 * LOG2E) - pen[...]
                        numer = jnp.exp2(logits).astype(BF16)
                        v_one = jnp.where(halves[half], v_ref[j, :, at], 1)
                        acc[2 * pair + half] += mm(numer, v_one, NN)
                return c

            lax.fori_loop(low_ref[i], i + 1, key_step, 0)
            for pair in range(PAIRS):
                at = slice(pair * PAIR, (pair + 1) * PAIR)
                low, high = acc[2 * pair], acc[2 * pair + 1]
                numer = jnp.where(halves[0], low, high)
                denom = pltpu.roll(jnp.where(halves[0], high, low), HEAD_DIM, 1)
                att_ref[slot, :, at] = numer / denom
                den_ref[slot, :, at] = denom

        return carry

    lax.fori_loop(0, tiles, row_step, 0)


def backward_kernel(
    tile, owned,
    own_ref, low_ref, q_ref, k_ref, v_ref, dx_ref, start_ref, rate_ref, kept_ref,
    dq_ref, dk_ref, dv_ref, later_ref,
    acc_q, acc_k, acc_v, pen, dpen, later,
):
    halves = half_masks(tile)
    acc_k[...] = jnp.zeros_like(acc_k)
    acc_v[...] = jnp.zeros_like(acc_v)
    later[...] = jnp.zeros_like(later)
    later_ref[...] = jnp.zeros_like(later_ref)

    def row_step(step, carry):
        slot = owned - 1 - step
        i = own_ref[slot]
        start = start_ref[i]
        rate = rate_ref[i]
        acc_q[...] = jnp.zeros_like(acc_q)

        def key_step(j, c):
            strict, allowed = tile_marks(tile, i, j, start)
            scores0 = head0_scores(q_ref[slot, :, :PAIR], k_ref[j, :, :PAIR], tile)
            chosen = jnp.where(strict, jnp.maximum(scores0, 0.0), 0.0)
            above, _ = before_sum(chosen, tile)
            pen[...] = jnp.where(allowed, (rate * LOG2E) * (kept_ref[slot, j] + above), FAR)
            dpen[...] = jnp.zeros_like(dpen)
            for head in range(HEADS - 1, -1, -1):
                pair, half = divmod(head, 2)
                at = slice(pair * PAIR, (pair + 1) * PAIR)
                rows_at = slice(half * HEAD_DIM, (half + 1) * HEAD_DIM)
                head_at = slice(head * HEAD_DIM, (head + 1) * HEAD_DIM)
                k_one = k_ref[j, :, at]
                q_pair = q_ref[slot, :, at]
                if head == 0:
                    logits = scores0 * LOG2E - pen[...]
                else:
                    q_one = jnp.where(halves[half], q_pair, 0)
                    logits = mm(q_one, k_one, NT) * (HEAD_DIM**-0.5 * LOG2E) - pen[...]
                numer = jnp.exp2(logits)
                dx = dx_ref[slot, :, head * PAIR : (head + 1) * PAIR]
                v_one = jnp.where(halves[half], v_ref[j, :, at], 1)
                d_logit = numer * mm(dx, v_one, NT)
                total_pen = dpen[...] + d_logit
                if head == 0:
                    below, total = after_sum(total_pen, tile)
                    picked = strict & (scores0 > 0.0)
                    d_logit = d_logit + jnp.where(picked, -rate * (later[j] + below), 0.0)
                    later[j] = later[j] + total
                    later_ref[slot, j] = total
                else:
                    dpen[...] = total_pen
                d_low = d_logit.astype(BF16)
                acc_v[j, head_at, :] += mm(dx, numer.astype(BF16), TN)[rows_at]
                acc_k[j, head_at, :] += mm(q_pair, d_low, TN)[rows_at]
                acc_q[:, at] += mm(d_low, jnp.where(halves[half], k_one, 0), NN)
            return c

        lax.fori_loop(low_ref[i], i + 1, key_step, 0)
        dq_ref[slot] = (acc_q[...] * HEAD_DIM**-0.5).astype(BF16)
        return carry

    lax.fori_loop(0, owned, row_step, 0)

    def finish(j, c):
        dk_ref[j] = (acc_k[j] * HEAD_DIM**-0.5).astype(BF16)
        dv_ref[j] = acc_v[j].astype(BF16)
        return c

    lax.fori_loop(0, dk_ref.shape[0], finish, 0)


def late_kernel(tile, owned, own_ref, low_ref, q_ref, k_ref, start_ref, rate_ref, later_ref, dq_ref, dk_ref):
    first, _ = half_masks(tile)
    dk_ref[...] = jnp.zeros_like(dk_ref)
    dq_ref[...] = jnp.zeros_like(dq_ref)

    def row_step(slot, carry):
        i = own_ref[slot]
        start = start_ref[i]
        rate = rate_ref[i]

        def key_step(j, c):
            strict, _ = tile_marks(tile, i, j, start)
            scores = head0_scores(q_ref[slot], k_ref[j], tile)
            d_low = jnp.where(strict & (scores > 0.0), -rate * later_ref[slot, j], 0.0).astype(BF16)
            dk_ref[j] += mm(q_ref[slot], d_low, TN)[:HEAD_DIM] * HEAD_DIM**-0.5
            dq_ref[slot] += mm(d_low, jnp.where(first, k_ref[j], 0), NN) * HEAD_DIM**-0.5
            return c

        lax.fori_loop(low_ref[i], i + 1, key_step, 0)
        return carry

    lax.fori_loop(0, owned, row_step, 0)


def call(kernel, outs, scratch, scalars, operands, cost):
    smem = pl.BlockSpec(memory_space=pltpu.SMEM)
    vmem = pl.BlockSpec(memory_space=pltpu.VMEM)
    return pl.pallas_call(
        kernel,
        out_shape=tuple(jax.ShapeDtypeStruct(shape, dtype) for shape, dtype in outs),
        in_specs=[smem] * len(scalars) + [vmem] * len(operands),
        out_specs=tuple(vmem for _ in outs),
        scratch_shapes=[pltpu.VMEM(shape, dtype) for shape, dtype in scratch],
        compiler_params=pltpu.CompilerParams(vmem_limit_bytes=VMEM_LIMIT),
        cost_estimate=pl.CostEstimate(flops=cost, bytes_accessed=cost // 600, transcendentals=0),
    )(*scalars, *operands)


def on_device(
    tokens, cotangent, lengths, threshold, attn_gain, qkv_weight, out_weight, mlp_gain, up_weight, down_weight
):
    _, block_len, width = tokens.shape
    blocks = lax.axis_size("seq")
    dp_count = lax.axis_size("dp")
    me = lax.axis_index("seq")
    tile = pick_tile(block_len)
    owned = block_len // tile
    tiles = owned * blocks
    rows = blocks * block_len
    hid = up_weight.shape[1]

    ends = jnp.cumsum(lengths[0])
    positions = jnp.arange(rows, dtype=jnp.int32)
    passed = positions[:, None] >= ends[None, :]
    segment = jnp.sum(passed.astype(jnp.int32), axis=1)
    start = jnp.max(jnp.where(passed, ends[None, :], 0), axis=1)
    slots = jnp.arange(lengths.shape[1], dtype=jnp.int32)
    seg_len = jnp.sum(jnp.where(segment[:, None] == slots[None, :], lengths[0][None, :], 0), axis=1)
    rate = 4.0 / seg_len.astype(F32)
    tile_ids = jnp.arange(tiles, dtype=jnp.int32)
    low = start[::tile] // tile
    slot_of = jnp.where(tile_ids // owned == me, tile_ids % owned, -1).astype(jnp.int32)
    own_ids = (me * owned + jnp.arange(owned)).astype(jnp.int32)
    start3 = start.reshape(tiles, tile, 1)
    rate3 = rate.reshape(tiles, tile, 1)

    token_own = tokens[0]
    if blocks == 2:
        other = lax.ppermute(token_own, "seq", [(0, 1), (1, 0)])
        both = jnp.stack([token_own, other])
        pack = jnp.where(me == 0, both, both[::-1]).reshape(rows, width)
    else:
        pack = lax.all_gather(token_own, "seq", axis=0, tiled=True)
    token_vals = token_own.astype(F32)
    normed_low = layer_norm(pack.astype(F32), attn_gain).astype(BF16)
    normed_own = layer_norm(token_vals, attn_gain).astype(BF16)
    q_own = mm(normed_own, qkv_weight[:, :width], NN).astype(BF16).reshape(owned, tile, width)
    q_first = mm(normed_low, qkv_weight[:, :PAIR], NN).astype(BF16).reshape(tiles, tile, PAIR)
    k_all = mm(normed_low, qkv_weight[:, width : 2 * width], NN).astype(BF16).reshape(tiles, tile, width)
    v_all = mm(normed_low, qkv_weight[:, 2 * width :], NN).astype(BF16).reshape(tiles, tile, width)

    pairs_cost = rows * block_len * HEADS * HEAD_DIM
    attended4, denom4, kept, sums = call(
        functools.partial(forward_kernel, tile, tiles),
        [
            ((owned, tile, width), F32),
            ((owned, tile, width), F32),
            ((owned, tiles, 1, tile), F32),
            ((tiles, 1, tile), F32),
        ],
        [((HEADS, tile, PAIR), F32), ((tile, tile), F32)],
        [slot_of, low.astype(jnp.int32)],
        [q_own, q_first, k_all, v_all, start3, rate3],
        4 * pairs_cost,
    )
    limit = threshold[0].astype(F32) / 1024.0
    own_sums = lax.dynamic_slice_in_dim(sums.reshape(rows), me * block_len, block_len)
    own_rate = lax.dynamic_slice_in_dim(rate, me * block_len, block_len)
    excess_part = jnp.sum(jnp.maximum(own_rate * own_sums - limit, 0.0))
    attended = attended4.reshape(block_len, width)
    denom = denom4.reshape(block_len, width)

    cot = cotangent[0]
    attended_low = attended.astype(BF16)
    residual = token_vals + mm(attended_low, out_weight, NN)
    normed_mlp = layer_norm(residual, mlp_gain).astype(BF16)
    pre = mm(normed_mlp, up_weight, NN)
    hidden = gelu_tanh(pre).astype(BF16)
    output = (residual + mm(hidden, down_weight, NN)).astype(BF16)
    down_grad = mm(hidden, cot, TN).astype(BF16)
    d_hidden = mm(cot, down_weight, NT)
    _, gelu_pull = jax.vjp(gelu_tanh, pre)
    d_pre = gelu_pull(d_hidden)[0].astype(BF16)
    up_grad = mm(normed_mlp, d_pre, TN).astype(BF16)
    d_normed_mlp = mm(d_pre, up_weight, NT)
    _, mlp_pull = jax.vjp(layer_norm, residual, mlp_gain)
    d_res_norm, mlp_gain_grad = mlp_pull(d_normed_mlp)
    d_residual = cot.astype(F32) + d_res_norm
    d_branch = d_residual.astype(BF16)
    out_grad = mm(attended_low, d_branch, TN).astype(BF16)
    d_attended = mm(d_branch, out_weight, NT).astype(BF16)

    def scatter(grad):
        return lax.psum_scatter(grad, "dp", scatter_dimension=0, tiled=True)

    early = [scatter(g) for g in (down_grad, up_grad, out_grad)]

    by_head = (block_len, HEADS, HEAD_DIM)
    scaled = (d_attended.astype(F32) / denom).astype(BF16)
    row_dot = jnp.sum((scaled.astype(F32) * attended).reshape(by_head), axis=2, keepdims=True)
    dot_high, dot_low = split2(-row_dot)
    side = jnp.concatenate(
        [dot_high, dot_low, jnp.zeros((block_len, HEADS, HEAD_DIM - 2), BF16)], axis=2
    )
    scaled3 = scaled.reshape(by_head)
    even = (jnp.arange(HEADS) % 2 == 0)[None, :, None]
    dx = jnp.concatenate([jnp.where(even, scaled3, side), jnp.where(even, side, scaled3)], axis=2)
    dx = dx.reshape(owned, tile, HEADS * PAIR)
    dq, dk, dv, totals = call(
        functools.partial(backward_kernel, tile, owned),
        [
            ((owned, tile, width), BF16),
            ((tiles, width, tile), BF16),
            ((tiles, width, tile), BF16),
            ((owned, tiles, 1, tile), F32),
        ],
        [
            ((tile, width), F32),
            ((tiles, width, tile), F32),
            ((tiles, width, tile), F32),
            ((tile, tile), F32),
            ((tile, tile), F32),
            ((tiles, 1, tile), F32),
        ],
        [own_ids, low.astype(jnp.int32)],
        [q_own, k_all, v_all, dx, start3, rate3, kept],
        10 * pairs_cost,
    )
    all_totals = lax.all_gather(jnp.sum(totals, axis=0), "seq", axis=0)
    from_later = jnp.sum(
        jnp.where((jnp.arange(blocks) > me)[:, None, None, None], all_totals, 0.0), axis=0
    )
    late_q, late_k = call(
        functools.partial(late_kernel, tile, owned),
        [((owned, tile, PAIR), F32), ((tiles, HEAD_DIM, tile), F32)],
        [],
        [own_ids, low.astype(jnp.int32)],
        [
            q_own[:, :, :PAIR],
            k_all[:, :, :PAIR],
            start3,
            rate3,
            jnp.broadcast_to(from_later, (owned,) + from_later.shape),
        ],
        pairs_cost,
    )
    dq = jnp.concatenate(
        [(dq[:, :, :PAIR].astype(F32) + late_q).astype(BF16), dq[:, :, PAIR:]], axis=2
    ).reshape(block_len, width)
    dk = jnp.concatenate(
        [(dk[:, :HEAD_DIM].astype(F32) + late_k).astype(BF16), dk[:, HEAD_DIM:]], axis=1
    )
    dkv = jnp.concatenate([dk, dv], axis=1)
    d_normed = lax.dot_general(
        dkv, qkv_weight[:, width:], (((1,), (1,)), ((), ())), preferred_element_type=F32
    ).reshape(rows, width)
    kv_grad = jnp.einsum(
        "rtd,rct->dc", normed_low.reshape(tiles, tile, width), dkv, preferred_element_type=F32
    )
    q_grad = mm(normed_own, dq, TN)
    late = scatter(jnp.concatenate([q_grad, kv_grad], axis=1).astype(BF16))
    d_own = mm(dq, qkv_weight[:, :width], NT)
    d_blocks = d_normed.reshape(blocks, block_len, width)
    if blocks == 2:
        away = lax.dynamic_index_in_dim(d_blocks, 1 - me, 0, keepdims=False).astype(BF16)
        back = lax.ppermute(away, "seq", [(0, 1), (1, 0)]).astype(F32)
        d_own += lax.dynamic_index_in_dim(d_blocks, me, 0, keepdims=False) + back
    else:
        d_own += lax.psum_scatter(
            d_blocks.astype(BF16), "seq", scatter_dimension=0, tiled=False
        ).astype(F32)
    _, attn_pull = jax.vjp(layer_norm, token_vals, attn_gain)
    d_tok_norm, attn_gain_grad = attn_pull(d_own)
    input_grad = (d_residual + d_tok_norm).astype(BF16)

    def over_seq(piece):
        if blocks == 2:
            return piece.astype(F32) + lax.ppermute(piece, "seq", [(0, 1), (1, 0)]).astype(F32)
        return lax.psum(piece, "seq").astype(F32)

    down_piece, up_piece, out_piece = [over_seq(piece) for piece in early]
    qkv_piece = over_seq(late)
    gains = jnp.concatenate([attn_gain_grad, mlp_gain_grad, excess_part.reshape(1)])
    gains = lax.psum(gains, ("seq", "dp"))
    part = width // dp_count
    at = lax.axis_index("dp") * part
    attn_piece = lax.dynamic_slice_in_dim(gains, at, part)
    mlp_piece = lax.dynamic_slice_in_dim(gains, width + at, part)
    excess = (gains[2 * width :] / (dp_count * rows)).reshape(1)
    return (
        output[None],
        input_grad[None],
        attn_piece,
        qkv_piece,
        out_piece,
        mlp_piece,
        up_piece,
        down_piece,
        excess,
    )


def solution(mesh):
    return jax.shard_map(
        on_device,
        mesh=mesh,
        in_specs=(
            P("dp", "seq", None),
            P("dp", "seq", None),
            P("dp", None),
            P(),
            P(),
            P(),
            P(),
            P(),
            P(),
            P(),
        ),
        out_specs=(
            P("dp", "seq", None),
            P("dp", "seq", None),
            P("dp"),
            P("dp", None),
            P("dp", None),
            P("dp"),
            P("dp", None),
            P("dp", None),
            P(),
        ),
        check_vma=False,
    )
```

time: 2220 us -> 685 us (0.31)
  starting transfers between devices: 523 us -> 19.5 us
  blocking collectives: 486 us -> 154 us
  matrix products: 371 us -> 145 us
  waiting for transfers between devices: 321 us -> 121 us
  other arithmetic: 218 us -> 41.5 us
  local copies, waits for them, and re-layouts: 267 us -> 90.6 us
  Pallas kernels: 0 us -> 85.8 us
    ppermute x8 -> x6, starting transfers between devices: 523 us -> 19.3 us  [the longest x1 11.4 us: on_device(): back = lax.ppermute(away, 'seq', [(0, 1), (1, 0)]).astype(F32)]
    unnamed x2 -> x0, blocking collectives: 462 us -> none
    ppermute x8 -> x6, waiting for transfers between devices: 321 us -> 31.3 us  [the longest x1 26.7 us: on_device(): other = lax.ppermute(token_own, 'seq', [(0, 1), (1, 0)])]
    dot_general x20 -> x17, matrix products: 371 us -> 145 us  [the longest x15 123 us: mm(): return lax.dot_general(left, right, dims, preferred_element_type=F32)]
    all_gather x4 -> x1, blocking collectives: 23.5 us -> 113 us  [on_device(): all_totals = lax.all_gather(jnp.sum(totals, axis=0), 'seq', axis=0)]
    reduce_scatter x0 -> x4, waiting for transfers between devices: none -> 89.7 us  [scatter(): return lax.psum_scatter(grad, 'dp', scatter_dimension=0, tiled=True)]
    pallas_call x0 -> x3, Pallas kernels: none -> 85.8 us  [call(): pl.pallas_call(kernel, out_shape=tuple((jax.ShapeDtypeStruct(shape, dtype...]
    another operation x17 -> x2, other arithmetic: 76.4 us -> 2.08 us  [the longest x1 1.91 us: on_device(): both = jnp.stack([token_own, other])]
  transfers between devices with their start and end apart: 8 -> 10, of which waited for: 2 -> 4; matrix products, arithmetic and copies ran while one was open for 9% -> 22% of each run, Pallas kernels for 0% -> 8%
where the time goes in v1:
time: 685 us; the launch traced here: 675 us
  blocking collectives  154 us (22%)
  matrix products  145 us (21%)
  waiting for transfers between devices  121 us (18%)
  local copies, waits for them, and re-layouts  90.6 us (13%)
  Pallas kernels  85.8 us (13%)
  other arithmetic  41.5 us (6%)
  starting transfers between devices  19.5 us (3%)
  between operations  17.2 us (3%)
    dot_general x15, matrix products, mm(): return lax.dot_general(left, right, dims, preferred_element_type=F32)  123 us
    all_gather x1, blocking collectives, on_device(): all_totals = lax.all_gather(jnp.sum(totals, axis=0), 'seq', axis=0)  113 us
    reduce_scatter x4, waiting for transfers between devices, scatter(): return lax.psum_scatter(grad, 'dp', scatter_dimension=0, tiled=True)  89.7 us
    pallas_call x3, Pallas kernels, call(): pl.pallas_call(kernel, out_shape=tuple((jax.ShapeDtypeStruct(shape, dtype...  85.8 us
    psum x1, blocking collectives, on_device(): gains = lax.psum(gains, ('seq', 'dp'))  40.8 us
    unnamed x91, local copies, waits for them, and re-layouts  29 us
    ppermute x1, waiting for transfers between devices, on_device(): other = lax.ppermute(token_own, 'seq', [(0, 1), (1, 0)])  26.7 us
  transfers between devices with their start and end apart: 10, of which 4 were waited for; matrix products, arithmetic and copies ran while one was open for 22% of the time, Pallas kernels for 8%

profile of v1, /device:TPU:0, one launch (start us, length us, event | category | flops | bytes accessed | tf_op | source)
XLA Modules:
  0.0 674.8 jit_solution(12419125176547003534)
XLA Ops:
  7.2 2.8 copy.81
  10.0 3.0 collective-permute-start
  13.6 2.2 reshape.314.start_ref
  15.8 2.2 div.119.rate_ref
  18.1 4.0 copy.87
  23.6 3.1 convolution_convert_fusion.6
  29.3 26.7 %collective-permute-done = bf16[1280,768]{0,1:T(8,128)(2,1)} collective-permute-done((bf16[1280,768]{0,1:T(8,128)(2,1)S(1)}, bf16[1280,768]{0,1:T(8,128)(2,1)}, u32[]{:S(2)}, u32[]{:S(2)}) %collective-permute-start) | collective-permute-done | bytes 1966112 | tf_op jit(solution)/shard_map/ppermute | solution.py:288
  61.2 7.3 %fusion.19 = f32[2,1280,768]{1,2,0:T(8,128)} fusion(bf16[2,1280,768]{1,2,0:T(8,128)(2,1)} %copy-done.4, pred[]{:T(512)S(6)} %eq.37), kind=kLoop, calls=%fused_computation.39 | loop fusion | flops 3932160 | bytes 11796481 | tf_op jit(solution)/shard_map/convert_element_type | solution.py:294
  68.5 9.1 %copy.83 = f32[2,1280,768]{2,1,0:T(8,128)} copy(f32[2,1280,768]{1,2,0:T(8,128)} %fusion.19) | data formatting | bytes 15728640 | tf_op jit(solution)/shard_map/convert_element_type | solution.py:294
  77.6 4.2 fusion.8
  81.9 4.7 convolution_convert_fusion.2
  86.6 4.9 convolution_convert_fusion.1
  93.5 30.3 %shard_map.169 = (f32[5,256,768]{2,1,0:T(8,128)}, f32[5,256,768]{2,1,0:T(8,128)}, f32[5,10,1,256]{3,2,1,0:T(1,128)}, f32[10,1,256]{2,1,0:T(1,128)}) custom-call(s32[10]{0:T(128)} %get-tuple-element.85.slot_ref, s32[10]{0:T(128)} %get-tuple-element.84.low_ref, bf16[5,256,768]{2,1,0:T(8,128)(2,1)} %bitcast.113, bf16[10,256,128]{2,1,0:T(8,128)(2,1)} %bitcast.107, ...), custom_call_target="tpu_custom_call" | custom-call | flops 10066329600 | bytes 16777216 | tf_op jit(solution)/shard_map/pallas_call | solution.py:247
  123.8 5.4 copy.89
  129.2 4.0 fusion.69
  134.0 14.1 %fusion.66 = f32[1280,3072]{1,0:T(8,128)} fusion(bf16[768,3072]{1,0:T(8,128)(2,1)} %param.18, f32[1280,768]{0,1:T(8,128)S(1)} %get-tuple-element.78, f32[768]{0:T(1024)S(1)} %copy-done.35, f32[1280]{0:T(1024)S(1)} %fusion.61, f32[1280]{0:T(1024)S(1)} %broadcast_multiply_fusion.1), kind=kOutput, calls=%fused_computation.145 | convolution fusion | flops 6043729920 | bytes 24392704 | tf_op jit(solution)/shard_map/dot_general | solution.py:29
  148.1 21.4 %fusion.3 = bf16[1280,3072]{1,0:T(8,128)(2,1)} fusion(f32[1280,3072]{1,0:T(8,128)} %fusion.66, bf16[3072,768]{1,0:T(8,128)(2,1)S(1)} %bitcast.121, bf16[1,1280,768]{2,1,0:T(8,128)(2,1)S(1)} %copy-done.14), kind=kOutput, calls=%fused_computation.7 | convolution fusion | flops 6134169600 | bytes 30277632 | tf_op jit(solution)/shard_map/dot_general | solution.py:29
  169.5 10.7 %multiply_reduce_fusion.1 = (f32[768]{0:T(1024)}, f32[1280]{0:T(1024)S(1)}, f32[1280,768]{0,1:T(8,128)S(1)}) fusion(f32[1280,768]{0,1:T(8,128)S(1)} %get-tuple-element.78, f32[1280]{0:T(1024)S(1)} %fusion.61, f32[1280]{0:T(1024)S(1)} %broadcast_multiply_fusion.1, f32[768]{0:T(1024)S(1)} %copy-done.35, bf16[1280,3072]{1,0:T(8,128)(2,1)} %fusion.3, ...), kind=kOutput, calls=%fused_computation.49 | convolution fusion | flops 6046676992 | bytes 20468736 | tf_op jit(solution)/shard_map/dot_general | solution.py:29
  185.5 2.8 convolution_convert_fusion.7
  188.2 5.8 copy.88
  194.1 7.5 %convert_multiply_fusion = (f32[1280,768]{0,1:T(8,128)}, bf16[1280,768]{0,1:T(8,128)(2,1)S(1)}) fusion(f32[1280,768]{0,1:T(8,128)} %copy.89, f32[1280,768]{0,1:T(8,128)} %copy.88, bf16[768,768]{1,0:T(8,128)(2,1)S(1)} %copy-done, bf16[1280,768]{0,1:T(8,128)(2,1)} %copy-done.16), kind=kOutput, calls=%fused_computation.51 | convolution fusion | flops 1515847680 | bytes 16908288 | tf_op jit(solution)/shard_map/dot_general | solution.py:29
  201.6 2.4 reduce_sum.175
  207.3 2.2 pad_maximum_fusion.2
  209.4 8.6 %copy.92 = bf16[1280,12,128]{2,1,0:T(8,128)(2,1)} copy(bf16[1280,12,128]{0,2,1:T(8,128)(2,1)} %pad_maximum_fusion.2) | data formatting | bytes 7864320 | tf_op jit(solution)/shard_map/concatenate | solution.py:356
  218.1 8.3 %reshape.302.dx_ref = bf16[5,256,1536]{2,1,0:T(8,128)(2,1)} reshape(bf16[1280,12,128]{2,1,0:T(8,128)(2,1)} %copy.92) | data formatting | bytes 7864320 | tf_op jit(solution)/shard_map/reshape | solution.py:357
  226.3 48.0 %shard_map.170 = (bf16[5,256,768]{2,1,0:T(8,128)(2,1)}, bf16[10,768,256]{2,1,0:T(8,128)(2,1)}, bf16[10,768,256]{2,1,0:T(8,128)(2,1)}, f32[5,10,1,256]{3,2,1,0:T(1,128)}) custom-call(s32[5]{0:T(128)} %iota_add_fusion.own_ref, s32[10]{0:T(128)} %get-tuple-element.84.low_ref, bf16[5,256,768]{2,1,0:T(8,128)(2,1)} %bitcast.114, bf16[10,256,768]{2,1,0:T(8,128)(2,1)} %bitcast.110, ...), custom_call_target="tpu_custom_call" | custom-call | flops 25165824000 | bytes 41943040 | tf_op jit(solution)/shard_map/pallas_call | solution.py:247
  275.3 113.5 %all-gather.1 = f32[2,10,256]{2,1,0:T(8,128)S(1)} all-gather(f32[1,10,256]{2,1,0:T(8,128)S(1)} %bitcast.111), channel_id=2, replica_groups=mesh['seq'=2,'dp'=16] {'seq'}, dimensions={0}, use_global_device_ids=true | all-gather | bytes 30720 | tf_op jit(solution)/shard_map/all_gather | solution.py:378
  388.7 4.1 slice.50
  393.7 7.5 %shard_map.171 = (f32[5,256,128]{2,1,0:T(8,128)}, f32[10,64,256]{2,1,0:T(8,128)}) custom-call(s32[5]{0:T(128)} %iota_add_fusion.own_ref, s32[10]{0:T(128)} %get-tuple-element.84.low_ref, bf16[5,256,128]{2,1,0:T(8,128)(2,1)} %slice.53.q_ref, bf16[10,256,128]{2,1,0:T(8,128)(2,1)} %slice.54.k_ref, s32[10,256,1]{2,1,0:T(8,128)} %reshape.314.start_ref, ...), custom_call_target="tpu_custom_call" | custom-call | flops 2516582400 | bytes 4194304 | tf_op jit(solution)/shard_map/pallas_call | solution.py:247
  404.3 2.2 fusion.44
  407.2 12.4 %bitcast_convert_fusion = bf16[768,1536]{1,0:T(8,128)(2,1)S(1)} fusion(f32[10,256,768]{2,1,0:T(8,128)} %bitcast.95, f32[768]{0:T(1024)S(1)} %copy-done.32, f32[10,256]{1,0:T(8,128)S(1)} %rsqrt.41, f32[10,256]{1,0:T(8,128)S(1)} %div.117, bf16[10,768,256]{2,1,0:T(8,128)(2,1)} %get-tuple-element.27, bf16[10,704,256]{2,1,0:T(8,128)(2,1)} %slice.50, ...), kind=kOutput, calls=%fused_computation.32 | convolution fusion | flops 6072434688 | bytes 18111488 | tf_op jit(solution)/shard_map/rtd,rct->dc/dot_general | solution.py:406
  421.7 11.5 %convolution_convert_fusion.3 = bf16[768,3072]{1,0:T(8,128)(2,1)} fusion(bf16[1280,3072]{1,0:T(8,128)(2,1)} %fusion.3, f32[1280,768]{0,1:T(8,128)} %copy-done.9, f32[768]{0:T(1024)S(1)} %copy-done.35, f32[1280]{0:T(1024)S(1)} %fusion.61, f32[1280]{0:T(1024)S(1)} %broadcast_multiply_fusion.1), kind=kOutput, calls=%fused_computation.31 | convolution fusion | flops 6046089216 | bytes 16528384 | tf_op jit(solution)/shard_map/dot_general | solution.py:29
  433.9 9.4 %fusion.25 = f32[10,256,768]{2,1,0:T(8,128)S(1)} fusion(bf16[10,768,256]{2,1,0:T(8,128)(2,1)} %get-tuple-element.27, bf16[10,704,256]{2,1,0:T(8,128)(2,1)} %slice.50, bf16[10,64,256]{2,1,0:T(8,128)(2,1)S(1)} %add_convert_fusion.2, bf16[768,2304]{1,0:T(8,128)(2,1)} %param.15), kind=kOutput, calls=%fused_computation.62 | convolution fusion | flops 6063390720 | bytes 18087936 | tf_op jit(solution)/shard_map/dot_general | solution.py:403
  443.4 3.1 copy-done.10
  446.6 2.3 copy.109
  449.0 11.4 %collective-permute-start.1 = (bf16[1280,768]{0,1:T(8,128)(2,1)}, bf16[1280,768]{0,1:T(8,128)(2,1)}, u32[]{:S(2)}, u32[]{:S(2)}) collective-permute-start(bf16[1280,768]{0,1:T(8,128)(2,1)} %bitcast.105), channel_id=1, source_target_pairs={{0,16},{16,0},{1,17},{17,1},{2,18},{18,2},{3,19},{19,3},{4,20},{20... | collective-permute-start | bytes 5898248 | tf_op jit(solution)/shard_map/ppermute | solution.py:415
  460.4 13.8 %convolution_convert_fusion = bf16[3072,768]{1,0:T(8,128)(2,1)} fusion(bf16[1,1280,768]{2,1,0:T(8,128)(2,1)} %param.11, f32[1280,3072]{1,0:T(8,128)} %fusion.66), kind=kOutput, calls=%fused_computation.28 | convolution fusion | flops 6077546496 | bytes 22413312 | tf_op jit(solution)/shard_map/dot_general | solution.py:29
  474.2 14.5 %fusion.26 = bf16[1,1280,768]{1,2,0:T(8,128)(2,1)} fusion(f32[1280,768]{0,1:T(8,128)} %copy-done.9, bf16[3072,768]{1,0:T(8,128)(2,1)} %param.19, f32[1280,3072]{1,0:T(8,128)} %fusion.66), kind=kOutput, calls=%fused_computation.63 | convolution fusion | flops 6077153280 | bytes 26345472 | tf_op jit(solution)/shard_map/dot_general | solution.py:29
  489.2 4.3 constant_dynamic-slice_fusion.1
  493.5 5.5 copy.99
  499.0 4.1 copy.104
  504.5 5.8 fusion.18
  513.3 3.0 fusion.31
  518.4 40.8 %psum.7 = f32[1537]{0:T(1024)S(1)} all-reduce(f32[1537]{0:T(1024)S(1)} %pad_maximum_fusion.7), channel_id=1, replica_groups=mesh['seq'=2,'dp'=16] {'seq','dp'}, use_global_device_ids=true, to_apply=%region_20.21 | all-reduce | flops 1537 | bytes 12296 | tf_op jit(solution)/shard_map/psum | solution.py:433
  559.7 3.9 copy.105
  564.9 13.2 %reduce-scatter.9.cloned.1.call-done = bf16[48,3072]{1,0:T(8,128)(2,1)} async-done(((bf16[768,3072]{1,0:T(8,128)(2,1)}), bf16[48,3072]{1,0:T(8,128)(2,1)}) %reduce-scatter.9.cloned.1.call-update) | async-done | bytes 294928 | tf_op jit(solution)/shard_map/reduce_scatter | solution.py:343
  580.4 76.5 %reduce-scatter.11.cloned.1.call-done = bf16[192,768]{1,0:T(8,128)(2,1)} async-done(((bf16[3072,768]{1,0:T(8,128)(2,1)}), bf16[192,768]{1,0:T(8,128)(2,1)}) %reduce-scatter.11.cloned.1.call-update) | async-done | bytes 294928 | tf_op jit(solution)/shard_map/reduce_scatter | solution.py:343
  660.2 4.6 collective-permute-done.5
  (167 shorter events, 44.3 us)
Async XLA Ops:
  7.2 122.1 %copy-start = (bf16[768,768]{1,0:T(8,128)(2,1)S(1)}, bf16[768,768]{1,0:T(8,128)(2,1)}, u32[]{:S(2)}) copy-start(bf16[768,768]{1,0:T(8,128)(2,1)} %param.16) | copy-start | bytes 3538948
  7.2 5.9 copy-start.38
  7.2 481.5 %reduce-scatter.7.cloned.1.call-start = ((), (), s32[]{:S(2)}) async-start(), calls=%async_computation.5 | async-start | bytes 1253376 | tf_op jit(solution)/shard_map/reduce_scatter | solution.py:343
  10.0 119.2 %copy-start.2 = (bf16[1,1280,768]{1,2,0:T(8,128)(2,1)}, bf16[1,1280,768]{1,2,0:T(8,128)(2,1)S(1)}, u32[]{:S(2)}) copy-start(bf16[1,1280,768]{1,2,0:T(8,128)(2,1)S(1)} %copy.81) | copy-start | bytes 5898244
  10.0 46.0 %collective-permute-start = (bf16[1280,768]{0,1:T(8,128)(2,1)S(1)}, bf16[1280,768]{0,1:T(8,128)(2,1)}, u32[]{:S(2)}, u32[]{:S(2)}) collective-permute-start(bf16[1280,768]{0,1:T(8,128)(2,1)S(1)} %bitcast.94), channel_id=1, source_target_pairs={{0,16},{16,0},{1,17},{17,1},{2,18},{18,2},{3,19},{19,3},{4,20},{20... | collective-permute-start | bytes 5898248 | tf_op jit(solution)/shard_map/ppermute | solution.py:288
  13.5 8.9 %copy-start.21 = (f32[2560]{0:T(1024)}, f32[2560]{0:T(1024)S(1)}, u32[]{:S(2)}) copy-start(f32[2560]{0:T(1024)S(1)} %convert_divide_fusion) | copy-start | bytes 30724
  18.1 5.5 copy-start.31
  22.4 4.3 copy-start.19
  23.6 3.2 copy-start.26
  26.7 29.2 %copy-start.30 = (bf16[1280,768]{1,0:T(8,128)(2,1)}, bf16[1280,768]{1,0:T(8,128)(2,1)S(1)}, u32[]{:S(2)}) copy-start(bf16[1280,768]{1,0:T(8,128)(2,1)S(1)} %convolution_convert_fusion.6) | copy-start | bytes 5898244
  57.9 2.0 copy-start.4
  77.6 4.3 copy-start.33
  133.3 47.0 %copy-start.9 = (f32[1280,768]{0,1:T(8,128)}, f32[1280,768]{0,1:T(8,128)S(1)}, u32[]{:S(2)}) copy-start(f32[1280,768]{0,1:T(8,128)S(1)} %get-tuple-element.78) | copy-start | bytes 11796484
  133.3 14.8 %slice-start.2 = ((s8[4718592]{0:T(1024)(128)(4,1)}), s8[4194304]{0:T(1024)(128)(4,1)S(1)}, s32[]{:S(2)}) async-start(s8[4718592]{0:T(1024)(128)(4,1)} %bitcast.120), calls=%async_computation.10 | async-start | bytes 8388608
  134.0 14.1 %copy-start.14 = (bf16[1,1280,768]{2,1,0:T(8,128)(2,1)S(1)}, bf16[1,1280,768]{2,1,0:T(8,128)(2,1)}, u32[]{:S(2)}) copy-start(bf16[1,1280,768]{2,1,0:T(8,128)(2,1)} %param.11) | copy-start | bytes 5898244
  134.0 14.1 %slice-start.3 = ((s8[4718592]{0:T(1024)(128)(4,1)}), s8[524288]{0:T(1024)(128)(4,1)S(1)}, s32[]{:S(2)}) async-start(s8[4718592]{0:T(1024)(128)(4,1)} %bitcast.120), calls=%async_computation.11 | async-start | bytes 1048576
  134.0 35.5 %slice-start = ((s8[4718592]{0:T(1024)(128)(4,1)}), s8[4194304]{0:T(1024)(128)(4,1)S(1)}, s32[]{:S(2)}) async-start(s8[4718592]{0:T(1024)(128)(4,1)} %bitcast.118), calls=%async_computation.8 | async-start | bytes 8388608
  148.1 21.4 %slice-start.1 = ((s8[4718592]{0:T(1024)(128)(4,1)}), s8[524288]{0:T(1024)(128)(4,1)S(1)}, s32[]{:S(2)}) async-start(s8[4718592]{0:T(1024)(128)(4,1)} %bitcast.118), calls=%async_computation.9 | async-start | bytes 1048576
  180.2 1.5 copy-start.7
  181.2 1.9 copy-start.5
  181.3 1.9 copy-start.28
  181.8 3.7 copy-start.11
  206.1 310.3 %reduce-scatter.5.cloned.1.call-start = ((), (), s32[]{:S(2)}) async-start(), calls=%async_computation.4 | async-start | bytes 3760128 | tf_op jit(solution)/shard_map/reduce_scatter | solution.py:343
  274.4 118.5 %copy-start.37 = (pred[2]{0:T(512)(128)(4,1)S(1)}, pred[2]{0:T(512)(128)(4,1)}, u32[]{:S(2)}) copy-start(pred[2]{0:T(512)(128)(4,1)} %iota_compare_fusion.2) | copy-start | bytes 10
  393.7 8.8 %copy-start.12 = (bf16[5,256,768]{2,1,0:T(8,128)(2,1)S(1)}, bf16[5,256,768]{2,1,0:T(8,128)(2,1)}, u32[]{:S(2)}) copy-start(bf16[5,256,768]{2,1,0:T(8,128)(2,1)} %get-tuple-element.22) | copy-start | bytes 5898244
  402.5 1.8 copy-start.13
  402.5 1.8 copy-start.20
  402.5 1.8 copy-start.27
  402.5 1.8 copy-start.32
  421.6 156.4 %reduce-scatter.9.cloned.1.call-start = ((), (), s32[]{:S(2)}) async-start(), calls=%async_computation.6 | async-start | bytes 5013504 | tf_op jit(solution)/shard_map/reduce_scatter | solution.py:343
  433.2 223.7 %reduce-scatter.11.cloned.1.call-start = ((), (), s32[]{:S(2)}) async-start(), calls=%async_computation.7 | async-start | bytes 5013504 | tf_op jit(solution)/shard_map/reduce_scatter | solution.py:343
  443.4 3.1 copy-start.10
  449.0 55.5 %collective-permute-start.1 = (bf16[1280,768]{0,1:T(8,128)(2,1)}, bf16[1280,768]{0,1:T(8,128)(2,1)}, u32[]{:S(2)}, u32[]{:S(2)}) collective-permute-start(bf16[1280,768]{0,1:T(8,128)(2,1)} %bitcast.105), channel_id=1, source_target_pairs={{0,16},{16,0},{1,17},{17,1},{2,18},{18,2},{3,19},{19,3},{4,20},{20... | collective-permute-start | bytes 5898248 | tf_op jit(solution)/shard_map/ppermute | solution.py:415
  488.7 15.1 %collective-permute-start.3 = (bf16[48,768]{1,0:T(8,128)(2,1)}, bf16[48,768]{1,0:T(8,128)(2,1)S(1)}, u32[]{:S(2)}, u32[]{:S(2)}) collective-permute-start(bf16[48,768]{1,0:T(8,128)(2,1)} %reduce-scatter.7.cloned.1.call-done), channel_id=1, source_target_pairs={{0,16},{16,0},{1,17},{17,1},{2,18},{18,2},{3,19},{19,3},{4,20},{20... | collective-permute-start | bytes 221192 | tf_op jit(solution)/shard_map/ppermute | solution.py:427
  493.5 5.5 copy-start.34
  499.0 4.2 copy-start.22
  499.0 4.8 copy-start.25
  499.0 5.5 copy-start.3
  504.5 5.8 copy-start.24
  510.3 2.3 copy-start.6
  510.3 3.1 copy-start.8
  510.3 3.0 copy-start.29
  513.3 4.4 copy-start.36
  513.3 153.4 %copy-start.1 = (bf16[768,768]{1,0:T(8,128)(2,1)S(1)}, bf16[768,768]{1,0:T(8,128)(2,1)}, u32[]{:S(2)}) copy-start(bf16[768,768]{1,0:T(8,128)(2,1)} %param.16) | copy-start | bytes 3538948
  516.3 63.2 %copy-start.18 = (bf16[48,2304]{1,0:T(8,128)(2,1)S(1)}, bf16[48,2304]{1,0:T(8,128)(2,1)}, u32[]{:S(2)}) copy-start(bf16[48,2304]{1,0:T(8,128)(2,1)} %reduce-scatter.5.cloned.1.call-done) | copy-start | bytes 663556
  516.3 63.2 %collective-permute-start.2 = (bf16[48,2304]{1,0:T(8,128)(2,1)}, bf16[48,2304]{1,0:T(8,128)(2,1)S(1)}, u32[]{:S(2)}, u32[]{:S(2)}) collective-permute-start(bf16[48,2304]{1,0:T(8,128)(2,1)} %reduce-scatter.5.cloned.1.call-done), channel_id=1, source_target_pairs={{0,16},{16,0},{1,17},{17,1},{2,18},{18,2},{3,19},{19,3},{4,20},{20... | collective-permute-start | bytes 663560 | tf_op jit(solution)/shard_map/ppermute | solution.py:427
  578.1 80.3 %collective-permute-start.4 = (bf16[48,3072]{1,0:T(8,128)(2,1)}, bf16[48,3072]{1,0:T(8,128)(2,1)S(1)}, u32[]{:S(2)}, u32[]{:S(2)}) collective-permute-start(bf16[48,3072]{1,0:T(8,128)(2,1)} %reduce-scatter.9.cloned.1.call-done), channel_id=1, source_target_pairs={{0,16},{16,0},{1,17},{17,1},{2,18},{18,2},{3,19},{19,3},{4,20},{20... | collective-permute-start | bytes 884744 | tf_op jit(solution)/shard_map/ppermute | solution.py:427
  656.9 8.0 %collective-permute-start.5 = (bf16[192,768]{1,0:T(8,128)(2,1)}, bf16[192,768]{1,0:T(8,128)(2,1)S(1)}, u32[]{:S(2)}, u32[]{:S(2)}) collective-permute-start(bf16[192,768]{1,0:T(8,128)(2,1)} %reduce-scatter.11.cloned.1.call-done), channel_id=1, source_target_pairs={{0,16},{16,0},{1,17},{17,1},{2,18},{18,2},{3,19},{19,3},{4,20},{20... | collective-permute-start | bytes 884744 | tf_op jit(solution)/shard_map/ppermute | solution.py:427
  (5 other events, 5.4 us)
Sparse Core Ops, SparseCore 0:
  206.2 83.4 reduce-scatter.6
  421.8 77.8 reduce-scatter.4
  503.5 74.5 reduce-scatter.8
  582.3 74.5 reduce-scatter.10

commit v2 on v1

v2 whole, which is shorter than its diff:
```python
import functools
import itertools

import jax
import jax.numpy as jnp
import numpy as np
from jax import lax
from jax.experimental import pallas as pl
from jax.experimental.pallas import tpu as pltpu
from jax.sharding import PartitionSpec as P

HEADS = 12
HEAD_DIM = 64
PAIRS = HEADS // 2
PAIR = 2 * HEAD_DIM

LONG = 2048
SHORT = 512

LN_EPS = 1e-05
GELU_C = 0.7978845608028654
LOG2E = 1.4426950408889634
FAR = 1e30
VMEM_LIMIT = 60 * 2**20

BF16 = jnp.bfloat16
F32 = jnp.float32
NN = (((1,), (0,)), ((), ()))
NT = (((1,), (1,)), ((), ()))
TN = (((0,), (0,)), ((), ()))


def mm(left, right, dims):
    return lax.dot_general(left, right, dims, preferred_element_type=F32)


def pick_tile(block_len):
    return 256 if block_len % 256 == 0 else block_len


def layer_norm(values, gain):
    centre = jnp.mean(values, axis=-1, keepdims=True)
    shifted = values - centre
    spread = jnp.mean(shifted * shifted, axis=-1, keepdims=True)
    return shifted * lax.rsqrt(spread + LN_EPS) * gain


def gelu_tanh(values):
    return 0.5 * values * (1.0 + jnp.tanh(GELU_C * (values + 0.044715 * values * values * values)))


def split2(values):
    high = values.astype(BF16)
    return high, (values - high.astype(F32)).astype(BF16)


def half_masks(rows):
    lane = lax.broadcasted_iota(jnp.int32, (rows, PAIR), 1)
    return (lane < HEAD_DIM, lane >= HEAD_DIM)


class Layout:
    def __init__(self, rows, slots, tile, owned, blocks):
        self.tile, self.owned, self.blocks, self.tiles = tile, owned, blocks, owned * blocks
        self.aligned = SHORT % tile == 0
        self.count = 2 if blocks == 2 and owned >= 4 else 0
        ways = [[LONG, SHORT], [SHORT, LONG], [SHORT] * (rows // SHORT)]
        made = [self.plan(way + [0] * (slots - len(way)), me) for way in ways for me in range(blocks)]
        self.at, at, columns = {}, 0, []
        for name in made[0]:
            size = max(len(m[name]) for m in made)
            self.at[name] = (at, size)
            at += size
            columns.append([m[name] + m[name][-1:] * (size - len(m[name])) for m in made])
        self.table = np.array([sum((c[n] for c in columns), []) for n in range(len(made))], np.int32)

    def plan(self, lengths, me):
        tile, owned, blocks, tiles = self.tile, self.owned, self.blocks, self.tiles
        ends = [int(e) for e in np.cumsum(lengths)]
        low = [max([e for e in ends if e <= t * tile], default=0) // tile for t in range(tiles)]
        last = [min(e for e in ends if e > t * tile) for t in range(tiles)]
        length = [e - max([f for f in ends if f < e], default=0) for e in last]
        cost = [t - low[t] + 1 for t in range(tiles)]
        homes = [[b * owned + t for t in range(owned)] for b in range(blocks)]
        works = [list(h) for h in homes]
        given = [[0], [0]]
        if self.count:
            options = list(itertools.combinations(range(owned), self.count))

            def apart(choice):
                a, b = choice
                gain = sum(cost[owned + t] for t in b) - sum(cost[t] for t in a)
                return abs(sum(cost[:owned]) - sum(cost[owned:]) + 2 * gain), -sum(a), sum(b)

            given = list(min(itertools.product(options, options), key=apart))
            for side in range(2):
                for t, u in zip(given[side], given[1 - side]):
                    works[side][t] = (1 - side) * owned + u
        own = works[me]
        slot = [own.index(t) if t in own else -1 for t in range(tiles)]
        loc = [((t // owned - me) % blocks) * owned + t % owned for t in range(tiles)]
        far = works[1 - me] if blocks == 2 else [t if t not in own else -1 for t in range(tiles)]
        pairs = [(i, j) for i in range(tiles) for j in range(low[i], i + 1)]
        forward = [(i, j) for i, j in pairs if slot[i] >= 0]
        backward, flags = [], []
        for j in range(tiles):
            mine = [(i, j) for i in reversed(range(j, tiles)) if slot[i] >= 0 and low[i] <= j]
            marks = [1] * len(mine)
            if not mine:
                mine, marks = [(j, j)], [0]
            marks[0] += 2
            marks[-1] += 4
            backward += mine
            flags += marks
        late = [(i, j) for i, j in forward if any(f > i and low[f] <= j for f in far)]
        return {
            "ends": ends,
            "length": length,
            "loc": loc,
            "slot": slot,
            "own": own,
            "own_at": [loc[t] for t in own],
            "slot_loc": [slot[loc.index(t)] for t in range(tiles)],
            "far": far,
            "given": list(given[me]) if self.count else [0],
            "taken": list(given[1 - me]) if self.count else [0],
            "all_n": [len(pairs)],
            "all_i": [i for i, _ in pairs],
            "all_j": [j for _, j in pairs],
            "fwd_i": [i for i, _ in forward],
            "fwd_j": [j for _, j in forward],
            "fwd_f": [1 + 2 * (j == low[i]) for i, j in forward] + [0],
            "bwd_i": [i for i, _ in backward],
            "bwd_j": [j for _, j in backward],
            "bwd_f": flags + [0],
            "late_n": [len(late)],
            "late_i": [i for i, _ in late] + [0],
            "late_j": [j for _, j in late] + [0],
        }

    def chosen(self, lengths, me):
        way = jnp.where(lengths[0] == LONG, 0, jnp.where(lengths[1] == LONG, 1, 2))
        return lax.dynamic_index_in_dim(jnp.array(self.table), way * self.blocks + me, 0, keepdims=False)

    def get(self, numbers, name, index):
        return numbers[self.at[name][0] + index]

    def part(self, numbers, name):
        at, size = self.at[name]
        return numbers[at : at + size]

    def size(self, name):
        return self.at[name][1]


def tile_marks(layout, numbers, i, j):
    tile = layout.tile
    row = lax.broadcasted_iota(jnp.int32, (tile, tile), 0)
    key = lax.broadcasted_iota(jnp.int32, (tile, tile), 1)
    if layout.aligned:
        apart = key - row
        ahead = jnp.where(i == j, 0, tile)
        length = jnp.full((1, 1), layout.get(numbers, "length", i), jnp.int32)
        return apart < ahead, apart <= ahead, 4.0 / length.astype(F32)
    places = i * tile + lax.broadcasted_iota(jnp.int32, (tile, 1), 0)
    start = jnp.zeros((tile, 1), jnp.int32)
    end = jnp.full((tile, 1), 2**30, jnp.int32)
    for n in range(layout.size("ends")):
        edge = layout.get(numbers, "ends", n)
        start = jnp.maximum(start, jnp.where(places >= edge, edge, 0))
        end = jnp.minimum(end, jnp.where(places < edge, edge, 2**30))
    inside = j * tile + key >= start
    apart = (j - i) * tile + key - row
    return inside & (apart < 0), inside & (apart <= 0), 4.0 / (end - start).astype(F32)


def head0_scores(q_pair, k_pair, tile):
    first, _ = half_masks(tile)
    return mm(jnp.where(first, q_pair, 0), k_pair, NT) * HEAD_DIM**-0.5


def before_sum(chosen, tile):
    rows = lax.broadcasted_iota(jnp.int32, (tile, tile), 0)
    cols = lax.broadcasted_iota(jnp.int32, (tile, tile), 1)
    lower = (cols < rows).astype(F32).astype(BF16)
    high, low = split2(chosen)
    above = mm(lower, high, NN) + mm(lower, low, NN)
    return above, above[tile - 1 :, :] + chosen[tile - 1 :, :]


def after_sum(values, tile):
    rows = lax.broadcasted_iota(jnp.int32, (tile, tile), 0)
    cols = lax.broadcasted_iota(jnp.int32, (tile, tile), 1)
    upper = (cols > rows).astype(F32).astype(BF16)
    high, low = split2(values)
    below = mm(upper, high, NN) + mm(upper, low, NN)
    return below, below[:1, :] + values[:1, :]


def project_kernel(x_ref, w_ref, gain_ref, *refs):
    q_ref, k_ref, v_ref, normed_ref = refs[-4:]
    width = x_ref.shape[2]
    normed = layer_norm(x_ref[0].astype(F32), gain_ref[...]).astype(BF16)
    normed_ref[0] = normed
    for part, ref in enumerate((q_ref, k_ref, v_ref)):
        ref[0] = mm(normed, w_ref[:, part * width : (part + 1) * width], NN).astype(BF16)


UNROLL = 4


def sums_kernel(layout, numbers, q_ref, k_ref, kept_ref, sums_ref, column):
    tile = layout.tile
    last = layout.size("all_i") - 1

    def group_step(group, carry):
        for n in range(UNROLL):
            at = jnp.minimum(group * UNROLL + n, last)
            i, j = layout.get(numbers, "all_i", at), layout.get(numbers, "all_j", at)
            at_i, at_j = layout.get(numbers, "loc", i), layout.get(numbers, "loc", j)
            strict, _, _ = tile_marks(layout, numbers, i, j)
            scores = head0_scores(q_ref[at_i], k_ref[at_j], tile)
            chosen = jnp.where(strict, jnp.maximum(scores, 0.0), 0.0)
            column[group * UNROLL + n] = jnp.sum(chosen, axis=0, keepdims=True)
        return carry

    count = layout.get(numbers, "all_n", 0)
    lax.fori_loop(0, lax.div(count + (UNROLL - 1), jnp.int32(UNROLL)), group_step, 0)
    sums_ref[...] = jnp.zeros_like(sums_ref)

    def add_step(n, carry):
        i, j = layout.get(numbers, "all_i", n), layout.get(numbers, "all_j", n)
        kept_ref[i, j] = sums_ref[j]
        sums_ref[j] += column[n]
        return carry

    lax.fori_loop(0, count, add_step, 0)


def forward_kernel(layout, numbers, q_ref, k_ref, v_ref, kept_ref, att_ref, inv_ref, acc, pen):
    tile = layout.tile
    step = pl.program_id(0)
    i, j = layout.get(numbers, "fwd_i", step), layout.get(numbers, "fwd_j", step)
    flag = layout.get(numbers, "fwd_f", step)
    halves = half_masks(tile)

    @pl.when((flag & 2) != 0)
    def _():
        acc[...] = jnp.zeros_like(acc)

    @pl.when((flag & 1) != 0)
    def _():
        def logits_of(head):
            pair, half = divmod(head, 2)
            at = slice(pair * PAIR, (pair + 1) * PAIR)
            return mm(jnp.where(halves[half], q_ref[0, :, at], 0), k_ref[0, :, at], NT)

        def gather(head, numer):
            pair, half = divmod(head, 2)
            at = slice(pair * PAIR, (pair + 1) * PAIR)
            acc[head] += mm(numer, jnp.where(halves[half], v_ref[0, :, at], 1), NN)

        raw = {head: logits_of(head) for head in range(3)}
        strict, allowed, rate = tile_marks(layout, numbers, i, j)
        chosen = jnp.where(strict, jnp.maximum(raw[0] * HEAD_DIM**-0.5, 0.0), 0.0)
        above, _ = before_sum(chosen, tile)
        pen[...] = jnp.where(allowed, (rate * LOG2E) * (kept_ref[i, j] + above), FAR)
        waiting = {}
        for head in range(HEADS + 2):
            if 3 <= head + 3 < HEADS:
                raw[head + 3] = logits_of(head + 3)
            if head < HEADS:
                waiting[head] = jnp.exp2(raw.pop(head) * (HEAD_DIM**-0.5 * LOG2E) - pen[...]).astype(BF16)
            if head >= 2:
                gather(head - 2, waiting.pop(head - 2))

        @pl.when(i == j)
        def _():
            for pair in range(PAIRS):
                at = slice(pair * PAIR, (pair + 1) * PAIR)
                low, high = acc[2 * pair], acc[2 * pair + 1]
                numer = jnp.where(halves[0], low, high)
                inverse = 1.0 / pltpu.roll(jnp.where(halves[0], high, low), HEAD_DIM, 1)
                att_ref[0, :, at] = numer * inverse
                inv_ref[0, :, at] = inverse


def middle_kernel(
    tile, owned, chunk,
    att_ref, inv_ref, x_ref, cot_ref, wo_ref, wu_ref, wd_ref, gain_ref,
    out_ref, branch_ref, dx_ref, gain_grad_ref, grads_ref,
    hid_s, dpre_s, low_s, normed_s, branch_s, stage_down, stage_rest, sems,
):
    step = pl.program_id(0)
    width = x_ref.shape[2]
    hid = wu_ref.shape[1]
    parts = hid // width
    joined = len(stage_rest.shape) == 4

    def shipment(n):
        source = stage_down.at[n] if n < parts else stage_rest.at[n - parts]
        if not joined:
            target = grads_ref.at[n]
        elif n < parts:
            some, long = stage_down.shape[1:3]
            target = grads_ref.at[pl.ds(n * some, some), pl.ds(0, long), :]
        else:
            share = stage_rest.shape[2]
            target = grads_ref.at[:, pl.ds(share * n, share), :]
        return pltpu.make_async_copy(source, target, sems.at[n])

    def ship(n, block):
        stage, at = (stage_down, n) if n < parts else (stage_rest, n - parts)
        stage[at] = block.astype(BF16).reshape(stage.shape[1:])
        shipment(n).start()

    @pl.when(step == 0)
    def _():
        gain_grad_ref[...] = jnp.zeros_like(gain_grad_ref)

    @pl.when(step < owned)
    def _():
        at = pl.ds(pl.multiple_of(step * tile, tile), tile)
        attended = att_ref[0]
        cot = cot_ref[at, :]
        gain = gain_ref[...]
        low = attended.astype(BF16)
        low_s[at, :] = low
        residual = x_ref[0].astype(F32) + mm(low, wo_ref[...], NN)
        centre = jnp.mean(residual, axis=1, keepdims=True)
        shifted = residual - centre
        scale = lax.rsqrt(jnp.mean(shifted * shifted, axis=1, keepdims=True) + LN_EPS)
        xhat = shifted * scale
        normed = (xhat * gain).astype(BF16)
        normed_s[at, :] = normed
        result = residual
        d_normed = jnp.zeros((tile, width), F32)
        for c in range(hid // chunk):
            cols = slice(c * chunk, (c + 1) * chunk)
            pre = mm(normed, wu_ref[:, cols], NN)
            square = pre * pre
            wave = jnp.tanh(GELU_C * pre * (1.0 + 0.044715 * square))
            rising = 0.5 * (1.0 + wave)
            hidden = (pre * rising).astype(BF16)
            slope = rising + (0.5 * GELU_C) * pre * (1.0 - wave * wave) * (1.0 + (3 * 0.044715) * square)
            d_pre = (mm(cot, wd_ref[cols, :], NT) * slope).astype(BF16)
            hid_s[at, cols] = hidden
            dpre_s[at, cols] = d_pre
            result = result + mm(hidden, wd_ref[cols, :], NN)
            d_normed = d_normed + mm(d_pre, wu_ref[:, cols], NT)
        out_ref[0] = result.astype(BF16)
        gain_grad_ref[...] += jnp.sum(d_normed * xhat, axis=0, keepdims=True)
        grown = d_normed * gain
        mean_grown = jnp.mean(grown, axis=1, keepdims=True)
        mean_both = jnp.mean(grown * xhat, axis=1, keepdims=True)
        branch = (cot.astype(F32) + scale * (grown - mean_grown - xhat * mean_both)).astype(BF16)
        branch_ref[0] = branch
        branch_s[at, :] = branch
        d_attended = mm(branch, wo_ref[...], NT).astype(BF16).astype(F32)
        scaled = (d_attended * inv_ref[0]).astype(BF16)
        product = scaled.astype(F32) * attended
        rows = lax.broadcasted_iota(jnp.int32, (PAIR, 2 * PAIR), 0)
        cols = lax.broadcasted_iota(jnp.int32, (PAIR, 2 * PAIR), 1)
        block = cols // HEAD_DIM
        spread = jnp.where(block == jnp.where(rows < HEAD_DIM, 1, 2), -1.0, 0.0).astype(BF16)
        lane = lax.broadcasted_iota(jnp.int32, (tile, 2 * PAIR), 1) % HEAD_DIM
        first, _ = half_masks(tile)
        for pair in range(PAIRS):
            here = slice(pair * PAIR, (pair + 1) * PAIR)
            high, rest = split2(product[:, here])
            minus_dot = mm(high, spread, NN) + mm(rest, spread, NN)
            dot_high, dot_low = split2(minus_dot)
            side = jnp.where(lane == 0, dot_high, jnp.where(lane == 1, dot_low, 0))
            mine = scaled[:, here]
            base = 2 * pair * PAIR
            dx_ref[0, :, base : base + PAIR] = jnp.where(first, mine, side[:, :PAIR])
            dx_ref[0, :, base + PAIR : base + 2 * PAIR] = jnp.where(first, side[:, PAIR:], mine)

    for c in range(parts):
        @pl.when(step == owned + c)
        def _(c=c):
            cols = slice(c * width, (c + 1) * width)
            ship(c, mm(hid_s[:, cols], cot_ref[...], TN))
            ship(parts + c, mm(normed_s[...], dpre_s[:, cols], TN))
            if c == parts - 1:
                ship(2 * parts, mm(low_s[...], branch_s[...], TN))
                for n in range(2 * parts + 1):
                    shipment(n).wait()


def backward_kernel(
    layout, numbers, q_ref, k_ref, v_ref, dx_ref, kept_ref,
    dq_ref, dk_ref, dv_ref, later_ref,
    acc_q, acc_k, acc_v, pen, dpen, later,
):
    tile = layout.tile
    step = pl.program_id(0)
    i, j = layout.get(numbers, "bwd_i", step), layout.get(numbers, "bwd_j", step)
    flag = layout.get(numbers, "bwd_f", step)
    halves = half_masks(tile)

    @pl.when(step == 0)
    def _():
        acc_q[...] = jnp.zeros_like(acc_q)
        later_ref[...] = jnp.zeros_like(later_ref)

    @pl.when((flag & 2) != 0)
    def _():
        acc_k[...] = jnp.zeros_like(acc_k)
        acc_v[...] = jnp.zeros_like(acc_v)
        later[...] = jnp.zeros_like(later)

    @pl.when((flag & 1) != 0)
    def _():
        slot = layout.get(numbers, "slot", i)
        scores0 = head0_scores(q_ref[0, :, :PAIR], k_ref[0, :, :PAIR], tile)

        def products(pair):
            at = slice(pair * PAIR, (pair + 1) * PAIR)
            k_pair, q_pair, v_pair = k_ref[0, :, at], q_ref[0, :, at], v_ref[0, :, at]
            made = []
            for half in range(2):
                head = 2 * pair + half
                scores = scores0 if head == 0 else mm(jnp.where(halves[half], q_pair, 0), k_pair, NT) * HEAD_DIM**-0.5
                dx = dx_ref[0, :, head * PAIR : (head + 1) * PAIR]
                made.append((scores, mm(dx, jnp.where(halves[half], v_pair, 1), NT)))
            return made

        made = {PAIRS - 1: products(PAIRS - 1)}
        ready = {}
        strict, allowed, rate = tile_marks(layout, numbers, i, j)
        chosen = jnp.where(strict, jnp.maximum(scores0, 0.0), 0.0)
        above, _ = before_sum(chosen, tile)
        pen[...] = jnp.where(allowed, (rate * LOG2E) * (kept_ref[i, j] + above), FAR)

        def pointwise(pair, made):
            grads, weights = [], []
            for scores, d_probs in made:
                numer = jnp.exp2(scores * LOG2E - pen[...])
                weights.append(numer.astype(BF16))
                grads.append(numer * d_probs)
            both = grads[0] + grads[1]
            if pair == PAIRS - 1:
                dpen[...] = both
            elif pair > 0:
                dpen[...] += both
            else:
                below, total = after_sum(dpen[...] + both, tile)
                picked = strict & (scores0 > 0.0)
                grads[0] = grads[0] + jnp.where(picked, -rate * (later[...] + below), 0.0)
                later[...] = later[...] + total
                later_ref[slot, j] = total
            return weights, [g.astype(BF16) for g in grads]

        def collect(pair, weights, lows):
            at = slice(pair * PAIR, (pair + 1) * PAIR)
            k_pair, q_pair = k_ref[0, :, at], q_ref[0, :, at]
            d_q = None
            for half in range(2):
                head = 2 * pair + half
                part = slice(half * HEAD_DIM, (half + 1) * HEAD_DIM)
                head_at = slice(head * HEAD_DIM, (head + 1) * HEAD_DIM)
                dx = dx_ref[0, :, head * PAIR : (head + 1) * PAIR]
                acc_v[head_at, :] += mm(dx, weights[half], TN)[part]
                acc_k[head_at, :] += mm(q_pair, lows[half], TN)[part]
                more = mm(lows[half], jnp.where(halves[half], k_pair, 0), NN)
                d_q = more if d_q is None else d_q + more
            acc_q[slot, :, at] += d_q

        for pair in range(PAIRS - 1, -2, -1):
            if pair > 0:
                made[pair - 1] = products(pair - 1)
            if pair >= 0:
                ready[pair] = pointwise(pair, made.pop(pair))
            if pair + 1 in ready:
                collect(pair + 1, *ready.pop(pair + 1))

    @pl.when((flag & 4) != 0)
    def _():
        dk_ref[0] = jnp.transpose((acc_k[...] * HEAD_DIM**-0.5).astype(BF16))
        dv_ref[0] = jnp.transpose(acc_v[...].astype(BF16))

    @pl.when(step == pl.num_programs(0) - 1)
    def _():
        for slot in range(acc_q.shape[0]):
            dq_ref[slot] = (acc_q[slot] * HEAD_DIM**-0.5).astype(BF16)


def late_kernel(
    layout, numbers, q_ref, k_ref, far_totals_ref, dq_in_ref, dk_in_ref,
    dq_ref, dk_ref,
    acc_q, acc_k,
):
    tile = layout.tile
    first, _ = half_masks(tile)
    acc_q[...] = jnp.zeros_like(acc_q)
    acc_k[...] = jnp.zeros_like(acc_k)
    count = layout.get(numbers, "late_n", 0)

    def group_step(group, carry):
        adds = []
        for n in range(UNROLL):
            at = group * UNROLL + n
            valid = at < count
            at = jnp.minimum(at, layout.size("late_i") - 1)
            i, j = layout.get(numbers, "late_i", at), layout.get(numbers, "late_j", at)
            slot, at_i, at_j = (layout.get(numbers, name, t) for name, t in (("slot", i), ("loc", i), ("loc", j)))
            slot = jnp.maximum(slot, 0)
            later = jnp.zeros((1, tile), F32)
            for f in range(layout.size("far")):
                later += jnp.where(valid & (layout.get(numbers, "far", f) > i), far_totals_ref[f, j], 0.0)
            strict, _, rate = tile_marks(layout, numbers, i, j)
            scores = head0_scores(q_ref[at_i], k_ref[at_j], tile)
            factor = (-(HEAD_DIM**-0.5) * rate) * later
            d_low = jnp.where(strict & (scores > 0.0), factor, 0.0).astype(BF16)
            adds.append((slot, at_j, mm(q_ref[at_i], d_low, TN), mm(d_low, k_ref[at_j], NN)))
        for slot, at_j, for_k, for_q in adds:
            acc_k[at_j] += for_k
            acc_q[slot] += for_q
        return carry

    lax.fori_loop(0, lax.div(count + (UNROLL - 1), jnp.int32(UNROLL)), group_step, 0)
    for slot in range(acc_q.shape[0]):
        dq_ref[slot] = (dq_in_ref[slot].astype(F32) + jnp.where(first, acc_q[slot], 0.0)).astype(BF16)

    def finish(t, carry):
        dk_ref[t] = (dk_in_ref[t].astype(F32) + jnp.where(first, jnp.transpose(acc_k[t]), 0.0)).astype(BF16)
        return carry

    lax.fori_loop(0, acc_k.shape[0], finish, 0)


def unproject_kernel(layout, base, numbers, dq_ref, dk_ref, dv_ref, normed_ref, w_ref, gain_ref, out_ref, gain_grad_ref):
    step = pl.program_id(0)
    width = normed_ref.shape[2]
    slot = layout.get(numbers, "slot_loc", base + step)

    @pl.when(step == 0)
    def _():
        gain_grad_ref[...] = jnp.zeros_like(gain_grad_ref)

    d_query = jnp.where(slot >= 0, dq_ref[0], jnp.zeros_like(dq_ref[0]))
    d_normed = (
        mm(dv_ref[0], w_ref[:, 2 * width :], NT)
        + mm(dk_ref[0], w_ref[:, width : 2 * width], NT)
        + mm(d_query, w_ref[:, :width], NT)
    )
    out_ref[0] = d_normed.astype(out_ref.dtype)
    gain_grad_ref[...] += jnp.sum(d_normed * normed_ref[0].astype(F32), axis=0, keepdims=True) / gain_ref[...]


def flat(ref, cols):
    block = ref[:, :, cols]
    return block.reshape(block.shape[0] * block.shape[1], block.shape[2])


def value_weight_kernel(normed_ref, dk_ref, dv_ref, out_ref):
    width = normed_ref.shape[2]
    half = width // 2
    normed = flat(normed_ref, slice(None))
    out_ref[:, :half] = mm(normed, flat(dk_ref, slice(half, width)), TN).astype(BF16)
    out_ref[:, half:] = mm(normed, flat(dv_ref, slice(None)), TN).astype(BF16)


def query_weight_kernel(layout, numbers, normed_ref, dq_ref, dk_ref, out_ref):
    width = normed_ref.shape[2]
    half = width // 2
    total = jnp.zeros((width, width), F32)
    for slot in range(layout.owned):
        total += mm(normed_ref[layout.get(numbers, "own_at", slot)], dq_ref[slot], TN)
    out_ref[:, :width] = total.astype(BF16)
    out_ref[:, width:] = mm(flat(normed_ref, slice(None)), flat(dk_ref, slice(0, half)), TN).astype(BF16)


def input_kernel(part_ref, back_ref, x_ref, branch_ref, gain_ref, out_ref):
    values = x_ref[0].astype(F32)
    shifted = values - jnp.mean(values, axis=1, keepdims=True)
    scale = lax.rsqrt(jnp.mean(shifted * shifted, axis=1, keepdims=True) + LN_EPS)
    xhat = shifted * scale
    grown = (part_ref[0] + back_ref[0].astype(F32)) * gain_ref[...]
    mean_grown = jnp.mean(grown, axis=1, keepdims=True)
    mean_both = jnp.mean(grown * xhat, axis=1, keepdims=True)
    dx = scale * (grown - mean_grown - xhat * mean_both)
    out_ref[0] = (branch_ref[0].astype(F32) + dx).astype(BF16)


SMEM = pl.BlockSpec(memory_space=pltpu.SMEM)
VMEM = pl.BlockSpec(memory_space=pltpu.VMEM)


def estimate(flops):
    flops = int(flops)
    return pl.CostEstimate(flops=flops, bytes_accessed=flops // 600, transcendentals=0)


def held(shape):
    return pl.BlockSpec(shape, lambda *_: (0,) * len(shape), pipeline_mode=pl.Buffered(1))


def fixed(shape):
    return pl.BlockSpec(shape, lambda *_: (0,) * len(shape))


def sds(shape, dtype):
    return jax.ShapeDtypeStruct(shape, dtype)


def project(x, weight, gain, tiles, first, into):
    owned, tile, width = x.shape
    outs = (sds((tiles, tile, width), BF16),) * 4
    row = pl.BlockSpec((1, tile, width), lambda s: (s, 0, 0))
    placed = pl.BlockSpec((1, tile, width), lambda s: (s + first, 0, 0))
    extra = [pl.BlockSpec(memory_space=pl.ANY)] * len(into)
    return pl.pallas_call(
        project_kernel,
        grid=(owned,),
        out_shape=outs,
        in_specs=[row, held(weight.shape), held(gain.shape)] + extra,
        out_specs=(placed,) * 4,
        input_output_aliases={3 + n: n for n in range(len(into))},
        compiler_params=pltpu.CompilerParams(vmem_limit_bytes=20 * 2**20),
        cost_estimate=estimate(2 * owned * tile * width * weight.shape[1]),
    )(x, weight, gain, *into)


def middle(attended, inverse, x, cot, wo, wu, wd, gain, dp_count):
    owned, tile, width = x.shape
    hid = wu.shape[1]
    parts = hid // width
    rows = owned * tile
    row = pl.BlockSpec((1, tile, width), lambda s: (jnp.minimum(s, owned - 1), 0, 0))
    wide = pl.BlockSpec((1, tile, 2 * width), lambda s: (jnp.minimum(s, owned - 1), 0, 0))

    share = width // dp_count
    joined = share % 16 == 0 and dp_count % parts == 0
    if joined:
        stage_down = (parts, dp_count // parts, share * parts, width)
        stage_rest = (parts + 1, dp_count, share, width)
        grads = (dp_count, share * (2 * parts + 1), width)
    else:
        stage_down, stage_rest, grads = ((n, width, width) for n in (parts, parts + 1, 2 * parts + 1))
    return pl.pallas_call(
        functools.partial(middle_kernel, tile, owned, width),
        grid=(owned + parts,),
        out_shape=(
            sds((owned, tile, width), BF16),
            sds((owned, tile, width), BF16),
            sds((owned, tile, 2 * width), BF16),
            sds((1, width), F32),
            sds(grads, BF16),
        ),
        in_specs=[
            row, row, row, held((rows, width)), held(wo.shape), held(wu.shape), held(wd.shape), held(gain.shape),
        ],
        out_specs=(
            row, row, wide,
            pl.BlockSpec((1, width), lambda s: (0, 0)),
            pl.BlockSpec(memory_space=pl.ANY),
        ),
        scratch_shapes=[
            pltpu.VMEM((rows, hid), BF16),
            pltpu.VMEM((rows, hid), BF16),
            pltpu.VMEM((rows, width), BF16),
            pltpu.VMEM((rows, width), BF16),
            pltpu.VMEM((rows, width), BF16),
            pltpu.VMEM(stage_down, BF16),
            pltpu.VMEM(stage_rest, BF16),
            pltpu.SemaphoreType.DMA((2 * parts + 1,)),
        ],
        compiler_params=pltpu.CompilerParams(vmem_limit_bytes=VMEM_LIMIT),
        cost_estimate=estimate(2 * rows * width * (3 * width + 6 * hid)),
    )(attended, inverse, x, cot, wo, wu, wd, gain)


def kernel_call(kernel, room, grid, numbers, operands, in_specs, outs, out_specs, scratch, flops, aliases=None):
    return pl.pallas_call(
        kernel,
        grid_spec=pltpu.PrefetchScalarGridSpec(
            num_scalar_prefetch=1, grid=grid, in_specs=in_specs, out_specs=out_specs, scratch_shapes=scratch
        ),
        out_shape=outs,
        input_output_aliases=aliases or {},
        compiler_params=pltpu.CompilerParams(vmem_limit_bytes=room * 2**20),
        cost_estimate=estimate(flops),
    )(numbers, *operands)


def run_sums(layout, numbers, q, k):
    tiles, tile, _ = q.shape
    every = pl.BlockSpec((tiles, tile, PAIR), lambda n, x: (0, 0, 0))
    kept, sums = (tiles, tiles, 1, tile), (tiles, 1, tile)
    groups = -(-layout.size("all_i") // UNROLL) * UNROLL
    return kernel_call(
        functools.partial(sums_kernel, layout), 12, (1,), numbers, (q, k), [every, every],
        (sds(kept, F32), sds(sums, F32)), (fixed(kept), fixed(sums)),
        [pltpu.VMEM((groups, 1, tile), F32)], tiles * tiles * tile * tile * PAIR,
    )


def run_forward(layout, numbers, q, k, v, kept):
    tiles, tile, width = q.shape
    get, owned = layout.get, layout.owned
    rows = pl.BlockSpec((1, tile, width), lambda n, x: (get(x, "loc", get(x, "fwd_i", n)), 0, 0))
    keys = pl.BlockSpec((1, tile, width), lambda n, x: (get(x, "loc", get(x, "fwd_j", n)), 0, 0))
    slots = pl.BlockSpec((1, tile, width), lambda n, x: (get(x, "slot", get(x, "fwd_i", n)), 0, 0))
    return kernel_call(
        functools.partial(forward_kernel, layout), 20, (layout.size("fwd_i"),), numbers,
        (q, k, v, kept), [rows, keys, keys, fixed(kept.shape)],
        (sds((owned, tile, width), F32),) * 2, (slots, slots),
        [pltpu.VMEM((HEADS, tile, PAIR), F32), pltpu.VMEM((tile, tile), F32)],
        4 * layout.size("fwd_i") * tile * tile * width,
    )


def run_backward(layout, numbers, q, k, v, dx, kept):
    tiles, tile, width = q.shape
    get, owned = layout.get, layout.owned
    rows = pl.BlockSpec((1, tile, width), lambda n, x: (get(x, "loc", get(x, "bwd_i", n)), 0, 0))
    keys = pl.BlockSpec((1, tile, width), lambda n, x: (get(x, "loc", get(x, "bwd_j", n)), 0, 0))
    slots = pl.BlockSpec(
        (1, tile, 2 * width), lambda n, x: (jnp.maximum(get(x, "slot", get(x, "bwd_i", n)), 0), 0, 0)
    )
    totals = (owned, tiles, 1, tile)
    return kernel_call(
        functools.partial(backward_kernel, layout), 28, (layout.size("bwd_i"),), numbers,
        (q, k, v, dx, kept), [rows, keys, keys, slots, fixed(kept.shape)],
        (
            sds((owned, tile, width), BF16),
            sds((tiles, tile, width), BF16),
            sds((tiles, tile, width), BF16),
            sds(totals, F32),
        ),
        (fixed((owned, tile, width)), keys, keys, fixed(totals)),
        [
            pltpu.VMEM((owned, tile, width), F32),
            pltpu.VMEM((width, tile), F32),
            pltpu.VMEM((width, tile), F32),
            pltpu.VMEM((tile, tile), F32),
            pltpu.VMEM((tile, tile), F32),
            pltpu.VMEM((1, tile), F32),
        ],
        10 * layout.size("bwd_i") * tile * tile * width,
    )


def run_late(layout, numbers, q, k, far_totals, dq, dk):
    tiles, tile, _ = q.shape
    owned = dq.shape[0]
    some = pl.BlockSpec((owned, tile, PAIR), lambda n, x: (0, 0, 0))
    every = pl.BlockSpec((tiles, tile, PAIR), lambda n, x: (0, 0, 0))
    return kernel_call(
        functools.partial(late_kernel, layout), 16, (1,), numbers,
        (q, k, far_totals, dq, dk), [every, every, fixed(far_totals.shape), some, every],
        (sds(dq.shape, BF16), sds(dk.shape, BF16)), (some, every),
        [pltpu.VMEM((owned, tile, PAIR), F32), pltpu.VMEM((tiles, PAIR, tile), F32)],
        6 * layout.size("late_i") * tile * tile * PAIR,
        {4: 0, 5: 1},
    )


def unproject(layout, numbers, base, count, dq, dk, dv, normed, weight, gain, dtype):
    tile, width = layout.tile, dq.shape[2]
    row = pl.BlockSpec((1, tile, width), lambda s, x: (s, 0, 0))
    placed = pl.BlockSpec((1, tile, width), lambda s, x: (base + s, 0, 0))
    picked = pl.BlockSpec((1, tile, width), lambda s, x: (jnp.maximum(layout.get(x, "slot_loc", base + s), 0), 0, 0))
    return kernel_call(
        functools.partial(unproject_kernel, layout, base), 20, (count,), numbers,
        (dq, dk, dv, normed, weight, gain),
        [picked, placed, placed, placed, held(weight.shape), held(gain.shape)],
        (sds((count, tile, width), dtype), sds((1, width), F32)), (row, fixed((1, width))),
        [], 2 * count * tile * width * weight.shape[1],
    )


def value_weight_grad(normed, dk, dv):
    width = normed.shape[2]
    return pl.pallas_call(
        value_weight_kernel,
        out_shape=sds((width, 3 * width // 2), BF16),
        in_specs=[VMEM] * 3,
        out_specs=VMEM,
        compiler_params=pltpu.CompilerParams(vmem_limit_bytes=30 * 2**20),
        cost_estimate=estimate(3 * normed.shape[0] * normed.shape[1] * width * width),
    )(normed, dk, dv)


def query_weight_grad(layout, numbers, normed, dq, dk):
    width = normed.shape[2]
    return pl.pallas_call(
        functools.partial(query_weight_kernel, layout),
        out_shape=sds((width, 3 * width // 2), BF16),
        in_specs=[SMEM, VMEM, VMEM, VMEM],
        out_specs=VMEM,
        compiler_params=pltpu.CompilerParams(vmem_limit_bytes=28 * 2**20),
        cost_estimate=estimate(2 * normed.shape[0] * normed.shape[1] * width * width),
    )(numbers, normed, dq, dk)


def finish_input(part, back, x, branch, gain):
    owned, tile, width = x.shape
    row = pl.BlockSpec((1, tile, width), lambda s: (s, 0, 0))
    return pl.pallas_call(
        input_kernel,
        grid=(owned,),
        out_shape=sds(x.shape, BF16),
        in_specs=[row, row, row, row, held(gain.shape)],
        out_specs=row,
        compiler_params=pltpu.CompilerParams(vmem_limit_bytes=16 * 2**20),
        cost_estimate=estimate(2 * owned * tile * width * 600),
    )(part, back, x, branch, gain)


def swap_seq(array):
    return lax.ppermute(array, "seq", [(0, 1), (1, 0)])


def powers(size):
    return [1 << n for n in range(size.bit_length() - 1)]


def is_power(size):
    return size & (size - 1) == 0


def sum_everywhere(values):
    for axis in ("seq", "dp"):
        size = lax.axis_size(axis)
        if not is_power(size):
            values = lax.psum(values, axis)
            continue
        for bit in powers(size):
            values = values + lax.ppermute(values, axis, [(i, i ^ bit) for i in range(size)])
    return values


def scatter_halving(grad, order):
    count = lax.axis_size("dp")
    index = lax.axis_index("dp")
    bits = len(powers(count))
    held_bits = list(range(bits))[::-1]
    parts = grad.reshape((2,) * bits + grad.shape[1:])
    for n in order:
        axis = held_bits.index(n)
        held_bits.remove(n)
        mine = (index >> n) & 1
        keep = lax.dynamic_index_in_dim(parts, mine, axis, keepdims=False)
        send = lax.dynamic_index_in_dim(parts, 1 - mine, axis, keepdims=False)
        got = lax.ppermute(send, "dp", [(i, i ^ (1 << n)) for i in range(count)])
        parts = (keep.astype(F32) + got.astype(F32)).astype(BF16)
    return parts


def on_device(
    tokens, cotangent, lengths, threshold, attn_gain, qkv_weight, out_weight, mlp_gain, up_weight, down_weight
):
    _, block_len, width = tokens.shape
    blocks = lax.axis_size("seq")
    dp_count = lax.axis_size("dp")
    me = lax.axis_index("seq")
    tile = pick_tile(block_len)
    owned = block_len // tile
    tiles = owned * blocks
    rows = blocks * block_len
    hid = up_weight.shape[1]
    token_own = tokens[0]
    cot_own = cotangent[0]
    attn_gain = attn_gain.reshape(1, width)
    mlp_gain = mlp_gain.reshape(1, width)
    by_tile = (owned, tile, width)

    layout = Layout(rows, lengths.shape[1], tile, owned, blocks)
    count = layout.count
    numbers = layout.chosen(lengths[0], me)
    given, taken = layout.part(numbers, "given"), layout.part(numbers, "taken")

    def put(array, pieces):
        for n in range(count):
            array = lax.dynamic_update_slice_in_dim(array, pieces[n][None], given[n], 0)
        return array

    def swap_tiles(array):
        if count == 0:
            return array
        sent = jnp.stack([lax.dynamic_index_in_dim(array, given[n], 0, False) for n in range(count)])
        return put(array, swap_seq(sent))

    x_own = token_own.reshape(by_tile)
    if blocks == 2:
        x_others = swap_seq(token_own).reshape(by_tile)
    else:
        gathered = lax.all_gather(token_own, "seq", axis=0, tiled=False)
        x_others = jnp.roll(gathered, -me, axis=0)[1:].reshape(tiles - owned, tile, width)
    cot_tiles, x_others = lax.optimization_barrier((cot_own.reshape(by_tile), x_others))
    cot = swap_tiles(cot_tiles).reshape(block_len, width)
    parts = project(x_own, qkv_weight, attn_gain, tiles, 0, ())
    q_all, k_all, v_all, normed_all = project(x_others, qkv_weight, attn_gain, tiles, owned, parts)
    x = x_own
    if count:
        x = put(x_own, [lax.dynamic_index_in_dim(x_others, taken[n], 0, False) for n in range(count)])

    kept, sums = run_sums(layout, numbers, q_all, k_all)
    attended, inverse = run_forward(layout, numbers, q_all, k_all, v_all, kept)
    limit = threshold[0].astype(F32) / 1024.0
    ends = jnp.cumsum(lengths[0])
    positions = jnp.arange(rows, dtype=jnp.int32)
    passed = positions[:, None] >= ends[None, :]
    start = jnp.max(jnp.where(passed, ends[None, :], 0), axis=1)
    end = jnp.min(jnp.where(passed, rows, ends[None, :]), axis=1)
    over = jnp.maximum(4.0 / (end - start).astype(F32) * sums.reshape(rows) - limit, 0.0)
    excess_part = jnp.sum(jnp.where(positions // block_len == me, over, 0.0))

    out_c, branch_c, dx, mlp_gain_grad, early_grads = middle(
        attended, inverse, x, cot, out_weight, up_weight, down_weight, mlp_gain, dp_count
    )
    output = swap_tiles(out_c)
    branch = swap_tiles(branch_c)
    parts_hid = hid // width
    if early_grads.shape[0] != dp_count or early_grads.ndim != 3 or early_grads.shape[1] == width:
        down_grad = early_grads[:parts_hid].reshape(dp_count, -1, width)
        rest = early_grads[parts_hid:].reshape(parts_hid + 1, dp_count, -1, width).transpose(1, 0, 2, 3)
        early_grads = jnp.concatenate([down_grad, rest.reshape(dp_count, -1, width)], axis=1)
    early = lax.psum_scatter(early_grads, "dp", scatter_dimension=0, tiled=False)

    dq, dk, dv, totals = run_backward(layout, numbers, q_all, k_all, v_all, dx, kept)
    dk, dv, output, branch = lax.optimization_barrier((dk, dv, output, branch))
    if blocks == 2:
        far_totals = swap_seq(totals)
    else:
        far_totals = lax.all_gather(totals, "seq", axis=0, tiled=True)
    value_grad = value_weight_grad(normed_all, dk, dv)
    dq, dk = run_late(layout, numbers, q_all, k_all, far_totals, dq, dk)

    def back_through(base, number, dtype):
        return unproject(layout, numbers, base, number, dq, dk, dv, normed_all, qkv_weight, attn_gain, dtype)

    away, gain_away = back_through(owned, tiles - owned, BF16)
    if blocks == 2:
        back = swap_seq(away)
    else:
        by_block = jnp.concatenate([jnp.zeros((owned, tile, width), BF16), away]).reshape(blocks, block_len, width)
        back = lax.psum_scatter(jnp.roll(by_block, me, axis=0), "seq", scatter_dimension=0, tiled=False)
        back = back.reshape(by_tile)
    away, dq, dk = lax.optimization_barrier((away, dq, dk))
    query_grad = query_weight_grad(layout, numbers, normed_all, dq, dk)
    d_part, gain_home = back_through(0, owned, F32)
    gains = sum_everywhere(
        jnp.concatenate([gain_away + gain_home, mlp_gain_grad, jnp.full((1, 128), excess_part)], axis=1)
    )

    def over_seq(piece):
        if blocks == 2:
            return piece.astype(F32) + swap_seq(piece).astype(F32)
        return lax.psum(piece, "seq").astype(F32)

    halves = [grad.reshape(dp_count, -1, 3 * width // 2) for grad in (query_grad, value_grad)]
    if is_power(dp_count) and dp_count > 1:
        bits = list(range(len(powers(dp_count))))
        halves = [scatter_halving(halves[0], bits), scatter_halving(halves[1], bits[:1] + bits[2:] + bits[1:2])]
    else:
        halves = [lax.psum_scatter(grad, "dp", scatter_dimension=0, tiled=False) for grad in halves]
    late = jnp.concatenate(halves, axis=1)
    back, late, early = lax.optimization_barrier((back, late, early))
    qkv_piece = over_seq(late)
    early = over_seq(early)
    input_grad = finish_input(d_part, back, x_own, branch, attn_gain)

    part = width // dp_count
    n_down = hid // dp_count
    down_piece = early[:n_down]
    up_piece = early[n_down : 2 * n_down].reshape(hid // width, part, width).transpose(1, 0, 2).reshape(part, hid)
    out_piece = early[2 * n_down :]
    at = lax.axis_index("dp") * part
    attn_piece = lax.dynamic_slice_in_dim(gains[0], at, part)
    mlp_piece = lax.dynamic_slice_in_dim(gains[0], width + at, part)
    excess = (gains[0, 2 * width : 2 * width + 1] / (dp_count * rows)).reshape(1)
    return (
        output.reshape(1, block_len, width),
        input_grad.reshape(1, block_len, width),
        attn_piece,
        qkv_piece,
        out_piece,
        mlp_piece,
        up_piece,
        down_piece,
        excess,
    )


def solution(mesh):
    return jax.shard_map(
        on_device,
        mesh=mesh,
        in_specs=(
            P("dp", "seq", None),
            P("dp", "seq", None),
            P("dp", None),
            P(),
            P(),
            P(),
            P(),
            P(),
            P(),
            P(),
        ),
        out_specs=(
            P("dp", "seq", None),
            P("dp", "seq", None),
            P("dp"),
            P("dp", None),
            P("dp", None),
            P("dp"),
            P("dp", None),
            P("dp", None),
            P(),
        ),
        check_vma=False,
    )
```

time: 685 us -> 381 us (0.56)
  blocking collectives: 154 us -> 0 us
  matrix products: 145 us -> 0 us
  Pallas kernels: 85.8 us -> 196 us
  waiting for transfers between devices: 121 us -> 66.2 us
  local copies, waits for them, and re-layouts: 90.6 us -> 54.8 us
  other arithmetic: 41.5 us -> 7.03 us
  between operations: 17.2 us -> 26.5 us
    dot_general x17 -> x0, matrix products: 145 us -> none  [the longest x15 123 us: mm(): return lax.dot_general(left, right, dims, preferred_element_type=F32)]
    all_gather x1 -> x0, blocking collectives: 113 us -> none  [on_device(): all_totals = lax.all_gather(jnp.sum(totals, axis=0), 'seq', axis=0)]
    pallas_call x3 -> x12, Pallas kernels: 85.8 us -> 196 us  [the longest x6 105 us: kernel_call(): pl.pallas_call(kernel, grid_spec=pltpu.PrefetchScalarGridSpec(num_scalar_...]
    reduce_scatter x4 -> x1, waiting for transfers between devices: 89.7 us -> 0.01 us  [on_device(): lax.psum_scatter(early_grads, 'dp', scatter_dimension=0, tiled=False)]
    psum x1 -> x0, blocking collectives: 40.8 us -> none  [on_device(): gains = lax.psum(gains, ('seq', 'dp'))]
    ppermute x6 -> x21, waiting for transfers between devices: 31.3 us -> 66.2 us  [the longest x8 30.9 us: swap_seq(): return lax.ppermute(array, 'seq', [(0, 1), (1, 0)])]
    reshape x5 -> x3, local copies, waits for them, and re-layouts: 21.8 us -> 1.45 us  [the longest x1 0.87 us: on_device(): early[n_down:2 * n_down].reshape(hid // width, part, width)]
    convert_element_type x7 -> x8, other arithmetic: 13.4 us -> 3.45 us  [scatter_halving(): parts = (keep.astype(F32) + got.astype(F32)).astype(BF16)]
  transfers between devices with their start and end apart: 10 -> 22, of which waited for: 4 -> 13; matrix products, arithmetic and copies ran while one was open for 22% -> 8% of each run, Pallas kernels for 8% -> 36%
where the time goes in v2:
time: 381 us; the launch traced here: 375 us
  Pallas kernels  196 us (51%)
  waiting for transfers between devices  66.2 us (17%)
  local copies, waits for them, and re-layouts  54.8 us (14%)
  between operations  26.5 us (7%)
  starting transfers between devices  24.6 us (6%)
  other arithmetic  7.03 us (2%)
    pallas_call x6, Pallas kernels, kernel_call(): pl.pallas_call(kernel, grid_spec=pltpu.PrefetchScalarGridSpec(num_scalar_...  105 us
    pallas_call x1, Pallas kernels, middle(): pl.pallas_call(functools.partial(middle_kernel, tile, owned, width), grid...  60.7 us
    ppermute x8, waiting for transfers between devices, swap_seq(): return lax.ppermute(array, 'seq', [(0, 1), (1, 0)])  30.9 us
    unnamed x62, local copies, waits for them, and re-layouts  30.6 us
    ppermute x8, waiting for transfers between devices, scatter_halving(): got = lax.ppermute(send, 'dp', [(i, i ^ 1 << n) for i in range(count)])  23.2 us
    pallas_call x2, Pallas kernels, project(): pl.pallas_call(project_kernel, grid=(owned,), out_shape=outs, in_specs=[r...  15.1 us
    ppermute x8, starting transfers between devices, swap_seq(): return lax.ppermute(array, 'seq', [(0, 1), (1, 0)])  15.1 us
    ppermute x5, waiting for transfers between devices, sum_everywhere(): lax.ppermute(values, axis, [(i, i ^ bit) for i in range(size)])  12.1 us
  transfers between devices with their start and end apart: 22, of which 13 were waited for; matrix products, arithmetic and copies ran while one was open for 8% of the time, Pallas kernels for 36%

profile of v2, /device:TPU:0, one launch (start us, length us, event | category | flops | bytes accessed | tf_op | source)
XLA Modules:
  0.0 375.3 jit_solution(13307308048411767243)
XLA Ops:
  7.2 3.0 copy.65
  10.2 3.0 collective-permute-start
  21.8 3.1 copy.53
  28.8 7.6 %shard_map.178 = (bf16[10,256,768]{2,1,0:T(8,128)(2,1)S(1)}, bf16[10,256,768]{2,1,0:T(8,128)(2,1)S(1)}, bf16[10,256,768]{2,1,0:T(8,128)(2,1)S(1)}, bf16[10,256,768]{2,1,0:T(8,128)(2,1)S(1)}) custom-call(bf16[5,256,768]{2,1,0:T(8,128)(2,1)} %bitcast.4.x_ref, bf16[768,2304]{1,0:T(8,128)(2,1)S(1)} %copy-done.7, f32[1,768]{1,0:T(1,128)S(1)} %reshape.185.gain_ref), custom_call_target="tpu_custom_call" | custom-call | flops 4529848320 | bytes 7549747 | tf_op jit(solution)/shard_map/pallas_call | solution.py:614
  36.4 20.0 %collective-permute-done = bf16[1280,768]{1,0:T(8,128)(2,1)} collective-permute-done((bf16[1280,768]{1,0:T(8,128)(2,1)}, bf16[1280,768]{1,0:T(8,128)(2,1)}, u32[]{:S(2)}, u32[]{:S(2)}) %collective-permute-start) | collective-permute-done | bytes 1966112 | tf_op jit(solution)/shard_map/ppermute | solution.py:814
  57.6 1.8 collective-permute-start.1
  59.4 7.6 %shard_map.179 = (bf16[10,256,768]{2,1,0:T(8,128)(2,1)S(1)}, bf16[10,256,768]{2,1,0:T(8,128)(2,1)S(1)}, bf16[10,256,768]{2,1,0:T(8,128)(2,1)S(1)}, bf16[10,256,768]{2,1,0:T(8,128)(2,1)S(1)}) custom-call(bf16[5,256,768]{2,1,0:T(8,128)(2,1)} %bitcast.3.x_ref, ...), custom_call_target="tpu_custom_call", output_to_operand_aliasing={{0}: (3, {}), {1}: (4, {}), {2}: (5, {}), {3}: (6, {})} | custom-call | flops 4529848320 | bytes 7549747 | tf_op jit(solution)/shard_map/pallas_call | solution.py:614
  67.0 4.6 %shard_map.180 = (f32[10,10,1,256]{3,2,1,0:T(1,128)S(1)}, f32[10,1,256]{2,1,0:T(1,128)S(1)}) custom-call(s32[320]{0:T(512)S(1)} %fusion.9.numbers, bf16[10,256,768]{2,1,0:T(8,128)(2,1)S(1)} %get-tuple-element.52.q_ref, bf16[10,256,768]{2,1,0:T(8,128)(2,1)S(1)} %get-tuple-element.53.k_ref), custom_call_target="tpu_custom_call" | custom-call | flops 838860800 | bytes 1398101 | tf_op jit(solution)/shard_map/pallas_call | solution.py:676
  72.2 1.8 dynamic-slice_dynamic-update-slice_fusion.1
  74.0 1.8 dynamic-slice_dynamic-update-slice_fusion.x_ref
  75.8 27.5 %shard_map.181 = (f32[5,256,768]{2,1,0:T(8,128)S(1)}, f32[5,256,768]{2,1,0:T(8,128)S(1)}) custom-call(s32[320]{0:T(512)S(1)} %fusion.9.numbers, bf16[10,256,768]{2,1,0:T(8,128)(2,1)S(1)} %get-tuple-element.52.q_ref, bf16[10,256,768]{2,1,0:T(8,128)(2,1)S(1)} %get-tuple-element.53.k_ref, bf16[10,256,768]{2,1,0:T(8,128)(2,1)S(1)} %get-tuple-element.54.v_ref, ...), custom_call_target="tpu_custom_call" | custom-call | flops 4026531840 | bytes 6710886 | tf_op jit(solution)/shard_map/pallas_call | solution.py:676
  103.3 1.9 copy-done.4
  105.2 2.0 copy-done.12
  107.2 2.0 copy-done.21
  109.1 1.8 copy-done.22
  112.6 60.7 %shard_map.182 = (bf16[5,256,768]{2,1,0:T(8,128)(2,1)}, bf16[5,256,768]{2,1,0:T(8,128)(2,1)}, bf16[5,256,1536]{2,1,0:T(8,128)(2,1)}, f32[1,768]{1,0:T(1,128)}, bf16[16,432,768]{2,1,0:T(8,128)(2,1)}) custom-call(f32[5,256,768]{2,1,0:T(8,128)} %copy-done.21, f32[5,256,768]{2,1,0:T(8,128)} %copy-done.22, ...), custom_call_target="tpu_custom_call" | custom-call | flops 40768634880 | bytes 67947728 | tf_op jit(solution)/shard_map/pallas_call | solution.py:642
  178.3 1.6 constant_dynamic-slice_fusion.7
  180.0 1.6 collective-permute-start.3
  182.3 2.7 copy-done.5
  185.0 2.6 copy-done.13
  187.6 2.5 copy-done.23
  190.1 52.7 %shard_map.183 = (bf16[5,256,768]{2,1,0:T(8,128)(2,1)S(1)}, bf16[10,256,768]{2,1,0:T(8,128)(2,1)S(1)}, bf16[10,256,768]{2,1,0:T(8,128)(2,1)S(1)}, f32[5,10,1,256]{3,2,1,0:T(1,128)S(1)}) custom-call(s32[320]{0:T(512)S(1)} %fusion.9.numbers, bf16[10,256,768]{2,1,0:T(8,128)(2,1)S(1)} %copy-done.3, bf16[10,256,768]{2,1,0:T(8,128)(2,1)S(1)} %copy-done.5, ...), custom_call_target="tpu_custom_call" | custom-call | flops 12079595520 | bytes 20132660 | tf_op jit(solution)/shard_map/pallas_call | solution.py:676
  242.8 4.1 %collective-permute-start.4 = (f32[5,10,1,256]{3,2,1,0:T(1,128)S(1)}, f32[5,10,1,256]{3,2,1,0:T(1,128)S(1)}, u32[]{:S(2)}, u32[]{:S(2)}) collective-permute-start(f32[5,10,1,256]{3,2,1,0:T(1,128)S(1)} %get-tuple-element.65), channel_id=1, source_target_pairs={{0,16},{16,0},{1,17},{17,1},{2,18},{18,2},{3,19},{19,3},{4,20},{20... | collective-permute-start | bytes 153608 | tf_op jit(solution)/shard_map/ppermute | solution.py:814
  250.0 5.3 %shard_map.188 = bf16[768,1152]{1,0:T(8,128)(2,1)S(1)} custom-call(bf16[10,256,768]{2,1,0:T(8,128)(2,1)S(1)} %copy-done.1, bf16[10,256,768]{2,1,0:T(8,128)(2,1)S(1)} %get-tuple-element.67.dk_in_ref.dk_ref, bf16[10,256,768]{2,1,0:T(8,128)(2,1)S(1)} %get-tuple-element.70.dv_ref), custom_call_target="tpu_custom_call" | custom-call | flops 4529848320 | bytes 7549747 | tf_op jit(solution)/shard_map/pallas_call | solution.py:777
  255.4 7.3 %shard_map.184 = (bf16[5,256,768]{2,1,0:T(8,128)(2,1)S(1)}, bf16[10,256,768]{2,1,0:T(8,128)(2,1)S(1)}) custom-call(s32[320]{0:T(512)S(1)} %fusion.9.numbers, bf16[10,256,768]{2,1,0:T(8,128)(2,1)S(1)} %copy-done.3, bf16[10,256,768]{2,1,0:T(8,128)(2,1)S(1)} %copy-done.6, ...), custom_call_target="tpu_custom_call", output_to_operand_aliasing={{0}: (4, {}), {1}: (5, {})} | custom-call | flops 1056964608 | bytes 1761607 | tf_op jit(solution)/shard_map/pallas_call | solution.py:676
  262.7 6.4 %shard_map.185 = (bf16[5,256,768]{2,1,0:T(8,128)(2,1)S(1)}, f32[1,768]{1,0:T(1,128)S(1)}) custom-call(s32[320]{0:T(512)S(1)} %fusion.9.numbers, bf16[5,256,768]{2,1,0:T(8,128)(2,1)S(1)} %get-tuple-element.73.dq_ref, bf16[10,256,768]{2,1,0:T(8,128)(2,1)S(1)} %get-tuple-element.74.dk_ref, bf16[10,256,768]{2,1,0:T(8,128)(2,1)S(1)} %get-tuple-element.70.dv_ref, ...), custom_call_target="tpu_custom_call" | custom-call | flops 4529848320 | bytes 7549747 | tf_op jit(solution)/shard_map/pallas_call | solution.py:676
  270.4 4.3 %shard_map.187 = bf16[768,1152]{1,0:T(8,128)(2,1)S(1)} custom-call(s32[320]{0:T(512)S(1)} %fusion.9.numbers, bf16[10,256,768]{2,1,0:T(8,128)(2,1)S(1)} %copy-done.1, bf16[5,256,768]{2,1,0:T(8,128)(2,1)S(1)} %get-tuple-element.73.dq_ref, bf16[10,256,768]{2,1,0:T(8,128)(2,1)S(1)} %get-tuple-element.74.dk_ref), custom_call_target="tpu_custom_call" | custom-call | flops 3019898880 | bytes 5033164 | tf_op jit(solution)/shard_map/pallas_call | solution.py:789
  279.5 6.4 %shard_map.186 = (f32[5,256,768]{2,1,0:T(8,128)S(1)}, f32[1,768]{1,0:T(1,128)S(1)}) custom-call(s32[320]{0:T(512)S(1)} %fusion.9.numbers, bf16[5,256,768]{2,1,0:T(8,128)(2,1)S(1)} %get-tuple-element.73.dq_ref, bf16[10,256,768]{2,1,0:T(8,128)(2,1)S(1)} %get-tuple-element.74.dk_ref, bf16[10,256,768]{2,1,0:T(8,128)(2,1)S(1)} %copy-done.9, ...), custom_call_target="tpu_custom_call" | custom-call | flops 4529848320 | bytes 7549747 | tf_op jit(solution)/shard_map/pallas_call | solution.py:676
  285.9 1.9 copy-done.10
  288.0 3.6 collective-permute-done.14
  292.9 1.8 collective-permute-start.16
  294.6 1.9 collective-permute-done.16
  296.6 3.6 collective-permute-done.17
  301.1 2.0 collective-permute-start.5
  303.1 1.7 collective-permute-done.18
  306.1 1.6 fusion.1
  307.8 1.8 collective-permute-start.7
  311.1 5.5 %collective-permute-done.7 = bf16[2,2,48,1152]{3,2,0,1:T(8,128)(2,1)S(1)} collective-permute-done((bf16[2,2,48,1152]{3,2,0,1:T(8,128)(2,1)S(1)}, bf16[2,2,48,1152]{3,2,0,1:T(8,128)(2,1)S(1)}, u32[]{:S(2)}, u32[]{:S(2)}) %collective-permute-start.7) | collective-permute-done | bytes 442400 | tf_op jit(solution)/shard_map/ppermute | solution.py:848
  317.7 6.6 %collective-permute-done.11 = bf16[2,2,48,1152]{3,2,1,0:T(8,128)(2,1)S(1)} collective-permute-done((bf16[2,2,48,1152]{3,2,1,0:T(8,128)(2,1)S(1)}, bf16[2,2,48,1152]{3,2,1,0:T(8,128)(2,1)S(1)}, u32[]{:S(2)}, u32[]{:S(2)}) %collective-permute-start.11) | collective-permute-done | bytes 442400 | tf_op jit(solution)/shard_map/ppermute | solution.py:848
  324.6 2.7 collective-permute-done.8
  328.9 5.3 %collective-permute-done.12 = bf16[2,48,1152]{2,1,0:T(8,128)(2,1)S(1)} collective-permute-done((bf16[2,48,1152]{2,1,0:T(8,128)(2,1)S(1)}, bf16[2,48,1152]{2,1,0:T(8,128)(2,1)S(1)}, u32[]{:S(2)}, u32[]{:S(2)}) %collective-permute-start.12) | collective-permute-done | bytes 221216 | tf_op jit(solution)/shard_map/ppermute | solution.py:848
  334.3 1.7 collective-permute-start.13
  336.0 3.1 collective-permute-done.13
  339.1 5.1 %collective-permute-done.5.back_ref = bf16[5,256,768]{2,1,0:T(8,128)(2,1)S(1)} collective-permute-done((bf16[5,256,768]{2,1,0:T(8,128)(2,1)}, bf16[5,256,768]{2,1,0:T(8,128)(2,1)S(1)}, u32[]{:S(2)}, u32[]{:S(2)}) %collective-permute-start.5) | collective-permute-done | bytes 1966112 | tf_op jit(solution)/shard_map/ppermute | solution.py:814
  345.5 1.7 collective-permute-start.19
  348.1 2.1 copy-done.11
  351.8 5.8 %shard_map.189 = bf16[5,256,768]{2,1,0:T(8,128)(2,1)} custom-call(f32[5,256,768]{2,1,0:T(8,128)S(1)} %copy-done.11, bf16[5,256,768]{2,1,0:T(8,128)(2,1)S(1)} %copy-done.16, bf16[5,256,768]{2,1,0:T(8,128)(2,1)} %bitcast.4.x_ref, bf16[5,256,768]{2,1,0:T(8,128)(2,1)S(1)} %copy-done.14, f32[1,768]{1,0:T(1,128)S(1)} %reshape.185.gain_ref), custom_call_target="tpu_custom_call" | custom-call | flops 1179648000 | bytes 1966080 | tf_op jit(solution)/shard_map/pallas_call | solution.py:802
  358.4 5.9 %collective-permute-done.20 = bf16[432,768]{1,0:T(8,128)(2,1)S(1)} collective-permute-done((bf16[432,768]{1,0:T(8,128)(2,1)}, bf16[432,768]{1,0:T(8,128)(2,1)S(1)}, u32[]{:S(2)}, u32[]{:S(2)}) %collective-permute-start.20) | collective-permute-done | bytes 663584 | tf_op jit(solution)/shard_map/ppermute | solution.py:814
  (129 shorter events, 35.6 us)
Async XLA Ops:
  7.2 6.0 %copy-start.29 = (s32[1,5]{1,0:T(1,128)S(1)}, s32[1,5]{1,0:T(1,128)}, u32[]{:S(2)}) copy-start(s32[1,5]{1,0:T(1,128)} %param.13) | copy-start | bytes 64
  7.2 338.3 %reduce-scatter.2.cloned.1.call-start = ((), (), s32[]{:S(2)}) async-start(), calls=%async_computation.1 | async-start | bytes 11280384 | tf_op jit(solution)/shard_map/reduce_scatter | solution.py:922
  10.2 46.1 %collective-permute-start = (bf16[1280,768]{1,0:T(8,128)(2,1)}, bf16[1280,768]{1,0:T(8,128)(2,1)}, u32[]{:S(2)}, u32[]{:S(2)}) collective-permute-start(bf16[1280,768]{1,0:T(8,128)(2,1)} %bitcast.2), channel_id=1, source_target_pairs={{0,16},{16,0},{1,17},{17,1},{2,18},{18,2},{3,19},{19,3},{4,20},{20... | collective-permute-start | bytes 5898248 | tf_op jit(solution)/shard_map/ppermute | solution.py:814
  21.7 3.1 copy-start.26
  21.7 3.1 copy-start.27
  21.7 7.0 %copy-start.7 = (bf16[768,2304]{1,0:T(8,128)(2,1)S(1)}, bf16[768,2304]{1,0:T(8,128)(2,1)}, u32[]{:S(2)}) copy-start(bf16[768,2304]{1,0:T(8,128)(2,1)} %w_ref.7) | copy-start | bytes 10616836
  57.6 53.4 %collective-permute-start.1 = (bf16[2,256,768]{2,1,0:T(8,128)(2,1)S(1)}, bf16[2,256,768]{2,1,0:T(8,128)(2,1)S(1)}, u32[]{:S(2)}, u32[]{:S(2)}) collective-permute-start(bf16[2,256,768]{2,1,0:T(8,128)(2,1)S(1)} %pad_maximum_fusion), channel_id=1, source_target_pairs={{0,16},{16,0},{1,17},{17,1},{2,18},{18,2},{3,19},{19,3},{4,20},{20... | collective-permute-start | bytes 2359304 | tf_op jit(solution)/shard_map/ppermute | solution.py:814
  67.0 4.7 %copy-start = (bf16[10,256,768]{2,1,0:T(8,128)(2,1)}, bf16[10,256,768]{2,1,0:T(8,128)(2,1)S(1)}, u32[]{:S(2)}) copy-start(bf16[10,256,768]{2,1,0:T(8,128)(2,1)S(1)} %get-tuple-element.71.normed_ref) | copy-start | bytes 11796484
  67.0 8.9 %copy-start.2 = (bf16[10,256,768]{2,1,0:T(8,128)(2,1)}, bf16[10,256,768]{2,1,0:T(8,128)(2,1)S(1)}, u32[]{:S(2)}) copy-start(bf16[10,256,768]{2,1,0:T(8,128)(2,1)S(1)} %get-tuple-element.52.q_ref) | copy-start | bytes 11796484
  72.2 31.1 %copy-start.19 = (f32[10,10,1,256]{3,2,1,0:T(1,128)}, f32[10,10,1,256]{3,2,1,0:T(1,128)S(1)}, u32[]{:S(2)}) copy-start(f32[10,10,1,256]{3,2,1,0:T(1,128)S(1)} %get-tuple-element.55.kept_ref) | copy-start | bytes 307204
  103.3 1.9 copy-start.4
  105.2 2.0 copy-start.12
  107.2 2.0 copy-start.21
  109.1 1.8 copy-start.22
  178.3 4.0 %copy-start.3 = (bf16[10,256,768]{2,1,0:T(8,128)(2,1)S(1)}, bf16[10,256,768]{2,1,0:T(8,128)(2,1)}, u32[]{:S(2)}) copy-start(bf16[10,256,768]{2,1,0:T(8,128)(2,1)} %copy-done.2) | copy-start | bytes 11796484
  179.9 2.3 copy-start.20
  180.0 66.9 %collective-permute-start.3 = (bf16[2,256,768]{2,1,0:T(8,128)(2,1)S(1)}, bf16[2,256,768]{2,1,0:T(8,128)(2,1)S(1)}, u32[]{:S(2)}, u32[]{:S(2)}) collective-permute-start(bf16[2,256,768]{2,1,0:T(8,128)(2,1)S(1)} %pad_maximum_fusion.2), channel_id=1, source_target_pairs={{0,16},{16,0},{1,17},{17,1},{2,18},{18,2},{3,19},{19,3},{4,20},{20... | collective-permute-start | bytes 2359304 | tf_op jit(solution)/shard_map/ppermute | solution.py:814
  181.7 66.8 %collective-permute-start.2 = (bf16[2,256,768]{2,1,0:T(8,128)(2,1)S(1)}, bf16[2,256,768]{2,1,0:T(8,128)(2,1)S(1)}, u32[]{:S(2)}, u32[]{:S(2)}) collective-permute-start(bf16[2,256,768]{2,1,0:T(8,128)(2,1)S(1)} %pad_maximum_fusion.1), channel_id=1, source_target_pairs={{0,16},{16,0},{1,17},{17,1},{2,18},{18,2},{3,19},{19,3},{4,20},{20... | collective-permute-start | bytes 2359304 | tf_op jit(solution)/shard_map/ppermute | solution.py:814
  182.3 2.7 copy-start.5
  185.0 2.6 copy-start.13
  187.6 2.5 copy-start.23
  190.1 59.9 %copy-start.1 = (bf16[10,256,768]{2,1,0:T(8,128)(2,1)S(1)}, bf16[10,256,768]{2,1,0:T(8,128)(2,1)}, u32[]{:S(2)}) copy-start(bf16[10,256,768]{2,1,0:T(8,128)(2,1)} %copy-done) | copy-start | bytes 11796484
  242.8 19.9 %copy-start.8 = (bf16[10,256,768]{2,1,0:T(8,128)(2,1)}, bf16[10,256,768]{2,1,0:T(8,128)(2,1)S(1)}, u32[]{:S(2)}) copy-start(bf16[10,256,768]{2,1,0:T(8,128)(2,1)S(1)} %get-tuple-element.70.dv_ref) | copy-start | bytes 11796484
  242.8 12.5 %collective-permute-start.4 = (f32[5,10,1,256]{3,2,1,0:T(1,128)S(1)}, f32[5,10,1,256]{3,2,1,0:T(1,128)S(1)}, u32[]{:S(2)}, u32[]{:S(2)}) collective-permute-start(f32[5,10,1,256]{3,2,1,0:T(1,128)S(1)} %get-tuple-element.65), channel_id=1, source_target_pairs={{0,16},{16,0},{1,17},{17,1},{2,18},{18,2},{3,19},{19,3},{4,20},{20... | collective-permute-start | bytes 153608 | tf_op jit(solution)/shard_map/ppermute | solution.py:814
  250.0 5.3 %copy-start.6 = (bf16[10,256,768]{2,1,0:T(8,128)(2,1)S(1)}, bf16[10,256,768]{2,1,0:T(8,128)(2,1)}, u32[]{:S(2)}) copy-start(bf16[10,256,768]{2,1,0:T(8,128)(2,1)} %copy-done.4) | copy-start | bytes 11796484
  276.7 29.3 %collective-permute-start.6 = (bf16[2,2,2,48,1152]{4,3,0,1,2:T(8,128)(2,1)}, bf16[2,2,2,48,1152]{4,3,0,1,2:T(8,128)(2,1)}, u32[]{:S(2)}, u32[]{:S(2)}) collective-permute-start(bf16[2,2,2,48,1152]{4,3,0,1,2:T(8,128)(2,1)} %bitcast.73), channel_id=1, source_target_pairs={{0,1},{1,0},{2,3},{3,2},{4,5},{5,4},{6,7},{7,6},{8,9},{9,8},{10,11... | collective-permute-start | bytes 2654216 | tf_op jit(solution)/shard_map/ppermute | solution.py:848
  276.7 2.8 copy-start.9
  278.8 9.0 %copy-start.28 = (f32[1,768]{1,0:T(1,128)S(1)}, f32[1,768]{1,0:T(1,128)}, u32[]{:S(2)}) copy-start(f32[1,768]{1,0:T(1,128)} %get-tuple-element.81) | copy-start | bytes 9220
  278.8 30.7 %collective-permute-start.10 = (bf16[2,2,2,48,1152]{4,3,2,0,1:T(8,128)(2,1)}, bf16[2,2,2,48,1152]{4,3,2,0,1:T(8,128)(2,1)}, u32[]{:S(2)}, u32[]{:S(2)}) collective-permute-start(bf16[2,2,2,48,1152]{4,3,2,0,1:T(8,128)(2,1)} %bitcast.72), channel_id=1, source_target_pairs={{0,1},{1,0},{2,3},{3,2},{4,5},{5,4},{6,7},{7,6},{8,9},{9,8},{10,11... | collective-permute-start | bytes 2654216 | tf_op jit(solution)/shard_map/ppermute | solution.py:848
  285.9 2.0 copy-start.10
  287.9 21.7 %copy-start.24 = (bf16[2,2,2,1,48,1152]{5,4,3,2,1,0:T(8,128)(2,1)S(1)}, bf16[2,2,2,1,48,1152]{5,4,3,2,1,0:T(8,128)(2,1)}, u32[]{:S(2)}) copy-start(bf16[2,2,2,1,48,1152]{5,4,3,2,1,0:T(8,128)(2,1)} %get-tuple-element.95) | copy-start | bytes 2654212
  287.9 3.7 collective-permute-start.14
  291.6 1.2 collective-permute-start.15
  292.9 3.7 collective-permute-start.16
  296.6 3.7 collective-permute-start.17
  300.3 4.6 %collective-permute-start.18 = (f32[1,1664]{1,0:T(1,128)S(1)}, f32[1,1664]{1,0:T(1,128)S(1)}, u32[]{:S(2)}, u32[]{:S(2)}) collective-permute-start(f32[1,1664]{1,0:T(1,128)S(1)} %add.178), channel_id=1, source_target_pairs={{0,8},{1,9},{2,10},{3,11},{4,12},{5,13},{6,14},{7,15},{8,0},{9,1},... | collective-permute-start | bytes 19976 | tf_op jit(solution)/shard_map/ppermute | solution.py:832
  301.1 43.1 %collective-permute-start.5 = (bf16[5,256,768]{2,1,0:T(8,128)(2,1)}, bf16[5,256,768]{2,1,0:T(8,128)(2,1)S(1)}, u32[]{:S(2)}, u32[]{:S(2)}) collective-permute-start(bf16[5,256,768]{2,1,0:T(8,128)(2,1)} %copy-done.18), channel_id=1, source_target_pairs={{0,16},{16,0},{1,17},{17,1},{2,18},{18,2},{3,19},{19,3},{4,20},{20... | collective-permute-start | bytes 5898248 | tf_op jit(solution)/shard_map/ppermute | solution.py:814
  307.8 8.9 %collective-permute-start.7 = (bf16[2,2,48,1152]{3,2,0,1:T(8,128)(2,1)S(1)}, bf16[2,2,48,1152]{3,2,0,1:T(8,128)(2,1)S(1)}, u32[]{:S(2)}, u32[]{:S(2)}) collective-permute-start(bf16[2,2,48,1152]{3,2,0,1:T(8,128)(2,1)S(1)} %dynamic-slice_bitcast_fusion.1), channel_id=1, source_target_pairs={{0,2},{1,3},{2,0},{3,1},{4,6},{5,7},{6,4},{7,5},{8,10},{9,11},{10,... | collective-permute-start | bytes 1327112 | tf_op jit(solution)/shard_map/ppermute | solution.py:848
  311.0 13.3 %collective-permute-start.11 = (bf16[2,2,48,1152]{3,2,1,0:T(8,128)(2,1)S(1)}, bf16[2,2,48,1152]{3,2,1,0:T(8,128)(2,1)S(1)}, u32[]{:S(2)}, u32[]{:S(2)}) collective-permute-start(bf16[2,2,48,1152]{3,2,1,0:T(8,128)(2,1)S(1)} %dynamic-slice_bitcast_fusion), channel_id=1, source_target_pairs={{0,4},{1,5},{2,6},{3,7},{4,0},{5,1},{6,2},{7,3},{8,12},{9,13},{10,... | collective-permute-start | bytes 1327112 | tf_op jit(solution)/shard_map/ppermute | solution.py:848
  316.8 10.5 %collective-permute-start.8 = (bf16[2,48,1152]{2,1,0:T(8,128)(2,1)S(1)}, bf16[2,48,1152]{2,1,0:T(8,128)(2,1)S(1)}, u32[]{:S(2)}, u32[]{:S(2)}) collective-permute-start(bf16[2,48,1152]{2,1,0:T(8,128)(2,1)S(1)} %dynamic-slice_bitcast_fusion.3), channel_id=1, source_target_pairs={{0,4},{1,5},{2,6},{3,7},{4,0},{5,1},{6,2},{7,3},{8,12},{9,13},{10,... | collective-permute-start | bytes 663560 | tf_op jit(solution)/shard_map/ppermute | solution.py:848
  324.4 23.6 %copy-start.14 = (bf16[5,256,768]{2,1,0:T(8,128)(2,1)S(1)}, bf16[5,256,768]{2,1,0:T(8,128)(2,1)}, u32[]{:S(2)}) copy-start(bf16[5,256,768]{2,1,0:T(8,128)(2,1)} %slice_dynamic-update-slice_fusion.branch_ref) | copy-start | bytes 5898244
  324.5 9.7 %collective-permute-start.12 = (bf16[2,48,1152]{2,1,0:T(8,128)(2,1)S(1)}, bf16[2,48,1152]{2,1,0:T(8,128)(2,1)S(1)}, u32[]{:S(2)}, u32[]{:S(2)}) collective-permute-start(bf16[2,48,1152]{2,1,0:T(8,128)(2,1)S(1)} %dynamic-slice_bitcast_fusion.2), channel_id=1, source_target_pairs={{0,8},{1,9},{2,10},{3,11},{4,12},{5,13},{6,14},{7,15},{8,0},{9,1},... | collective-permute-start | bytes 663560 | tf_op jit(solution)/shard_map/ppermute | solution.py:848
  327.4 8.5 %collective-permute-start.9 = (bf16[48,1152]{1,0:T(8,128)(2,1)S(1)}, bf16[48,1152]{1,0:T(8,128)(2,1)S(1)}, u32[]{:S(2)}, u32[]{:S(2)}) collective-permute-start(bf16[48,1152]{1,0:T(8,128)(2,1)S(1)} %dynamic-slice_bitcast_fusion.5), channel_id=1, source_target_pairs={{0,8},{1,9},{2,10},{3,11},{4,12},{5,13},{6,14},{7,15},{8,0},{9,1},... | collective-permute-start | bytes 331784 | tf_op jit(solution)/shard_map/ppermute | solution.py:848
  334.3 4.8 %collective-permute-start.13 = (bf16[48,1152]{1,0:T(8,128)(2,1)S(1)}, bf16[48,1152]{1,0:T(8,128)(2,1)S(1)}, u32[]{:S(2)}, u32[]{:S(2)}) collective-permute-start(bf16[48,1152]{1,0:T(8,128)(2,1)S(1)} %dynamic-slice_bitcast_fusion.4), channel_id=1, source_target_pairs={{0,2},{1,3},{2,0},{3,1},{4,6},{5,7},{6,4},{7,5},{8,10},{9,11},{10,... | collective-permute-start | bytes 331784 | tf_op jit(solution)/shard_map/ppermute | solution.py:848
  345.5 12.1 %collective-permute-start.19 = (bf16[48,2304]{1,0:T(8,128)(2,1)S(1)}, bf16[48,2304]{1,0:T(8,128)(2,1)S(1)}, u32[]{:S(2)}, u32[]{:S(2)}) collective-permute-start(bf16[48,2304]{1,0:T(8,128)(2,1)S(1)} %pad_maximum_fusion.3), channel_id=1, source_target_pairs={{0,16},{16,0},{1,17},{17,1},{2,18},{18,2},{3,19},{19,3},{4,20},{20... | collective-permute-start | bytes 663560 | tf_op jit(solution)/shard_map/ppermute | solution.py:814
  347.8 16.4 %collective-permute-start.20 = (bf16[432,768]{1,0:T(8,128)(2,1)}, bf16[432,768]{1,0:T(8,128)(2,1)S(1)}, u32[]{:S(2)}, u32[]{:S(2)}) collective-permute-start(bf16[432,768]{1,0:T(8,128)(2,1)} %bitcast.78), channel_id=1, source_target_pairs={{0,16},{16,0},{1,17},{17,1},{2,18},{18,2},{3,19},{19,3},{4,20},{20... | collective-permute-start | bytes 1990664 | tf_op jit(solution)/shard_map/ppermute | solution.py:814
  348.1 2.1 copy-start.11
  351.8 12.5 %copy-start.25 = (bf16[1,432,768]{2,1,0:T(8,128)(2,1)S(1)}, bf16[1,432,768]{2,1,0:T(8,128)(2,1)}, u32[]{:S(2)}) copy-start(bf16[1,432,768]{2,1,0:T(8,128)(2,1)} %reduce-scatter.2.cloned.1.call-done) | copy-start | bytes 1990660
  (4 other events, 4.7 us)
Sparse Core Ops, SparseCore 0:
  173.5 121.7 reduce-scatter.1

commit v3 on v2

--- a/solution.py
+++ b/solution.py
@@ -198,7 +198,8 @@
 
 
 def project_kernel(x_ref, w_ref, gain_ref, *refs):
-    q_ref, k_ref, v_ref, normed_ref = refs[-4:]
+    q_ref, k_ref, v_ref, normed_ref, x_out_ref = refs[-5:]
+    x_out_ref[0] = x_ref[0]
     width = x_ref.shape[2]
     normed = layer_norm(x_ref[0].astype(F32), gain_ref[...]).astype(BF16)
     normed_ref[0] = normed
@@ -287,8 +288,8 @@
 
 def middle_kernel(
     tile, owned, chunk,
-    att_ref, inv_ref, x_ref, cot_ref, wo_ref, wu_ref, wd_ref, gain_ref,
-    out_ref, branch_ref, dx_ref, gain_grad_ref, grads_ref,
+    numbers, att_ref, inv_ref, x_ref, cot_ref, wo_ref, wu_ref, wd_ref, gain_ref,
+    out_ref, branch_ref, dx_ref, grads_ref,
     hid_s, dpre_s, low_s, normed_s, branch_s, stage_down, stage_rest, sems,
 ):
     step = pl.program_id(0)
@@ -313,10 +314,6 @@
         stage, at = (stage_down, n) if n < parts else (stage_rest, n - parts)
         stage[at] = block.astype(BF16).reshape(stage.shape[1:])
         shipment(n).start()
-
-    @pl.when(step == 0)
-    def _():
-        gain_grad_ref[...] = jnp.zeros_like(gain_grad_ref)
 
     @pl.when(step < owned)
     def _():
@@ -339,17 +336,16 @@
             cols = slice(c * chunk, (c + 1) * chunk)
             pre = mm(normed, wu_ref[:, cols], NN)
             square = pre * pre
-            wave = jnp.tanh(GELU_C * pre * (1.0 + 0.044715 * square))
-            rising = 0.5 * (1.0 + wave)
+            wave = jnp.tanh(pre * (GELU_C + (GELU_C * 0.044715) * square))
+            rising = 0.5 + 0.5 * wave
             hidden = (pre * rising).astype(BF16)
-            slope = rising + (0.5 * GELU_C) * pre * (1.0 - wave * wave) * (1.0 + (3 * 0.044715) * square)
-            d_pre = (mm(cot, wd_ref[cols, :], NT) * slope).astype(BF16)
+            bend = pre * ((0.5 * GELU_C) + (1.5 * GELU_C * 0.044715) * square)
+            d_pre = (mm(cot, wd_ref[cols, :], NT) * (rising + bend * (1.0 - wave * wave))).astype(BF16)
             hid_s[at, cols] = hidden
             dpre_s[at, cols] = d_pre
             result = result + mm(hidden, wd_ref[cols, :], NN)
             d_normed = d_normed + mm(d_pre, wu_ref[:, cols], NT)
         out_ref[0] = result.astype(BF16)
-        gain_grad_ref[...] += jnp.sum(d_normed * xhat, axis=0, keepdims=True)
         grown = d_normed * gain
         mean_grown = jnp.mean(grown, axis=1, keepdims=True)
         mean_both = jnp.mean(grown * xhat, axis=1, keepdims=True)
@@ -530,23 +526,32 @@
     lax.fori_loop(0, acc_k.shape[0], finish, 0)
 
 
-def unproject_kernel(layout, base, numbers, dq_ref, dk_ref, dv_ref, normed_ref, w_ref, gain_ref, out_ref, gain_grad_ref):
-    step = pl.program_id(0)
-    width = normed_ref.shape[2]
-    slot = layout.get(numbers, "slot_loc", base + step)
-
-    @pl.when(step == 0)
-    def _():
-        gain_grad_ref[...] = jnp.zeros_like(gain_grad_ref)
-
+def through_weight(layout, base, numbers, dq_ref, dk_ref, dv_ref, w_ref):
+    width = dq_ref.shape[2]
+    slot = layout.get(numbers, "slot_loc", base + pl.program_id(0))
     d_query = jnp.where(slot >= 0, dq_ref[0], jnp.zeros_like(dq_ref[0]))
-    d_normed = (
+    return (
         mm(dv_ref[0], w_ref[:, 2 * width :], NT)
         + mm(dk_ref[0], w_ref[:, width : 2 * width], NT)
         + mm(d_query, w_ref[:, :width], NT)
     )
-    out_ref[0] = d_normed.astype(out_ref.dtype)
-    gain_grad_ref[...] += jnp.sum(d_normed * normed_ref[0].astype(F32), axis=0, keepdims=True) / gain_ref[...]
+
+
+def away_kernel(layout, base, numbers, dq_ref, dk_ref, dv_ref, w_ref, out_ref):
+    out_ref[0] = through_weight(layout, base, numbers, dq_ref, dk_ref, dv_ref, w_ref).astype(BF16)
+
+
+def home_kernel(layout, numbers, dq_ref, dk_ref, dv_ref, w_ref, back_ref, x_ref, branch_ref, gain_ref, out_ref):
+    values = x_ref[0].astype(F32)
+    shifted = values - jnp.mean(values, axis=1, keepdims=True)
+    scale = lax.rsqrt(jnp.mean(shifted * shifted, axis=1, keepdims=True) + LN_EPS)
+    xhat = shifted * scale
+    d_normed = through_weight(layout, 0, numbers, dq_ref, dk_ref, dv_ref, w_ref)
+    grown = (d_normed + back_ref[0].astype(F32)) * gain_ref[...]
+    mean_grown = jnp.mean(grown, axis=1, keepdims=True)
+    mean_both = jnp.mean(grown * xhat, axis=1, keepdims=True)
+    dx = scale * (grown - mean_grown - xhat * mean_both)
+    out_ref[0] = (branch_ref[0].astype(F32) + dx).astype(BF16)
 
 
 def flat(ref, cols):
@@ -572,18 +577,6 @@
     out_ref[:, width:] = mm(flat(normed_ref, slice(None)), flat(dk_ref, slice(0, half)), TN).astype(BF16)
 
 
-def input_kernel(part_ref, back_ref, x_ref, branch_ref, gain_ref, out_ref):
-    values = x_ref[0].astype(F32)
-    shifted = values - jnp.mean(values, axis=1, keepdims=True)
-    scale = lax.rsqrt(jnp.mean(shifted * shifted, axis=1, keepdims=True) + LN_EPS)
-    xhat = shifted * scale
-    grown = (part_ref[0] + back_ref[0].astype(F32)) * gain_ref[...]
-    mean_grown = jnp.mean(grown, axis=1, keepdims=True)
-    mean_both = jnp.mean(grown * xhat, axis=1, keepdims=True)
-    dx = scale * (grown - mean_grown - xhat * mean_both)
-    out_ref[0] = (branch_ref[0].astype(F32) + dx).astype(BF16)
-
-
 SMEM = pl.BlockSpec(memory_space=pltpu.SMEM)
 VMEM = pl.BlockSpec(memory_space=pltpu.VMEM)
 
@@ -607,7 +600,7 @@
 
 def project(x, weight, gain, tiles, first, into):
     owned, tile, width = x.shape
-    outs = (sds((tiles, tile, width), BF16),) * 4
+    outs = (sds((tiles, tile, width), BF16),) * 5
     row = pl.BlockSpec((1, tile, width), lambda s: (s, 0, 0))
     placed = pl.BlockSpec((1, tile, width), lambda s: (s + first, 0, 0))
     extra = [pl.BlockSpec(memory_space=pl.ANY)] * len(into)
@@ -616,20 +609,23 @@
         grid=(owned,),
         out_shape=outs,
         in_specs=[row, held(weight.shape), held(gain.shape)] + extra,
-        out_specs=(placed,) * 4,
+        out_specs=(placed,) * 5,
         input_output_aliases={3 + n: n for n in range(len(into))},
         compiler_params=pltpu.CompilerParams(vmem_limit_bytes=20 * 2**20),
         cost_estimate=estimate(2 * owned * tile * width * weight.shape[1]),
     )(x, weight, gain, *into)
 
 
-def middle(attended, inverse, x, cot, wo, wu, wd, gain, dp_count):
-    owned, tile, width = x.shape
+def middle(layout, numbers, attended, inverse, x, cot, wo, wu, wd, gain, dp_count):
+    owned, tile, width = attended.shape
     hid = wu.shape[1]
     parts = hid // width
     rows = owned * tile
-    row = pl.BlockSpec((1, tile, width), lambda s: (jnp.minimum(s, owned - 1), 0, 0))
-    wide = pl.BlockSpec((1, tile, 2 * width), lambda s: (jnp.minimum(s, owned - 1), 0, 0))
+    row = pl.BlockSpec((1, tile, width), lambda s, n: (jnp.minimum(s, owned - 1), 0, 0))
+    wide = pl.BlockSpec((1, tile, 2 * width), lambda s, n: (jnp.minimum(s, owned - 1), 0, 0))
+
+    def token_place(s, n):
+        return layout.get(n, "own_at", jnp.minimum(s, owned - 1)), 0, 0
 
     share = width // dp_count
     joined = share % 16 == 0 and dp_count % parts == 0
@@ -639,25 +635,21 @@
         grads = (dp_count, share * (2 * parts + 1), width)
     else:
         stage_down, stage_rest, grads = ((n, width, width) for n in (parts, parts + 1, 2 * parts + 1))
-    return pl.pallas_call(
-        functools.partial(middle_kernel, tile, owned, width),
-        grid=(owned + parts,),
-        out_shape=(
+    return kernel_call(
+        functools.partial(middle_kernel, tile, owned, width), VMEM_LIMIT // 2**20, (owned + parts,), numbers,
+        (attended, inverse, x, cot, wo, wu, wd, gain),
+        [
+            row, row, pl.BlockSpec((1, tile, width), token_place), held((rows, width)),
+            held(wo.shape), held(wu.shape), held(wd.shape), held(gain.shape),
+        ],
+        (
             sds((owned, tile, width), BF16),
             sds((owned, tile, width), BF16),
             sds((owned, tile, 2 * width), BF16),
-            sds((1, width), F32),
             sds(grads, BF16),
         ),
-        in_specs=[
-            row, row, row, held((rows, width)), held(wo.shape), held(wu.shape), held(wd.shape), held(gain.shape),
-        ],
-        out_specs=(
-            row, row, wide,
-            pl.BlockSpec((1, width), lambda s: (0, 0)),
-            pl.BlockSpec(memory_space=pl.ANY),
-        ),
-        scratch_shapes=[
+        (row, row, wide, pl.BlockSpec(memory_space=pl.ANY)),
+        [
             pltpu.VMEM((rows, hid), BF16),
             pltpu.VMEM((rows, hid), BF16),
             pltpu.VMEM((rows, width), BF16),
@@ -667,9 +659,8 @@
             pltpu.VMEM(stage_rest, BF16),
             pltpu.SemaphoreType.DMA((2 * parts + 1,)),
         ],
-        compiler_params=pltpu.CompilerParams(vmem_limit_bytes=VMEM_LIMIT),
-        cost_estimate=estimate(2 * rows * width * (3 * width + 6 * hid)),
-    )(attended, inverse, x, cot, wo, wu, wd, gain)
+        2 * rows * width * (3 * width + 6 * hid),
+    )
 
 
 def kernel_call(kernel, room, grid, numbers, operands, in_specs, outs, out_specs, scratch, flops, aliases=None):
@@ -691,7 +682,7 @@
     kept, sums = (tiles, tiles, 1, tile), (tiles, 1, tile)
     groups = -(-layout.size("all_i") // UNROLL) * UNROLL
     return kernel_call(
-        functools.partial(sums_kernel, layout), 12, (1,), numbers, (q, k), [every, every],
+        functools.partial(sums_kernel, layout), 20, (1,), numbers, (q, k), [every, every],
         (sds(kept, F32), sds(sums, F32)), (fixed(kept), fixed(sums)),
         [pltpu.VMEM((groups, 1, tile), F32)], tiles * tiles * tile * tile * PAIR,
     )
@@ -758,17 +749,32 @@
     )
 
 
-def unproject(layout, numbers, base, count, dq, dk, dv, normed, weight, gain, dtype):
-    tile, width = layout.tile, dq.shape[2]
+def tile_specs(layout, base, width):
+    tile = layout.tile
     row = pl.BlockSpec((1, tile, width), lambda s, x: (s, 0, 0))
     placed = pl.BlockSpec((1, tile, width), lambda s, x: (base + s, 0, 0))
     picked = pl.BlockSpec((1, tile, width), lambda s, x: (jnp.maximum(layout.get(x, "slot_loc", base + s), 0), 0, 0))
+    return row, placed, picked
+
+
+def run_away(layout, numbers, dq, dk, dv, weight):
+    width, count, base = dq.shape[2], layout.tiles - layout.owned, layout.owned
+    row, placed, picked = tile_specs(layout, base, width)
     return kernel_call(
-        functools.partial(unproject_kernel, layout, base), 20, (count,), numbers,
-        (dq, dk, dv, normed, weight, gain),
-        [picked, placed, placed, placed, held(weight.shape), held(gain.shape)],
-        (sds((count, tile, width), dtype), sds((1, width), F32)), (row, fixed((1, width))),
-        [], 2 * count * tile * width * weight.shape[1],
+        functools.partial(away_kernel, layout, base), 20, (count,), numbers, (dq, dk, dv, weight),
+        [picked, placed, placed, held(weight.shape)], sds((count, layout.tile, width), BF16), row,
+        [], 2 * count * layout.tile * width * weight.shape[1],
+    )
+
+
+def run_home(layout, numbers, dq, dk, dv, weight, back, x, branch, gain):
+    width = dq.shape[2]
+    row, placed, picked = tile_specs(layout, 0, width)
+    return kernel_call(
+        functools.partial(home_kernel, layout), 56, (layout.owned,), numbers,
+        (dq, dk, dv, weight, back, x, branch, gain),
+        [picked, placed, placed, held(weight.shape), row, row, row, held(gain.shape)],
+        sds(x.shape, BF16), row, [], 2 * x.shape[0] * layout.tile * width * weight.shape[1],
     )
 
 
@@ -796,20 +802,6 @@
     )(numbers, normed, dq, dk)
 
 
-def finish_input(part, back, x, branch, gain):
-    owned, tile, width = x.shape
-    row = pl.BlockSpec((1, tile, width), lambda s: (s, 0, 0))
-    return pl.pallas_call(
-        input_kernel,
-        grid=(owned,),
-        out_shape=sds(x.shape, BF16),
-        in_specs=[row, row, row, row, held(gain.shape)],
-        out_specs=row,
-        compiler_params=pltpu.CompilerParams(vmem_limit_bytes=16 * 2**20),
-        cost_estimate=estimate(2 * owned * tile * width * 600),
-    )(part, back, x, branch, gain)
-
-
 def swap_seq(array):
     return lax.ppermute(array, "seq", [(0, 1), (1, 0)])
 
@@ -820,17 +812,6 @@
 
 def is_power(size):
     return size & (size - 1) == 0
-
-
-def sum_everywhere(values):
-    for axis in ("seq", "dp"):
-        size = lax.axis_size(axis)
-        if not is_power(size):
-            values = lax.psum(values, axis)
-            continue
-        for bit in powers(size):
-            values = values + lax.ppermute(values, axis, [(i, i ^ bit) for i in range(size)])
-    return values
 
 
 def scatter_halving(grad, order):
@@ -871,7 +852,7 @@
     layout = Layout(rows, lengths.shape[1], tile, owned, blocks)
     count = layout.count
     numbers = layout.chosen(lengths[0], me)
-    given, taken = layout.part(numbers, "given"), layout.part(numbers, "taken")
+    given = layout.part(numbers, "given")
 
     def put(array, pieces):
         for n in range(count):
@@ -893,10 +874,7 @@
     cot_tiles, x_others = lax.optimization_barrier((cot_own.reshape(by_tile), x_others))
     cot = swap_tiles(cot_tiles).reshape(block_len, width)
     parts = project(x_own, qkv_weight, attn_gain, tiles, 0, ())
-    q_all, k_all, v_all, normed_all = project(x_others, qkv_weight, attn_gain, tiles, owned, parts)
-    x = x_own
-    if count:
-        x = put(x_own, [lax.dynamic_index_in_dim(x_others, taken[n], 0, False) for n in range(count)])
+    q_all, k_all, v_all, normed_all, x_all = project(x_others, qkv_weight, attn_gain, tiles, owned, parts)
 
     kept, sums = run_sums(layout, numbers, q_all, k_all)
     attended, inverse = run_forward(layout, numbers, q_all, k_all, v_all, kept)
@@ -907,11 +885,23 @@
     start = jnp.max(jnp.where(passed, ends[None, :], 0), axis=1)
     end = jnp.min(jnp.where(passed, rows, ends[None, :]), axis=1)
     over = jnp.maximum(4.0 / (end - start).astype(F32) * sums.reshape(rows) - limit, 0.0)
-    excess_part = jnp.sum(jnp.where(positions // block_len == me, over, 0.0))
-
-    out_c, branch_c, dx, mlp_gain_grad, early_grads = middle(
-        attended, inverse, x, cot, out_weight, up_weight, down_weight, mlp_gain, dp_count
-    )
+    excess = jnp.full((1, 128), jnp.sum(jnp.where(positions // block_len == me, over, 0.0)))
+    hops = [("dp", bit) for bit in powers(dp_count)] + [("seq", bit) for bit in powers(blocks)]
+    if not (is_power(dp_count) and is_power(blocks)):
+        excess, hops = lax.psum(excess, ("seq", "dp")), []
+
+    def hop_beside(excess, result):
+        if hops:
+            axis, bit = hops.pop(0)
+            excess += lax.ppermute(excess, axis, [(i, i ^ bit) for i in range(lax.axis_size(axis))])
+        return lax.optimization_barrier((excess, result))
+
+    excess, attended = hop_beside(excess, attended)
+
+    out_c, branch_c, dx, early_grads = middle(
+        layout, numbers, attended, inverse, x_all, cot, out_weight, up_weight, down_weight, mlp_gain, dp_count
+    )
+    excess, dx = hop_beside(excess, dx)
     output = swap_tiles(out_c)
     branch = swap_tiles(branch_c)
     parts_hid = hid // width
@@ -922,18 +912,16 @@
     early = lax.psum_scatter(early_grads, "dp", scatter_dimension=0, tiled=False)
 
     dq, dk, dv, totals = run_backward(layout, numbers, q_all, k_all, v_all, dx, kept)
-    dk, dv, output, branch = lax.optimization_barrier((dk, dv, output, branch))
+    excess, (dk, dv, output, branch) = hop_beside(excess, (dk, dv, output, branch))
     if blocks == 2:
         far_totals = swap_seq(totals)
     else:
         far_totals = lax.all_gather(totals, "seq", axis=0, tiled=True)
     value_grad = value_weight_grad(normed_all, dk, dv)
+    excess, far_totals = hop_beside(excess, far_totals)
     dq, dk = run_late(layout, numbers, q_all, k_all, far_totals, dq, dk)
 
-    def back_through(base, number, dtype):
-        return unproject(layout, numbers, base, number, dq, dk, dv, normed_all, qkv_weight, attn_gain, dtype)
-
-    away, gain_away = back_through(owned, tiles - owned, BF16)
+    away = run_away(layout, numbers, dq, dk, dv, qkv_weight)
     if blocks == 2:
         back = swap_seq(away)
     else:
@@ -941,12 +929,8 @@
         back = lax.psum_scatter(jnp.roll(by_block, me, axis=0), "seq", scatter_dimension=0, tiled=False)
         back = back.reshape(by_tile)
     away, dq, dk = lax.optimization_barrier((away, dq, dk))
+    excess, dq = hop_beside(excess, dq)
     query_grad = query_weight_grad(layout, numbers, normed_all, dq, dk)
-    d_part, gain_home = back_through(0, owned, F32)
-    gains = sum_everywhere(
-        jnp.concatenate([gain_away + gain_home, mlp_gain_grad, jnp.full((1, 128), excess_part)], axis=1)
-    )
-
     def over_seq(piece):
         if blocks == 2:
             return piece.astype(F32) + swap_seq(piece).astype(F32)
@@ -962,7 +946,7 @@
     back, late, early = lax.optimization_barrier((back, late, early))
     qkv_piece = over_seq(late)
     early = over_seq(early)
-    input_grad = finish_input(d_part, back, x_own, branch, attn_gain)
+    input_grad = run_home(layout, numbers, dq, dk, dv, qkv_weight, back, x_own, branch, attn_gain)
 
     part = width // dp_count
     n_down = hid // dp_count
@@ -970,9 +954,16 @@
     up_piece = early[n_down : 2 * n_down].reshape(hid // width, part, width).transpose(1, 0, 2).reshape(part, hid)
     out_piece = early[2 * n_down :]
     at = lax.axis_index("dp") * part
-    attn_piece = lax.dynamic_slice_in_dim(gains[0], at, part)
-    mlp_piece = lax.dynamic_slice_in_dim(gains[0], width + at, part)
-    excess = (gains[0, 2 * width : 2 * width + 1] / (dp_count * rows)).reshape(1)
+
+    def gain_grad(weight, weight_grad, gain):
+        mine = lax.dynamic_slice_in_dim(weight, at, part).astype(F32)
+        return jnp.sum(mine * weight_grad, axis=1) / lax.dynamic_slice_in_dim(gain[0], at, part)
+
+    attn_piece = gain_grad(qkv_weight, qkv_piece, attn_gain)
+    mlp_piece = gain_grad(up_weight, up_piece, mlp_gain)
+    while hops:
+        excess, _ = hop_beside(excess, excess)
+    excess = excess[0, :1] / (dp_count * rows)
     return (
         output.reshape(1, block_len, width),
         input_grad.reshape(1, block_len, width),

time: 381 us -> 367 us (0.963)
  local copies, waits for them, and re-layouts: 54.8 us -> 38.5 us
  starting transfers between devices: 24.6 us -> 29.7 us
  between operations: 26.5 us -> 22.1 us
    pallas_call x2 -> x0, Pallas kernels: 66.5 us -> none  [the longest x1 60.7 us: middle(): pl.pallas_call(functools.partial(middle_kernel, tile, owned, width), grid...]
    pallas_call x6 -> x7, Pallas kernels: 105 us -> 169 us  [kernel_call(): pl.pallas_call(kernel, grid_spec=pltpu.PrefetchScalarGridSpec(num_scalar_...]
    ppermute x8, waiting for transfers between devices: 23.2 us -> 34.7 us  [scatter_halving(): got = lax.ppermute(send, 'dp', [(i, i ^ 1 << n) for i in range(count)])]
    ppermute x5, waiting for transfers between devices: 12.1 us -> 3.53 us  [hop_beside(): lax.ppermute(excess, axis, [(i, i ^ bit) for i in range(lax.axis_size(axi...]
    unnamed x62 -> x65, local copies, waits for them, and re-layouts: 30.6 us -> 22.4 us
    ppermute x8, starting transfers between devices: 6.6 us -> 12.6 us  [scatter_halving(): got = lax.ppermute(send, 'dp', [(i, i ^ 1 << n) for i in range(count)])]
    dynamic_update_slice x8 -> x6, local copies, waits for them, and re-layouts: 8.27 us -> 3.25 us  [put(): array = lax.dynamic_update_slice_in_dim(array, pieces[n][None], given[n], 0)]
  transfers between devices with their start and end apart: 22 -> 22, of which waited for: 13 -> 7; matrix products, arithmetic and copies ran while one was open for 8% -> 5% of each run, Pallas kernels for 36% -> 37%
where the time goes in v3:
time: 367 us; the launch traced here: 361 us
  Pallas kernels  193 us (53%)
  waiting for transfers between devices  67.4 us (18%)
  local copies, waits for them, and re-layouts  38.5 us (10%)
  starting transfers between devices  29.7 us (8%)
  between operations  22.1 us (6%)
  other arithmetic  10.4 us (3%)
    pallas_call x7, Pallas kernels, kernel_call(): pl.pallas_call(kernel, grid_spec=pltpu.PrefetchScalarGridSpec(num_scalar_...  169 us
    ppermute x8, waiting for transfers between devices, scatter_halving(): got = lax.ppermute(send, 'dp', [(i, i ^ 1 << n) for i in range(count)])  34.7 us
    ppermute x8, waiting for transfers between devices, swap_seq(): return lax.ppermute(array, 'seq', [(0, 1), (1, 0)])  29.1 us
    unnamed x65, local copies, waits for them, and re-layouts  22.4 us
    pallas_call x2, Pallas kernels, project(): pl.pallas_call(project_kernel, grid=(owned,), out_shape=outs, in_specs=[r...  14.3 us
    ppermute x8, starting transfers between devices, swap_seq(): return lax.ppermute(array, 'seq', [(0, 1), (1, 0)])  14.2 us
    ppermute x8, starting transfers between devices, scatter_halving(): got = lax.ppermute(send, 'dp', [(i, i ^ 1 << n) for i in range(count)])  12.6 us
  transfers between devices with their start and end apart: 22, of which 7 were waited for; matrix products, arithmetic and copies ran while one was open for 5% of the time, Pallas kernels for 37%

profile of v3, /device:TPU:0, one launch (start us, length us, event | category | flops | bytes accessed | tf_op | source)
XLA Modules:
  0.0 361.3 jit_solution(17389038074734118531)
XLA Ops:
  7.3 3.1 copy.65
  10.3 3.0 collective-permute-start
  15.2 1.4 fusion.11
  20.8 1.3 reshape.182.gain_ref
  24.1 1.5 copy-done.15
  25.7 6.6 %shard_map.178 = (bf16[10,256,768]{2,1,0:T(8,128)(2,1)S(1)}, bf16[10,256,768]{2,1,0:T(8,128)(2,1)S(1)}, bf16[10,256,768]{2,1,0:T(8,128)(2,1)S(1)}, bf16[10,256,7...) custom-call(bf16[5,256,768]{2,1,0:T(8,128)(2,1)S(1)} %bitcast.72, bf16[768,2304]{1,0:T(8,128)(2,1)S(1)} %copy-done.9, ...), custom_call_target="tpu_custom_call" | custom-call | flops 4529848320 | bytes 7549747 | tf_op jit(solution)/shard_map/pallas_call | solution.py:607
  32.3 24.1 %collective-permute-done = bf16[1280,768]{1,0:T(8,128)(2,1)} collective-permute-done((bf16[1280,768]{1,0:T(8,128)(2,1)}, bf16[1280,768]{1,0:T(8,128)(2,1)}, u32[]{:S(2)}, u32[]{:S(2)}) %collective-permute-start) | collective-permute-done | bytes 1966112 | tf_op jit(solution)/shard_map/ppermute | solution.py:806
  56.5 1.2 constant_dynamic-slice_fusion.9
  57.7 1.8 collective-permute-start.3
  59.5 7.7 %shard_map.179 = (bf16[10,256,768]{2,1,0:T(8,128)(2,1)S(1)}, bf16[10,256,768]{2,1,0:T(8,128)(2,1)S(1)}, bf16[10,256,768]{2,1,0:T(8,128)(2,1)S(1)}, bf16[10,256,7...) custom-call(bf16[5,256,768]{2,1,0:T(8,128)(2,1)} %bitcast.5.x_ref, ...), custom_call_target="tpu_custom_call", output_to_operand_aliasing={{0}: (3, {}), {1}: (4, {}), {2}: (5, {}), {3}: (6, {}), {4}... | custom-call | flops 4529848320 | bytes 7549747 | tf_op jit(solution)/shard_map/pallas_call | solution.py:607
  67.2 1.9 copy-done.7
  69.1 2.0 copy-done.13
  71.1 4.6 %shard_map.180 = (f32[10,10,1,256]{3,2,1,0:T(1,128)S(1)}, f32[10,1,256]{2,1,0:T(1,128)S(1)}) custom-call(s32[320]{0:T(512)S(1)} %fusion.9.numbers, bf16[10,256,768]{2,1,0:T(8,128)(2,1)S(1)} %get-tuple-element.59.q_ref, bf16[10,256,768]{2,1,0:T(8,128)(2,1)S(1)} %get-tuple-element.60.k_ref), custom_call_target="tpu_custom_call" | custom-call | flops 838860800 | bytes 1398101 | tf_op jit(solution)/shard_map/pallas_call | solution.py:667
  77.1 28.8 %shard_map.181 = (f32[5,256,768]{2,1,0:T(8,128)S(1)}, f32[5,256,768]{2,1,0:T(8,128)S(1)}) custom-call(s32[320]{0:T(512)S(1)} %fusion.9.numbers, bf16[10,256,768]{2,1,0:T(8,128)(2,1)S(1)} %get-tuple-element.59.q_ref, bf16[10,256,768]{2,1,0:T(8,128)(2,1)S(1)} %get-tuple-element.60.k_ref, bf16[10,256,768]{2,1,0:T(8,128)(2,1)S(1)} %get-tuple-element.62.v_ref, ...), custom_call_target="tpu_custom_call" | custom-call | flops 4026531840 | bytes 6710886 | tf_op jit(solution)/shard_map/pallas_call | solution.py:667
  105.9 1.9 copy-done.11
  107.8 2.0 copy-done.21
  109.8 1.9 copy-done.22
  113.9 60.7 %shard_map.182 = (bf16[5,256,768]{2,1,0:T(8,128)(2,1)}, bf16[5,256,768]{2,1,0:T(8,128)(2,1)}, bf16[5,256,1536]{2,1,0:T(8,128)(2,1)}, bf16[16,432,768]{2,1,0:T(8,128)(2,1)}) custom-call(s32[320]{0:T(512)} %copy-done.16, f32[5,256,768]{2,1,0:T(8,128)} %copy-done.21, f32[5,256,768]{2,1,0:T(8,128)} %copy-done.22, bf16[10,256,768]{2,1,0:T(8,128)(2,1)} %copy-done.13, ...), custom_call_target="tpu_custom_call" | custom-call | flops 40768634880 | bytes 67947728 | tf_op jit(solution)/shard_map/pallas_call | solution.py:667
  174.7 3.5 collective-permute-done.2
  178.3 1.6 collective-permute-start.4
  179.8 1.4 constant_dynamic-slice_fusion.5
  181.3 1.9 collective-permute-start.5
  183.5 2.6 copy-done.3
  186.2 2.6 copy-done.12
  188.8 2.6 copy-done.23
  191.4 53.3 %shard_map.183 = (bf16[5,256,768]{2,1,0:T(8,128)(2,1)S(1)}, bf16[10,256,768]{2,1,0:T(8,128)(2,1)S(1)}, bf16[10,256,768]{2,1,0:T(8,128)(2,1)S(1)}, f32[5,10,1,256]{3,2,1,0:T(1,128)S(1)}) custom-call(s32[320]{0:T(512)S(1)} %copy-done.17, bf16[10,256,768]{2,1,0:T(8,128)(2,1)S(1)} %copy-done.1, bf16[10,256,768]{2,1,0:T(8,128)(2,1)S(1)} %copy-done.3, ...), custom_call_target="tpu_custom_call" | custom-call | flops 12079595520 | bytes 20132660 | tf_op jit(solution)/shard_map/pallas_call | solution.py:667
  244.7 4.4 %collective-permute-start.8 = (f32[5,10,1,256]{3,2,1,0:T(1,128)S(1)}, f32[5,10,1,256]{3,2,1,0:T(1,128)S(1)}, u32[]{:S(2)}, u32[]{:S(2)}) collective-permute-start(f32[5,10,1,256]{3,2,1,0:T(1,128)S(1)} %get-tuple-element.79), channel_id=1, source_target_pairs={{0,16},{16,0},{1,17},{17,1},{2,18},{18,2},{3,19},{19,3},{4,20},{20... | collective-permute-start | bytes 153608 | tf_op jit(solution)/shard_map/ppermute | solution.py:806
  250.8 5.3 %shard_map.187 = bf16[768,1152]{1,0:T(8,128)(2,1)S(1)} custom-call(bf16[10,256,768]{2,1,0:T(8,128)(2,1)S(1)} %copy-done.8, bf16[10,256,768]{2,1,0:T(8,128)(2,1)S(1)} %get-tuple-element.83.dk_in_ref.dk_ref, bf16[10,256,768]{2,1,0:T(8,128)(2,1)S(1)} %get-tuple-element.86.dv_ref), custom_call_target="tpu_custom_call" | custom-call | flops 4529848320 | bytes 7549747 | tf_op jit(solution)/shard_map/pallas_call | solution.py:783
  258.7 3.5 shard_map.184
  262.3 6.2 %shard_map.185 = bf16[5,256,768]{2,1,0:T(8,128)(2,1)S(1)} custom-call(s32[320]{0:T(512)S(1)} %copy-done.17, bf16[5,256,768]{2,1,0:T(8,128)(2,1)S(1)} %get-tuple-element.88.dq_ref, bf16[10,256,768]{2,1,0:T(8,128)(2,1)S(1)} %get-tuple-element.89.dk_ref, bf16[10,256,768]{2,1,0:T(8,128)(2,1)S(1)} %get-tuple-element.86.dv_ref, bf16[768,2304]{1,0:T(8,128)(2,1)S(1)} %copy-done.10), custom_call_target="tpu_custom_call" | custom-call | flops 4529848320 | bytes 7549747 | tf_op jit(solution)/shard_map/pallas_call | solution.py:667
  268.6 4.4 %shard_map.186 = bf16[768,1152]{1,0:T(8,128)(2,1)S(1)} custom-call(s32[320]{0:T(512)S(1)} %copy-done.17, bf16[10,256,768]{2,1,0:T(8,128)(2,1)S(1)} %copy-done.8, bf16[5,256,768]{2,1,0:T(8,128)(2,1)S(1)} %get-tuple-element.88.dq_ref, bf16[10,256,768]{2,1,0:T(8,128)(2,1)S(1)} %get-tuple-element.89.dk_ref), custom_call_target="tpu_custom_call" | custom-call | flops 3019898880 | bytes 5033164 | tf_op jit(solution)/shard_map/pallas_call | solution.py:795
  275.2 3.9 %collective-permute-start.11 = (bf16[2,2,2,48,1152]{4,3,0,1,2:T(8,128)(2,1)}, bf16[2,2,2,48,1152]{4,3,0,1,2:T(8,128)(2,1)}, u32[]{:S(2)}, u32[]{:S(2)}) collective-permute-start(bf16[2,2,2,48,1152]{4,3,0,1,2:T(8,128)(2,1)} %bitcast.67), channel_id=1, source_target_pairs={{0,1},{1,0},{2,3},{3,2},{4,5},{5,4},{6,7},{7,6},{8,9},{9,8},{10,11... | collective-permute-start | bytes 2654216 | tf_op jit(solution)/shard_map/ppermute | solution.py:829
  280.0 1.4 fusion
  281.4 1.4 collective-permute-start.16
  282.9 1.4 fusion.1
  284.3 2.4 collective-permute-start.12
  286.7 18.2 %collective-permute-done.16 = bf16[2,2,48,1152]{3,2,1,0:T(8,128)(2,1)S(1)} collective-permute-done((bf16[2,2,48,1152]{3,2,1,0:T(8,128)(2,1)S(1)}, bf16[2,2,48,1152]{3,2,1,0:T(8,128)(2,1)S(1)}, u32[]{:S(2)}, u32[]{:S(2)}) %collective-permute-start.16) | collective-permute-done | bytes 442400 | tf_op jit(solution)/shard_map/ppermute | solution.py:829
  305.8 2.5 collective-permute-start.13
  308.3 9.7 %collective-permute-done.17 = bf16[2,48,1152]{2,1,0:T(8,128)(2,1)S(1)} collective-permute-done((bf16[2,48,1152]{2,1,0:T(8,128)(2,1)S(1)}, bf16[2,48,1152]{2,1,0:T(8,128)(2,1)S(1)}, u32[]{:S(2)}, u32[]{:S(2)}) %collective-permute-start.17) | collective-permute-done | bytes 221216 | tf_op jit(solution)/shard_map/ppermute | solution.py:829
  318.1 1.7 collective-permute-start.18
  319.9 3.2 collective-permute-done.18
  323.2 3.6 collective-permute-done.14
  326.8 1.4 collective-permute-start.19
  328.9 12.0 %shard_map.188 = bf16[5,256,768]{2,1,0:T(8,128)(2,1)} custom-call(s32[320]{0:T(512)} %copy-done.16, bf16[5,256,768]{2,1,0:T(8,128)(2,1)} %copy-done.6, bf16[10,256,768]{2,1,0:T(8,128)(2,1)} %copy-done.5, bf16[10,256,768]{2,1,0:T(8,128)(2,1)} %copy-done.14, bf16[768,2304]{1,0:T(8,128)(2,1)} %w_ref.7, bf16[5,256,768]{2,1,0:T(8,128)(2,1)} %collective-permute-done.10.back_ref, ...), custom_call_target="tpu_custom_call" | custom-call | flops 4529848320 | bytes 7549747 | tf_op jit(solution)/shard_map/pallas_call | solution.py:667
  341.0 1.9 multiply_reduce_fusion.1
  343.5 5.0 %collective-permute-done.20 = bf16[432,768]{1,0:T(8,128)(2,1)S(1)} collective-permute-done((bf16[432,768]{1,0:T(8,128)(2,1)}, bf16[432,768]{1,0:T(8,128)(2,1)S(1)}, u32[]{:S(2)}, u32[]{:S(2)}) %collective-permute-start.20) | collective-permute-done | bytes 663584 | tf_op jit(solution)/shard_map/ppermute | solution.py:806
  350.3 1.4 multiply_reduce_fusion
  351.6 1.3 dynamic-slice_divide_fusion
  (127 shorter events, 18.1 us)
Async XLA Ops:
  7.2 6.1 %copy-start.31 = (s32[1,5]{1,0:T(1,128)S(1)}, s32[1,5]{1,0:T(1,128)}, u32[]{:S(2)}) copy-start(s32[1,5]{1,0:T(1,128)} %param.13) | copy-start | bytes 64
  7.2 12.9 %copy-start.30 = (f32[768]{0:T(1024)S(1)}, f32[768]{0:T(1024)}, u32[]{:S(2)}) copy-start(f32[768]{0:T(1024)} %param.15) | copy-start | bytes 9220
  7.2 16.9 %copy-start.9 = (bf16[768,2304]{1,0:T(8,128)(2,1)S(1)}, bf16[768,2304]{1,0:T(8,128)(2,1)}, u32[]{:S(2)}) copy-start(bf16[768,2304]{1,0:T(8,128)(2,1)} %w_ref.7) | copy-start | bytes 10616836
  7.2 319.6 %reduce-scatter.2.cloned.1.call-start = ((), (), s32[]{:S(2)}) async-start(), calls=%async_computation.1 | async-start | bytes 11280384 | tf_op jit(solution)/shard_map/reduce_scatter | solution.py:912
  10.3 46.1 %collective-permute-start = (bf16[1280,768]{1,0:T(8,128)(2,1)}, bf16[1280,768]{1,0:T(8,128)(2,1)}, u32[]{:S(2)}, u32[]{:S(2)}) collective-permute-start(bf16[1280,768]{1,0:T(8,128)(2,1)} %bitcast.70), channel_id=1, source_target_pairs={{0,16},{16,0},{1,17},{17,1},{2,18},{18,2},{3,19},{19,3},{4,20},{20... | collective-permute-start | bytes 5898248 | tf_op jit(solution)/shard_map/ppermute | solution.py:806
  20.1 39.4 %copy-start.18 = (f32[1,768]{1,0:T(1,128)}, f32[1,768]{1,0:T(1,128)S(1)}, u32[]{:S(2)}) copy-start(f32[1,768]{1,0:T(1,128)S(1)} %reshape.180.gain_ref) | copy-start | bytes 9220
  24.1 53.0 %copy-start.16 = (s32[320]{0:T(512)}, s32[320]{0:T(512)S(1)}, u32[]{:S(2)}) copy-start(s32[320]{0:T(512)S(1)} %fusion.9.numbers) | copy-start | bytes 3844
  57.7 54.7 %collective-permute-start.3 = (bf16[2,256,768]{2,1,0:T(8,128)(2,1)S(1)}, bf16[2,256,768]{2,1,0:T(8,128)(2,1)S(1)}, u32[]{:S(2)}, u32[]{:S(2)}) collective-permute-start(bf16[2,256,768]{2,1,0:T(8,128)(2,1)S(1)} %pad_maximum_fusion), channel_id=1, source_target_pairs={{0,16},{16,0},{1,17},{17,1},{2,18},{18,2},{3,19},{19,3},{4,20},{20... | collective-permute-start | bytes 2359304 | tf_op jit(solution)/shard_map/ppermute | solution.py:806
  71.1 6.0 %copy-start = (bf16[10,256,768]{2,1,0:T(8,128)(2,1)}, bf16[10,256,768]{2,1,0:T(8,128)(2,1)S(1)}, u32[]{:S(2)}) copy-start(bf16[10,256,768]{2,1,0:T(8,128)(2,1)S(1)} %get-tuple-element.59.q_ref) | copy-start | bytes 11796484
  71.1 6.0 %copy-start.2 = (bf16[10,256,768]{2,1,0:T(8,128)(2,1)}, bf16[10,256,768]{2,1,0:T(8,128)(2,1)S(1)}, u32[]{:S(2)}) copy-start(bf16[10,256,768]{2,1,0:T(8,128)(2,1)S(1)} %get-tuple-element.60.k_ref) | copy-start | bytes 11796484
  71.1 4.7 %copy-start.29 = (f32[10,1,256]{2,1,0:T(1,128)S(1)}, f32[10,1,256]{2,1,0:T(1,128)}, u32[]{:S(2)}) copy-start(f32[10,1,256]{2,1,0:T(1,128)} %div.48) | copy-start | bytes 30724
  77.0 34.7 %collective-permute-start.1 = (f32[1,128]{1,0:T(1,128)S(1)}, f32[1,128]{1,0:T(1,128)S(1)}, u32[]{:S(2)}, u32[]{:S(2)}) collective-permute-start(f32[1,128]{1,0:T(1,128)S(1)} %broadcast_in_dim.31), channel_id=1, source_target_pairs={{0,1},{1,0},{2,3},{3,2},{4,5},{5,4},{6,7},{7,6},{8,9},{9,8},{10,11... | collective-permute-start | bytes 1544 | tf_op jit(solution)/shard_map/ppermute | solution.py:896
  174.6 5.2 %copy-start.27 = (bf16[5,256,768]{2,1,0:T(8,128)(2,1)S(1)}, bf16[5,256,768]{2,1,0:T(8,128)(2,1)}, u32[]{:S(2)}) copy-start(bf16[5,256,768]{2,1,0:T(8,128)(2,1)} %get-tuple-element.75) | copy-start | bytes 5898244
  174.6 3.6 collective-permute-start.2
  178.3 70.8 %collective-permute-start.4 = (f32[1,128]{1,0:T(1,128)S(1)}, f32[1,128]{1,0:T(1,128)S(1)}, u32[]{:S(2)}, u32[]{:S(2)}) collective-permute-start(f32[1,128]{1,0:T(1,128)S(1)} %add.142), channel_id=1, source_target_pairs={{0,4},{1,5},{2,6},{3,7},{4,0},{5,1},{6,2},{7,3},{8,12},{9,13},{10,... | collective-permute-start | bytes 1544 | tf_op jit(solution)/shard_map/ppermute | solution.py:896
  179.8 3.7 %copy-start.1 = (bf16[10,256,768]{2,1,0:T(8,128)(2,1)S(1)}, bf16[10,256,768]{2,1,0:T(8,128)(2,1)}, u32[]{:S(2)}) copy-start(bf16[10,256,768]{2,1,0:T(8,128)(2,1)} %copy-done) | copy-start | bytes 11796484
  181.2 2.3 copy-start.17
  181.3 67.8 %collective-permute-start.5 = (bf16[2,256,768]{2,1,0:T(8,128)(2,1)S(1)}, bf16[2,256,768]{2,1,0:T(8,128)(2,1)S(1)}, u32[]{:S(2)}, u32[]{:S(2)}) collective-permute-start(bf16[2,256,768]{2,1,0:T(8,128)(2,1)S(1)} %pad_maximum_fusion.1), channel_id=1, source_target_pairs={{0,16},{16,0},{1,17},{17,1},{2,18},{18,2},{3,19},{19,3},{4,20},{20... | collective-permute-start | bytes 2359304 | tf_op jit(solution)/shard_map/ppermute | solution.py:806
  183.3 65.9 %collective-permute-start.6 = (bf16[2,256,768]{2,1,0:T(8,128)(2,1)S(1)}, bf16[2,256,768]{2,1,0:T(8,128)(2,1)S(1)}, u32[]{:S(2)}, u32[]{:S(2)}) collective-permute-start(bf16[2,256,768]{2,1,0:T(8,128)(2,1)S(1)} %pad_maximum_fusion.2), channel_id=1, source_target_pairs={{0,16},{16,0},{1,17},{17,1},{2,18},{18,2},{3,19},{19,3},{4,20},{20... | collective-permute-start | bytes 2359304 | tf_op jit(solution)/shard_map/ppermute | solution.py:806
  183.5 2.6 copy-start.3
  186.2 2.6 copy-start.12
  188.8 2.6 copy-start.23
  191.4 59.5 %copy-start.8 = (bf16[10,256,768]{2,1,0:T(8,128)(2,1)S(1)}, bf16[10,256,768]{2,1,0:T(8,128)(2,1)}, u32[]{:S(2)}) copy-start(bf16[10,256,768]{2,1,0:T(8,128)(2,1)} %copy-done.7) | copy-start | bytes 11796484
  244.7 17.6 %copy-start.14 = (bf16[10,256,768]{2,1,0:T(8,128)(2,1)}, bf16[10,256,768]{2,1,0:T(8,128)(2,1)S(1)}, u32[]{:S(2)}) copy-start(bf16[10,256,768]{2,1,0:T(8,128)(2,1)S(1)} %get-tuple-element.86.dv_ref) | copy-start | bytes 11796484
  244.7 12.8 %collective-permute-start.8 = (f32[5,10,1,256]{3,2,1,0:T(1,128)S(1)}, f32[5,10,1,256]{3,2,1,0:T(1,128)S(1)}, u32[]{:S(2)}, u32[]{:S(2)}) collective-permute-start(f32[5,10,1,256]{3,2,1,0:T(1,128)S(1)} %get-tuple-element.79), channel_id=1, source_target_pairs={{0,16},{16,0},{1,17},{17,1},{2,18},{18,2},{3,19},{19,3},{4,20},{20... | collective-permute-start | bytes 153608 | tf_op jit(solution)/shard_map/ppermute | solution.py:806
  249.2 7.0 %copy-start.28 = (bf16[5,256,768]{2,1,0:T(8,128)(2,1)}, bf16[5,256,768]{2,1,0:T(8,128)(2,1)S(1)}, u32[]{:S(2)}) copy-start(bf16[5,256,768]{2,1,0:T(8,128)(2,1)S(1)} %slice_dynamic-update-slice_fusion.2) | copy-start | bytes 5898244
  250.8 6.6 %collective-permute-start.7 = (f32[1,128]{1,0:T(1,128)S(1)}, f32[1,128]{1,0:T(1,128)S(1)}, u32[]{:S(2)}, u32[]{:S(2)}) collective-permute-start(f32[1,128]{1,0:T(1,128)S(1)} %add.145), channel_id=1, source_target_pairs={{0,8},{1,9},{2,10},{3,11},{4,12},{5,13},{6,14},{7,15},{8,0},{9,1},... | collective-permute-start | bytes 1544 | tf_op jit(solution)/shard_map/ppermute | solution.py:896
  256.2 2.6 copy-start.4
  257.3 22.6 %collective-permute-start.15 = (bf16[2,2,2,48,1152]{4,3,2,0,1:T(8,128)(2,1)}, bf16[2,2,2,48,1152]{4,3,2,0,1:T(8,128)(2,1)}, u32[]{:S(2)}, u32[]{:S(2)}) collective-permute-start(bf16[2,2,2,48,1152]{4,3,2,0,1:T(8,128)(2,1)} %bitcast.66), channel_id=1, source_target_pairs={{0,1},{1,0},{2,3},{3,2},{4,5},{5,4},{6,7},{7,6},{8,9},{9,8},{10,11... | collective-permute-start | bytes 2654216 | tf_op jit(solution)/shard_map/ppermute | solution.py:829
  257.5 11.1 %collective-permute-start.9 = (f32[1,128]{1,0:T(1,128)S(1)}, f32[1,128]{1,0:T(1,128)S(1)}, u32[]{:S(2)}, u32[]{:S(2)}) collective-permute-start(f32[1,128]{1,0:T(1,128)S(1)} %add.146), channel_id=1, source_target_pairs={{0,16},{16,0},{1,17},{17,1},{2,18},{18,2},{3,19},{19,3},{4,20},{20... | collective-permute-start | bytes 1544 | tf_op jit(solution)/shard_map/ppermute | solution.py:896
  258.7 3.6 copy-start.10
  262.3 6.3 %copy-start.5 = (bf16[10,256,768]{2,1,0:T(8,128)(2,1)}, bf16[10,256,768]{2,1,0:T(8,128)(2,1)S(1)}, u32[]{:S(2)}) copy-start(bf16[10,256,768]{2,1,0:T(8,128)(2,1)S(1)} %get-tuple-element.89.dk_ref) | copy-start | bytes 11796484
  262.3 6.3 %copy-start.6 = (bf16[5,256,768]{2,1,0:T(8,128)(2,1)}, bf16[5,256,768]{2,1,0:T(8,128)(2,1)S(1)}, u32[]{:S(2)}) copy-start(bf16[5,256,768]{2,1,0:T(8,128)(2,1)S(1)} %get-tuple-element.88.dq_ref) | copy-start | bytes 5898244
  268.5 4.5 %copy-start.19 = (bf16[5,256,768]{2,1,0:T(8,128)(2,1)}, bf16[5,256,768]{2,1,0:T(8,128)(2,1)S(1)}, u32[]{:S(2)}) copy-start(bf16[5,256,768]{2,1,0:T(8,128)(2,1)S(1)} %shard_map.185) | copy-start | bytes 5898244
  273.0 6.1 %copy-start.20 = (bf16[5,256,768]{2,1,0:T(8,128)(2,1)S(1)}, bf16[5,256,768]{2,1,0:T(8,128)(2,1)}, u32[]{:S(2)}) copy-start(bf16[5,256,768]{2,1,0:T(8,128)(2,1)} %copy-done.19) | copy-start | bytes 5898244
  275.2 7.7 %collective-permute-start.11 = (bf16[2,2,2,48,1152]{4,3,0,1,2:T(8,128)(2,1)}, bf16[2,2,2,48,1152]{4,3,0,1,2:T(8,128)(2,1)}, u32[]{:S(2)}, u32[]{:S(2)}) collective-permute-start(bf16[2,2,2,48,1152]{4,3,0,1,2:T(8,128)(2,1)} %bitcast.67), channel_id=1, source_target_pairs={{0,1},{1,0},{2,3},{3,2},{4,5},{5,4},{6,7},{7,6},{8,9},{9,8},{10,11... | collective-permute-start | bytes 2654216 | tf_op jit(solution)/shard_map/ppermute | solution.py:829
  279.1 3.8 %copy-start.24 = (bf16[2,2,2,1,48,1152]{5,4,3,2,1,0:T(8,128)(2,1)S(1)}, bf16[2,2,2,1,48,1152]{5,4,3,2,1,0:T(8,128)(2,1)}, u32[]{:S(2)}) copy-start(bf16[2,2,2,1,48,1152]{5,4,3,2,1,0:T(8,128)(2,1)} %get-tuple-element.107) | copy-start | bytes 2654212
  279.1 47.7 %collective-permute-start.10 = (bf16[5,256,768]{2,1,0:T(8,128)(2,1)S(1)}, bf16[5,256,768]{2,1,0:T(8,128)(2,1)}, u32[]{:S(2)}, u32[]{:S(2)}) collective-permute-start(bf16[5,256,768]{2,1,0:T(8,128)(2,1)S(1)} %copy-done.20), channel_id=1, source_target_pairs={{0,16},{16,0},{1,17},{17,1},{2,18},{18,2},{3,19},{19,3},{4,20},{20... | collective-permute-start | bytes 5898248 | tf_op jit(solution)/shard_map/ppermute | solution.py:806
  281.4 23.4 %collective-permute-start.16 = (bf16[2,2,48,1152]{3,2,1,0:T(8,128)(2,1)S(1)}, bf16[2,2,48,1152]{3,2,1,0:T(8,128)(2,1)S(1)}, u32[]{:S(2)}, u32[]{:S(2)}) collective-permute-start(bf16[2,2,48,1152]{3,2,1,0:T(8,128)(2,1)S(1)} %dynamic-slice_bitcast_fusion), channel_id=1, source_target_pairs={{0,4},{1,5},{2,6},{3,7},{4,0},{5,1},{6,2},{7,3},{8,12},{9,13},{10,... | collective-permute-start | bytes 1327112 | tf_op jit(solution)/shard_map/ppermute | solution.py:829
  284.3 21.3 %collective-permute-start.12 = (bf16[2,2,48,1152]{3,2,0,1:T(8,128)(2,1)S(1)}, bf16[2,2,48,1152]{3,2,0,1:T(8,128)(2,1)S(1)}, u32[]{:S(2)}, u32[]{:S(2)}) collective-permute-start(bf16[2,2,48,1152]{3,2,0,1:T(8,128)(2,1)S(1)} %dynamic-slice_bitcast_fusion.1), channel_id=1, source_target_pairs={{0,2},{1,3},{2,0},{3,1},{4,6},{5,7},{6,4},{7,5},{8,10},{9,11},{10,... | collective-permute-start | bytes 1327112 | tf_op jit(solution)/shard_map/ppermute | solution.py:829
  305.0 13.0 %collective-permute-start.17 = (bf16[2,48,1152]{2,1,0:T(8,128)(2,1)S(1)}, bf16[2,48,1152]{2,1,0:T(8,128)(2,1)S(1)}, u32[]{:S(2)}, u32[]{:S(2)}) collective-permute-start(bf16[2,48,1152]{2,1,0:T(8,128)(2,1)S(1)} %dynamic-slice_bitcast_fusion.2), channel_id=1, source_target_pairs={{0,8},{1,9},{2,10},{3,11},{4,12},{5,13},{6,14},{7,15},{8,0},{9,1},... | collective-permute-start | bytes 663560 | tf_op jit(solution)/shard_map/ppermute | solution.py:829
  305.8 14.0 %collective-permute-start.13 = (bf16[2,48,1152]{2,1,0:T(8,128)(2,1)S(1)}, bf16[2,48,1152]{2,1,0:T(8,128)(2,1)S(1)}, u32[]{:S(2)}, u32[]{:S(2)}) collective-permute-start(bf16[2,48,1152]{2,1,0:T(8,128)(2,1)S(1)} %dynamic-slice_bitcast_fusion.3), channel_id=1, source_target_pairs={{0,4},{1,5},{2,6},{3,7},{4,0},{5,1},{6,2},{7,3},{8,12},{9,13},{10,... | collective-permute-start | bytes 663560 | tf_op jit(solution)/shard_map/ppermute | solution.py:829
  318.1 5.0 %collective-permute-start.18 = (bf16[48,1152]{1,0:T(8,128)(2,1)S(1)}, bf16[48,1152]{1,0:T(8,128)(2,1)S(1)}, u32[]{:S(2)}, u32[]{:S(2)}) collective-permute-start(bf16[48,1152]{1,0:T(8,128)(2,1)S(1)} %dynamic-slice_bitcast_fusion.4), channel_id=1, source_target_pairs={{0,2},{1,3},{2,0},{3,1},{4,6},{5,7},{6,4},{7,5},{8,10},{9,11},{10,... | collective-permute-start | bytes 331784 | tf_op jit(solution)/shard_map/ppermute | solution.py:829
  319.9 6.9 %collective-permute-start.14 = (bf16[48,1152]{1,0:T(8,128)(2,1)S(1)}, bf16[48,1152]{1,0:T(8,128)(2,1)S(1)}, u32[]{:S(2)}, u32[]{:S(2)}) collective-permute-start(bf16[48,1152]{1,0:T(8,128)(2,1)S(1)} %dynamic-slice_bitcast_fusion.5), channel_id=1, source_target_pairs={{0,8},{1,9},{2,10},{3,11},{4,12},{5,13},{6,14},{7,15},{8,0},{9,1},... | collective-permute-start | bytes 331784 | tf_op jit(solution)/shard_map/ppermute | solution.py:829
  326.8 21.6 %copy-start.26 = (bf16[1,432,768]{2,1,0:T(8,128)(2,1)S(1)}, bf16[1,432,768]{2,1,0:T(8,128)(2,1)}, u32[]{:S(2)}) copy-start(bf16[1,432,768]{2,1,0:T(8,128)(2,1)} %reduce-scatter.2.cloned.1.call-done) | copy-start | bytes 1990660
  326.8 14.1 %collective-permute-start.19 = (bf16[48,2304]{1,0:T(8,128)(2,1)S(1)}, bf16[48,2304]{1,0:T(8,128)(2,1)S(1)}, u32[]{:S(2)}, u32[]{:S(2)}) collective-permute-start(bf16[48,2304]{1,0:T(8,128)(2,1)S(1)} %pad_maximum_fusion.3), channel_id=1, source_target_pairs={{0,16},{16,0},{1,17},{17,1},{2,18},{18,2},{3,19},{19,3},{4,20},{20... | collective-permute-start | bytes 663560 | tf_op jit(solution)/shard_map/ppermute | solution.py:806
  328.3 20.2 %collective-permute-start.20 = (bf16[432,768]{1,0:T(8,128)(2,1)}, bf16[432,768]{1,0:T(8,128)(2,1)S(1)}, u32[]{:S(2)}, u32[]{:S(2)}) collective-permute-start(bf16[432,768]{1,0:T(8,128)(2,1)} %bitcast.78), channel_id=1, source_target_pairs={{0,16},{16,0},{1,17},{17,1},{2,18},{18,2},{3,19},{19,3},{4,20},{20... | collective-permute-start | bytes 1990664 | tf_op jit(solution)/shard_map/ppermute | solution.py:806
  350.3 2.7 copy-start.25
  (6 other events, 11.2 us)
Sparse Core Ops, SparseCore 0:
  174.8 129.1 reduce-scatter.1

commit v4 on v3

--- a/solution.py
+++ b/solution.py
@@ -594,13 +594,21 @@
     return pl.BlockSpec(shape, lambda *_: (0,) * len(shape))
 
 
+def in_hbm(shape, dtype):
+    return pltpu.HBM(shape, dtype)
+
+
+def stay(*arrays):
+    return tuple(pltpu.with_memory_space_constraint(a, pltpu.HBM) for a in arrays)
+
+
 def sds(shape, dtype):
     return jax.ShapeDtypeStruct(shape, dtype)
 
 
 def project(x, weight, gain, tiles, first, into):
     owned, tile, width = x.shape
-    outs = (sds((tiles, tile, width), BF16),) * 5
+    outs = (sds((tiles, tile, width), BF16),) * 2 + (in_hbm((tiles, tile, width), BF16),) * 3
     row = pl.BlockSpec((1, tile, width), lambda s: (s, 0, 0))
     placed = pl.BlockSpec((1, tile, width), lambda s: (s + first, 0, 0))
     extra = [pl.BlockSpec(memory_space=pl.ANY)] * len(into)
@@ -697,7 +705,7 @@
     return kernel_call(
         functools.partial(forward_kernel, layout), 20, (layout.size("fwd_i"),), numbers,
         (q, k, v, kept), [rows, keys, keys, fixed(kept.shape)],
-        (sds((owned, tile, width), F32),) * 2, (slots, slots),
+        (in_hbm((owned, tile, width), F32),) * 2, (slots, slots),
         [pltpu.VMEM((HEADS, tile, PAIR), F32), pltpu.VMEM((tile, tile), F32)],
         4 * layout.size("fwd_i") * tile * tile * width,
     )
@@ -714,7 +722,7 @@
     totals = (owned, tiles, 1, tile)
     return kernel_call(
         functools.partial(backward_kernel, layout), 28, (layout.size("bwd_i"),), numbers,
-        (q, k, v, dx, kept), [rows, keys, keys, slots, fixed(kept.shape)],
+        (*stay(q, k, v), dx, kept), [rows, keys, keys, slots, fixed(kept.shape)],
         (
             sds((owned, tile, width), BF16),
             sds((tiles, tile, width), BF16),
@@ -943,7 +951,7 @@
     else:
         halves = [lax.psum_scatter(grad, "dp", scatter_dimension=0, tiled=False) for grad in halves]
     late = jnp.concatenate(halves, axis=1)
-    back, late, early = lax.optimization_barrier((back, late, early))
+    _, late, early = lax.optimization_barrier((back, late, early))
     qkv_piece = over_seq(late)
     early = over_seq(early)
     input_grad = run_home(layout, numbers, dq, dk, dv, qkv_weight, back, x_own, branch, attn_gain)

time: 367 us -> 359 us (0.978)
  local copies, waits for them, and re-layouts: 38.5 us -> 21.4 us
  Pallas kernels: 193 us -> 203 us
  waiting for transfers between devices: 67.4 us -> 72.3 us
  starting transfers between devices: 29.7 us -> 25.1 us
    unnamed x65 -> x53, local copies, waits for them, and re-layouts: 22.4 us -> 5.26 us
    pallas_call x7, Pallas kernels: 169 us -> 177 us  [kernel_call(): pl.pallas_call(kernel, grid_spec=pltpu.PrefetchScalarGridSpec(num_scalar_...]
    ppermute x8, waiting for transfers between devices: 34.7 us -> 40.3 us  [scatter_halving(): got = lax.ppermute(send, 'dp', [(i, i ^ 1 << n) for i in range(count)])]
    ppermute x8, starting transfers between devices: 12.6 us -> 7.85 us  [scatter_halving(): got = lax.ppermute(send, 'dp', [(i, i ^ 1 << n) for i in range(count)])]
  transfers between devices with their start and end apart: 22 -> 22, of which waited for: 7 -> 8; matrix products, arithmetic and copies ran while one was open for 5% -> 5% of each run, Pallas kernels for 37% -> 40%
where the time goes in v4:
time: 359 us; the launch traced here: 354 us
  Pallas kernels  203 us (57%)
  waiting for transfers between devices  72.3 us (20%)
  starting transfers between devices  25.1 us (7%)
  between operations  22.1 us (6%)
  local copies, waits for them, and re-layouts  21.4 us (6%)
  other arithmetic  10.5 us (3%)
    pallas_call x7, Pallas kernels, kernel_call(): pl.pallas_call(kernel, grid_spec=pltpu.PrefetchScalarGridSpec(num_scalar_...  177 us
    ppermute x8, waiting for transfers between devices, scatter_halving(): got = lax.ppermute(send, 'dp', [(i, i ^ 1 << n) for i in range(count)])  40.3 us
    ppermute x8, waiting for transfers between devices, swap_seq(): return lax.ppermute(array, 'seq', [(0, 1), (1, 0)])  28.4 us
    pallas_call x2, Pallas kernels, project(): pl.pallas_call(project_kernel, grid=(owned,), out_shape=outs, in_specs=[r...  15.8 us
    ppermute x8, starting transfers between devices, swap_seq(): return lax.ppermute(array, 'seq', [(0, 1), (1, 0)])  12.6 us
    ppermute x8, starting transfers between devices, scatter_halving(): got = lax.ppermute(send, 'dp', [(i, i ^ 1 << n) for i in range(count)])  7.85 us
  transfers between devices with their start and end apart: 22, of which 8 were waited for; matrix products, arithmetic and copies ran while one was open for 5% of the time, Pallas kernels for 40%

profile of v4, /device:TPU:0, one launch (start us, length us, event | category | flops | bytes accessed | tf_op | source)
XLA Modules:
  0.0 354.1 jit_solution(11523136838882162347)
XLA Ops:
  7.3 3.1 copy.65
  10.3 3.0 collective-permute-start
  15.2 1.4 fusion.11
  20.8 1.3 reshape.182.gain_ref
  24.1 1.5 copy-done.11
  25.7 7.4 %shard_map.178 = (bf16[10,256,768]{2,1,0:T(8,128)(2,1)S(1)}, bf16[10,256,768]{2,1,0:T(8,128)(2,1)S(1)}, bf16[10,256,768]{2,1,0:T(8,128)(2,1)}, bf16[10,256,768]{2,1,0:T(8,128)(2,1)}, bf16[10,256,768]{2,1,0:T(8,128)(2,1)}) custom-call(bf16[5,256,768]{2,1,0:T(8,128)(2,1)S(1)} %bitcast.72, bf16[768,2304]{1,0:T(8,128)(2,1)S(1)} %copy-done.7, ...), custom_call_target="tpu_custom_call" | custom-call | flops 4529848320 | bytes 7549747 | tf_op jit(solution)/shard_map/pallas_call | solution.py:615
  33.0 23.4 %collective-permute-done = bf16[1280,768]{1,0:T(8,128)(2,1)} collective-permute-done((bf16[1280,768]{1,0:T(8,128)(2,1)}, bf16[1280,768]{1,0:T(8,128)(2,1)}, u32[]{:S(2)}, u32[]{:S(2)}) %collective-permute-start) | collective-permute-done | bytes 1966112 | tf_op jit(solution)/shard_map/ppermute | solution.py:814
  56.5 1.2 constant_dynamic-slice_fusion.9
  57.7 1.8 collective-permute-start.3
  59.5 8.5 %shard_map.179 = (bf16[10,256,768]{2,1,0:T(8,128)(2,1)S(1)}, bf16[10,256,768]{2,1,0:T(8,128)(2,1)S(1)}, bf16[10,256,768]{2,1,0:T(8,128)(2,1)}, bf16[10,256,768]{2,1,0:T(8,128)(2,1)}, bf16[10,256,768]{2,1,0:T(8,128)(2,1)}) custom-call(bf16[5,256,768]{2,1,0:T(8,128)(2,1)} %bitcast.5.x_ref, ...), custom_call_target="tpu_custom_call", output_to_operand_aliasing={{0}: (3, {}), {1}: (4, {}), {2}: (5, {}), {3}: (6, {}), {4}... | custom-call | flops 4529848320 | bytes 7549747 | tf_op jit(solution)/shard_map/pallas_call | solution.py:615
  68.0 4.6 %shard_map.180 = (f32[10,10,1,256]{3,2,1,0:T(1,128)S(1)}, f32[10,1,256]{2,1,0:T(1,128)S(1)}) custom-call(s32[320]{0:T(512)S(1)} %fusion.9.numbers, bf16[10,256,768]{2,1,0:T(8,128)(2,1)S(1)} %get-tuple-element.58.q_ref, bf16[10,256,768]{2,1,0:T(8,128)(2,1)S(1)} %get-tuple-element.59.k_ref), custom_call_target="tpu_custom_call" | custom-call | flops 838860800 | bytes 1398101 | tf_op jit(solution)/shard_map/pallas_call | solution.py:675
  74.1 30.6 %shard_map.181 = (f32[5,256,768]{2,1,0:T(8,128)}, f32[5,256,768]{2,1,0:T(8,128)}) custom-call(s32[320]{0:T(512)S(1)} %fusion.9.numbers, bf16[10,256,768]{2,1,0:T(8,128)(2,1)S(1)} %get-tuple-element.58.q_ref, bf16[10,256,768]{2,1,0:T(8,128)(2,1)S(1)} %get-tuple-element.59.k_ref, bf16[10,256,768]{2,1,0:T(8,128)(2,1)S(1)} %copy-done.9, ...), custom_call_target="tpu_custom_call" | custom-call | flops 4026531840 | bytes 6710886 | tf_op jit(solution)/shard_map/pallas_call | solution.py:675
  105.3 0.8 slice_dynamic-update-slice_fusion.5
  106.9 60.6 %shard_map.182 = (bf16[5,256,768]{2,1,0:T(8,128)(2,1)}, bf16[5,256,768]{2,1,0:T(8,128)(2,1)}, bf16[5,256,1536]{2,1,0:T(8,128)(2,1)}, bf16[16,432,768]{2,1,0:T(8,128)(2,1)}) custom-call(s32[320]{0:T(512)} %copy-done.12, f32[5,256,768]{2,1,0:T(8,128)} %get-tuple-element.65.att_ref, f32[5,256,768]{2,1,0:T(8,128)} %get-tuple-element.66.inv_ref, ...), custom_call_target="tpu_custom_call" | custom-call | flops 40768634880 | bytes 67947728 | tf_op jit(solution)/shard_map/pallas_call | solution.py:675
  167.7 3.5 collective-permute-done.2
  171.2 1.1 collective-permute-start.4
  172.2 1.4 constant_dynamic-slice_fusion.5
  173.7 1.9 collective-permute-start.5
  175.9 55.8 %shard_map.183 = (bf16[5,256,768]{2,1,0:T(8,128)(2,1)S(1)}, bf16[10,256,768]{2,1,0:T(8,128)(2,1)S(1)}, bf16[10,256,768]{2,1,0:T(8,128)(2,1)S(1)}, f32[5,10,1,256]{3,2,1,0:T(1,128)S(1)}) custom-call(s32[320]{0:T(512)S(1)} %copy-done.13, bf16[10,256,768]{2,1,0:T(8,128)(2,1)} %copy-done, bf16[10,256,768]{2,1,0:T(8,128)(2,1)} %copy-done.2, ...), custom_call_target="tpu_custom_call" | custom-call | flops 12079595520 | bytes 20132660 | tf_op jit(solution)/shard_map/pallas_call | solution.py:675
  231.8 3.5 collective-permute-start.8
  235.4 0.9 slice_dynamic-update-slice_fusion.1
  236.3 0.8 slice_dynamic-update-slice_fusion.branch_ref
  237.0 2.6 collective-permute-start.7
  239.6 5.3 %shard_map.188 = bf16[768,1152]{1,0:T(8,128)(2,1)S(1)} custom-call(bf16[10,256,768]{2,1,0:T(8,128)(2,1)S(1)} %copy-done.6, bf16[10,256,768]{2,1,0:T(8,128)(2,1)S(1)} %get-tuple-element.82.dk_in_ref.dk_ref, bf16[10,256,768]{2,1,0:T(8,128)(2,1)S(1)} %get-tuple-element.85.dv_ref), custom_call_target="tpu_custom_call" | custom-call | flops 4529848320 | bytes 7549747 | tf_op jit(solution)/shard_map/pallas_call | solution.py:791
  245.1 1.0 copy.48
  246.1 0.8 collective-permute-start.9
  247.5 7.3 %shard_map.184 = (bf16[5,256,768]{2,1,0:T(8,128)(2,1)S(1)}, bf16[10,256,768]{2,1,0:T(8,128)(2,1)S(1)}) custom-call(s32[320]{0:T(512)S(1)} %copy-done.13, bf16[10,256,768]{2,1,0:T(8,128)(2,1)S(1)} %copy-done.1, bf16[10,256,768]{2,1,0:T(8,128)(2,1)S(1)} %copy-done.3, ...), custom_call_target="tpu_custom_call", output_to_operand_aliasing={{0}: (4, {}), {1}: (5, {})} | custom-call | flops 1056964608 | bytes 1761607 | tf_op jit(solution)/shard_map/pallas_call | solution.py:675
  254.8 6.2 %shard_map.185 = bf16[5,256,768]{2,1,0:T(8,128)(2,1)S(1)} custom-call(s32[320]{0:T(512)S(1)} %copy-done.13, bf16[5,256,768]{2,1,0:T(8,128)(2,1)S(1)} %get-tuple-element.87.dq_ref, bf16[10,256,768]{2,1,0:T(8,128)(2,1)S(1)} %get-tuple-element.88.dk_ref, bf16[10,256,768]{2,1,0:T(8,128)(2,1)S(1)} %get-tuple-element.85.dv_ref, bf16[768,2304]{1,0:T(8,128)(2,1)S(1)} %copy-done.8), custom_call_target="tpu_custom_call" | custom-call | flops 4529848320 | bytes 7549747 | tf_op jit(solution)/shard_map/pallas_call | solution.py:675
  261.1 4.4 %shard_map.187 = bf16[768,1152]{1,0:T(8,128)(2,1)S(1)} custom-call(s32[320]{0:T(512)S(1)} %copy-done.13, bf16[10,256,768]{2,1,0:T(8,128)(2,1)S(1)} %copy-done.6, bf16[5,256,768]{2,1,0:T(8,128)(2,1)S(1)} %get-tuple-element.87.dq_ref, bf16[10,256,768]{2,1,0:T(8,128)(2,1)S(1)} %get-tuple-element.88.dk_ref), custom_call_target="tpu_custom_call" | custom-call | flops 3019898880 | bytes 5033164 | tf_op jit(solution)/shard_map/pallas_call | solution.py:803
  265.6 1.2 constant_dynamic-slice_fusion.3
  266.7 1.0 copy.49
  267.8 1.5 fusion
  269.5 1.0 collective-permute-done.11
  270.5 1.4 fusion.1
  271.9 3.0 collective-permute-start.12
  274.9 22.8 %collective-permute-done.16 = bf16[2,2,48,1152]{3,2,1,0:T(8,128)(2,1)S(1)} collective-permute-done((bf16[2,2,48,1152]{3,2,1,0:T(8,128)(2,1)S(1)}, bf16[2,2,48,1152]{3,2,1,0:T(8,128)(2,1)S(1)}, u32[]{:S(2)}, u32[]{:S(2)}) %collective-permute-start.16) | collective-permute-done | bytes 442400 | tf_op jit(solution)/shard_map/ppermute | solution.py:837
  298.6 2.5 collective-permute-start.13
  301.2 9.6 %collective-permute-done.17 = bf16[2,48,1152]{2,1,0:T(8,128)(2,1)S(1)} collective-permute-done((bf16[2,48,1152]{2,1,0:T(8,128)(2,1)S(1)}, bf16[2,48,1152]{2,1,0:T(8,128)(2,1)S(1)}, u32[]{:S(2)}, u32[]{:S(2)}) %collective-permute-start.17) | collective-permute-done | bytes 221216 | tf_op jit(solution)/shard_map/ppermute | solution.py:837
  310.9 1.6 collective-permute-start.18
  312.6 3.2 collective-permute-done.18
  315.9 3.6 %collective-permute-done.14 = bf16[48,1152]{1,0:T(8,128)(2,1)S(1)} collective-permute-done((bf16[48,1152]{1,0:T(8,128)(2,1)S(1)}, bf16[48,1152]{1,0:T(8,128)(2,1)S(1)}, u32[]{:S(2)}, u32[]{:S(2)}) %collective-permute-start.14) | collective-permute-done | bytes 110624 | tf_op jit(solution)/shard_map/ppermute | solution.py:837
  319.6 1.6 collective-permute-start.19
  321.7 12.0 %shard_map.186 = bf16[5,256,768]{2,1,0:T(8,128)(2,1)} custom-call(s32[320]{0:T(512)} %copy-done.12, bf16[5,256,768]{2,1,0:T(8,128)(2,1)} %copy-done.5, bf16[10,256,768]{2,1,0:T(8,128)(2,1)} %copy-done.4, bf16[10,256,768]{2,1,0:T(8,128)(2,1)} %copy-done.10, bf16[768,2304]{1,0:T(8,128)(2,1)} %w_ref.7, bf16[5,256,768]{2,1,0:T(8,128)(2,1)} %collective-permute-done.10.back_ref, ...), custom_call_target="tpu_custom_call" | custom-call | flops 4529848320 | bytes 7549747 | tf_op jit(solution)/shard_map/pallas_call | solution.py:675
  333.7 1.9 multiply_reduce_fusion.1
  336.2 5.0 %collective-permute-done.20 = bf16[432,768]{1,0:T(8,128)(2,1)S(1)} collective-permute-done((bf16[432,768]{1,0:T(8,128)(2,1)}, bf16[432,768]{1,0:T(8,128)(2,1)S(1)}, u32[]{:S(2)}, u32[]{:S(2)}) %collective-permute-start.20) | collective-permute-done | bytes 663584 | tf_op jit(solution)/shard_map/ppermute | solution.py:814
  342.1 0.9 fusion.10
  343.0 1.4 multiply_reduce_fusion
  344.4 1.3 dynamic-slice_divide_fusion
  (115 shorter events, 9.9 us)
Async XLA Ops:
  7.2 6.1 %copy-start.25 = (s32[1,5]{1,0:T(1,128)S(1)}, s32[1,5]{1,0:T(1,128)}, u32[]{:S(2)}) copy-start(s32[1,5]{1,0:T(1,128)} %param.13) | copy-start | bytes 64
  7.2 12.9 %copy-start.24 = (f32[768]{0:T(1024)S(1)}, f32[768]{0:T(1024)}, u32[]{:S(2)}) copy-start(f32[768]{0:T(1024)} %param.15) | copy-start | bytes 9220
  7.2 16.9 %copy-start.7 = (bf16[768,2304]{1,0:T(8,128)(2,1)S(1)}, bf16[768,2304]{1,0:T(8,128)(2,1)}, u32[]{:S(2)}) copy-start(bf16[768,2304]{1,0:T(8,128)(2,1)} %w_ref.7) | copy-start | bytes 10616836
  7.2 312.4 %reduce-scatter.2.cloned.1.call-start = ((), (), s32[]{:S(2)}) async-start(), calls=%async_computation.1 | async-start | bytes 11280384 | tf_op jit(solution)/shard_map/reduce_scatter | solution.py:920
  10.3 46.1 %collective-permute-start = (bf16[1280,768]{1,0:T(8,128)(2,1)}, bf16[1280,768]{1,0:T(8,128)(2,1)}, u32[]{:S(2)}, u32[]{:S(2)}) collective-permute-start(bf16[1280,768]{1,0:T(8,128)(2,1)} %bitcast.70), channel_id=1, source_target_pairs={{0,16},{16,0},{1,17},{17,1},{2,18},{18,2},{3,19},{19,3},{4,20},{20... | collective-permute-start | bytes 5898248 | tf_op jit(solution)/shard_map/ppermute | solution.py:814
  20.1 39.4 %copy-start.14 = (f32[1,768]{1,0:T(1,128)}, f32[1,768]{1,0:T(1,128)S(1)}, u32[]{:S(2)}) copy-start(f32[1,768]{1,0:T(1,128)S(1)} %reshape.180.gain_ref) | copy-start | bytes 9220
  24.1 49.9 %copy-start.12 = (s32[320]{0:T(512)}, s32[320]{0:T(512)S(1)}, u32[]{:S(2)}) copy-start(s32[320]{0:T(512)S(1)} %fusion.9.numbers) | copy-start | bytes 3844
  24.1 1.5 copy-start.11
  57.7 47.6 %collective-permute-start.3 = (bf16[2,256,768]{2,1,0:T(8,128)(2,1)S(1)}, bf16[2,256,768]{2,1,0:T(8,128)(2,1)S(1)}, u32[]{:S(2)}, u32[]{:S(2)}) collective-permute-start(bf16[2,256,768]{2,1,0:T(8,128)(2,1)S(1)} %pad_maximum_fusion), channel_id=1, source_target_pairs={{0,16},{16,0},{1,17},{17,1},{2,18},{18,2},{3,19},{19,3},{4,20},{20... | collective-permute-start | bytes 2359304 | tf_op jit(solution)/shard_map/ppermute | solution.py:814
  68.0 6.1 %copy-start = (bf16[10,256,768]{2,1,0:T(8,128)(2,1)}, bf16[10,256,768]{2,1,0:T(8,128)(2,1)S(1)}, u32[]{:S(2)}) copy-start(bf16[10,256,768]{2,1,0:T(8,128)(2,1)S(1)} %get-tuple-element.58.q_ref) | copy-start | bytes 11796484
  68.0 6.1 %copy-start.2 = (bf16[10,256,768]{2,1,0:T(8,128)(2,1)}, bf16[10,256,768]{2,1,0:T(8,128)(2,1)S(1)}, u32[]{:S(2)}) copy-start(bf16[10,256,768]{2,1,0:T(8,128)(2,1)S(1)} %get-tuple-element.59.k_ref) | copy-start | bytes 11796484
  68.0 4.7 %copy-start.23 = (f32[10,1,256]{2,1,0:T(1,128)S(1)}, f32[10,1,256]{2,1,0:T(1,128)}, u32[]{:S(2)}) copy-start(f32[10,1,256]{2,1,0:T(1,128)} %div.48) | copy-start | bytes 30724
  68.0 6.1 %copy-start.9 = (bf16[10,256,768]{2,1,0:T(8,128)(2,1)S(1)}, bf16[10,256,768]{2,1,0:T(8,128)(2,1)}, u32[]{:S(2)}) copy-start(bf16[10,256,768]{2,1,0:T(8,128)(2,1)} %get-tuple-element.61.v_ref) | copy-start | bytes 11796484
  74.0 30.7 %collective-permute-start.1 = (f32[1,128]{1,0:T(1,128)S(1)}, f32[1,128]{1,0:T(1,128)S(1)}, u32[]{:S(2)}, u32[]{:S(2)}) collective-permute-start(f32[1,128]{1,0:T(1,128)S(1)} %broadcast_in_dim.31), channel_id=1, source_target_pairs={{0,1},{1,0},{2,3},{3,2},{4,5},{5,4},{6,7},{7,6},{8,9},{9,8},{10,11... | collective-permute-start | bytes 1544 | tf_op jit(solution)/shard_map/ppermute | solution.py:904
  167.5 4.7 %copy-start.21 = (bf16[5,256,768]{2,1,0:T(8,128)(2,1)S(1)}, bf16[5,256,768]{2,1,0:T(8,128)(2,1)}, u32[]{:S(2)}) copy-start(bf16[5,256,768]{2,1,0:T(8,128)(2,1)} %get-tuple-element.74) | copy-start | bytes 5898244
  167.6 3.6 %collective-permute-start.2 = (f32[1,128]{1,0:T(1,128)S(1)}, f32[1,128]{1,0:T(1,128)S(1)}, u32[]{:S(2)}, u32[]{:S(2)}) collective-permute-start(f32[1,128]{1,0:T(1,128)S(1)} %broadcast_add_fusion), channel_id=1, source_target_pairs={{0,2},{1,3},{2,0},{3,1},{4,6},{5,7},{6,4},{7,5},{8,10},{9,11},{10,... | collective-permute-start | bytes 1544 | tf_op jit(solution)/shard_map/ppermute | solution.py:904
  171.2 64.1 %collective-permute-start.4 = (f32[1,128]{1,0:T(1,128)S(1)}, f32[1,128]{1,0:T(1,128)S(1)}, u32[]{:S(2)}, u32[]{:S(2)}) collective-permute-start(f32[1,128]{1,0:T(1,128)S(1)} %add.142), channel_id=1, source_target_pairs={{0,4},{1,5},{2,6},{3,7},{4,0},{5,1},{6,2},{7,3},{8,12},{9,13},{10,... | collective-permute-start | bytes 1544 | tf_op jit(solution)/shard_map/ppermute | solution.py:904
  172.2 3.7 %copy-start.17 = (bf16[5,256,1536]{2,1,0:T(8,128)(2,1)S(1)}, bf16[5,256,1536]{2,1,0:T(8,128)(2,1)}, u32[]{:S(2)}) copy-start(bf16[5,256,1536]{2,1,0:T(8,128)(2,1)} %get-tuple-element.71.dx_ref) | copy-start | bytes 11796484
  173.6 2.3 copy-start.13
  173.7 61.6 %collective-permute-start.5 = (bf16[2,256,768]{2,1,0:T(8,128)(2,1)S(1)}, bf16[2,256,768]{2,1,0:T(8,128)(2,1)S(1)}, u32[]{:S(2)}, u32[]{:S(2)}) collective-permute-start(bf16[2,256,768]{2,1,0:T(8,128)(2,1)S(1)} %pad_maximum_fusion.1), channel_id=1, source_target_pairs={{0,16},{16,0},{1,17},{17,1},{2,18},{18,2},{3,19},{19,3},{4,20},{20... | collective-permute-start | bytes 2359304 | tf_op jit(solution)/shard_map/ppermute | solution.py:814
  175.7 59.7 %collective-permute-start.6 = (bf16[2,256,768]{2,1,0:T(8,128)(2,1)S(1)}, bf16[2,256,768]{2,1,0:T(8,128)(2,1)S(1)}, u32[]{:S(2)}, u32[]{:S(2)}) collective-permute-start(bf16[2,256,768]{2,1,0:T(8,128)(2,1)S(1)} %pad_maximum_fusion.2), channel_id=1, source_target_pairs={{0,16},{16,0},{1,17},{17,1},{2,18},{18,2},{3,19},{19,3},{4,20},{20... | collective-permute-start | bytes 2359304 | tf_op jit(solution)/shard_map/ppermute | solution.py:814
  175.9 63.7 %copy-start.6 = (bf16[10,256,768]{2,1,0:T(8,128)(2,1)S(1)}, bf16[10,256,768]{2,1,0:T(8,128)(2,1)}, u32[]{:S(2)}) copy-start(bf16[10,256,768]{2,1,0:T(8,128)(2,1)} %get-tuple-element.90.normed_ref) | copy-start | bytes 11796484
  231.8 23.1 %copy-start.10 = (bf16[10,256,768]{2,1,0:T(8,128)(2,1)}, bf16[10,256,768]{2,1,0:T(8,128)(2,1)S(1)}, u32[]{:S(2)}) copy-start(bf16[10,256,768]{2,1,0:T(8,128)(2,1)S(1)} %get-tuple-element.85.dv_ref) | copy-start | bytes 11796484
  231.8 14.4 %collective-permute-start.8 = (f32[5,10,1,256]{3,2,1,0:T(1,128)S(1)}, f32[5,10,1,256]{3,2,1,0:T(1,128)S(1)}, u32[]{:S(2)}, u32[]{:S(2)}) collective-permute-start(f32[5,10,1,256]{3,2,1,0:T(1,128)S(1)} %get-tuple-element.78), channel_id=1, source_target_pairs={{0,16},{16,0},{1,17},{17,1},{2,18},{18,2},{3,19},{19,3},{4,20},{20... | collective-permute-start | bytes 153608 | tf_op jit(solution)/shard_map/ppermute | solution.py:814
  235.4 9.6 %copy-start.22 = (bf16[5,256,768]{2,1,0:T(8,128)(2,1)}, bf16[5,256,768]{2,1,0:T(8,128)(2,1)S(1)}, u32[]{:S(2)}) copy-start(bf16[5,256,768]{2,1,0:T(8,128)(2,1)S(1)} %slice_dynamic-update-slice_fusion.2) | copy-start | bytes 5898244
  237.0 9.1 %collective-permute-start.7 = (f32[1,128]{1,0:T(1,128)S(1)}, f32[1,128]{1,0:T(1,128)S(1)}, u32[]{:S(2)}, u32[]{:S(2)}) collective-permute-start(f32[1,128]{1,0:T(1,128)S(1)} %add.145), channel_id=1, source_target_pairs={{0,8},{1,9},{2,10},{3,11},{4,12},{5,13},{6,14},{7,15},{8,0},{9,1},... | collective-permute-start | bytes 1544 | tf_op jit(solution)/shard_map/ppermute | solution.py:904
  239.6 7.3 %copy-start.3 = (bf16[10,256,768]{2,1,0:T(8,128)(2,1)S(1)}, bf16[10,256,768]{2,1,0:T(8,128)(2,1)}, u32[]{:S(2)}) copy-start(bf16[10,256,768]{2,1,0:T(8,128)(2,1)} %copy-done.2) | copy-start | bytes 11796484
  245.0 2.5 copy-start.1
  246.1 21.7 %collective-permute-start.15 = (bf16[2,2,2,48,1152]{4,3,2,0,1:T(8,128)(2,1)}, bf16[2,2,2,48,1152]{4,3,2,0,1:T(8,128)(2,1)}, u32[]{:S(2)}, u32[]{:S(2)}) collective-permute-start(bf16[2,2,2,48,1152]{4,3,2,0,1:T(8,128)(2,1)} %bitcast.66), channel_id=1, source_target_pairs={{0,1},{1,0},{2,3},{3,2},{4,5},{5,4},{6,7},{7,6},{8,9},{9,8},{10,11... | collective-permute-start | bytes 2654216 | tf_op jit(solution)/shard_map/ppermute | solution.py:837
  246.1 14.9 %collective-permute-start.9 = (f32[1,128]{1,0:T(1,128)S(1)}, f32[1,128]{1,0:T(1,128)S(1)}, u32[]{:S(2)}, u32[]{:S(2)}) collective-permute-start(f32[1,128]{1,0:T(1,128)S(1)} %add.146), channel_id=1, source_target_pairs={{0,16},{16,0},{1,17},{17,1},{2,18},{18,2},{3,19},{19,3},{4,20},{20... | collective-permute-start | bytes 1544 | tf_op jit(solution)/shard_map/ppermute | solution.py:904
  247.5 7.4 %copy-start.8 = (bf16[768,2304]{1,0:T(8,128)(2,1)S(1)}, bf16[768,2304]{1,0:T(8,128)(2,1)}, u32[]{:S(2)}) copy-start(bf16[768,2304]{1,0:T(8,128)(2,1)} %w_ref.7) | copy-start | bytes 10616836
  254.8 6.3 %copy-start.4 = (bf16[10,256,768]{2,1,0:T(8,128)(2,1)}, bf16[10,256,768]{2,1,0:T(8,128)(2,1)S(1)}, u32[]{:S(2)}) copy-start(bf16[10,256,768]{2,1,0:T(8,128)(2,1)S(1)} %get-tuple-element.88.dk_ref) | copy-start | bytes 11796484
  254.8 6.3 %copy-start.5 = (bf16[5,256,768]{2,1,0:T(8,128)(2,1)}, bf16[5,256,768]{2,1,0:T(8,128)(2,1)S(1)}, u32[]{:S(2)}) copy-start(bf16[5,256,768]{2,1,0:T(8,128)(2,1)S(1)} %get-tuple-element.87.dq_ref) | copy-start | bytes 5898244
  261.1 4.5 %copy-start.15 = (bf16[5,256,768]{2,1,0:T(8,128)(2,1)}, bf16[5,256,768]{2,1,0:T(8,128)(2,1)S(1)}, u32[]{:S(2)}) copy-start(bf16[5,256,768]{2,1,0:T(8,128)(2,1)S(1)} %shard_map.185) | copy-start | bytes 5898244
  265.5 2.2 copy-start.16
  267.7 2.8 collective-permute-start.11
  267.7 2.8 copy-start.18
  267.7 51.8 %collective-permute-start.10 = (bf16[5,256,768]{2,1,0:T(8,128)(2,1)S(1)}, bf16[5,256,768]{2,1,0:T(8,128)(2,1)}, u32[]{:S(2)}, u32[]{:S(2)}) collective-permute-start(bf16[5,256,768]{2,1,0:T(8,128)(2,1)S(1)} %copy-done.16), channel_id=1, source_target_pairs={{0,16},{16,0},{1,17},{17,1},{2,18},{18,2},{3,19},{19,3},{4,20},{20... | collective-permute-start | bytes 5898248 | tf_op jit(solution)/shard_map/ppermute | solution.py:814
  269.4 28.4 %collective-permute-start.16 = (bf16[2,2,48,1152]{3,2,1,0:T(8,128)(2,1)S(1)}, bf16[2,2,48,1152]{3,2,1,0:T(8,128)(2,1)S(1)}, u32[]{:S(2)}, u32[]{:S(2)}) collective-permute-start(bf16[2,2,48,1152]{3,2,1,0:T(8,128)(2,1)S(1)} %dynamic-slice_bitcast_fusion), channel_id=1, source_target_pairs={{0,4},{1,5},{2,6},{3,7},{4,0},{5,1},{6,2},{7,3},{8,12},{9,13},{10,... | collective-permute-start | bytes 1327112 | tf_op jit(solution)/shard_map/ppermute | solution.py:837
  271.9 26.5 %collective-permute-start.12 = (bf16[2,2,48,1152]{3,2,0,1:T(8,128)(2,1)S(1)}, bf16[2,2,48,1152]{3,2,0,1:T(8,128)(2,1)S(1)}, u32[]{:S(2)}, u32[]{:S(2)}) collective-permute-start(bf16[2,2,48,1152]{3,2,0,1:T(8,128)(2,1)S(1)} %dynamic-slice_bitcast_fusion.1), channel_id=1, source_target_pairs={{0,2},{1,3},{2,0},{3,1},{4,6},{5,7},{6,4},{7,5},{8,10},{9,11},{10,... | collective-permute-start | bytes 1327112 | tf_op jit(solution)/shard_map/ppermute | solution.py:837
  297.9 12.8 %collective-permute-start.17 = (bf16[2,48,1152]{2,1,0:T(8,128)(2,1)S(1)}, bf16[2,48,1152]{2,1,0:T(8,128)(2,1)S(1)}, u32[]{:S(2)}, u32[]{:S(2)}) collective-permute-start(bf16[2,48,1152]{2,1,0:T(8,128)(2,1)S(1)} %dynamic-slice_bitcast_fusion.2), channel_id=1, source_target_pairs={{0,8},{1,9},{2,10},{3,11},{4,12},{5,13},{6,14},{7,15},{8,0},{9,1},... | collective-permute-start | bytes 663560 | tf_op jit(solution)/shard_map/ppermute | solution.py:837
  298.6 13.8 %collective-permute-start.13 = (bf16[2,48,1152]{2,1,0:T(8,128)(2,1)S(1)}, bf16[2,48,1152]{2,1,0:T(8,128)(2,1)S(1)}, u32[]{:S(2)}, u32[]{:S(2)}) collective-permute-start(bf16[2,48,1152]{2,1,0:T(8,128)(2,1)S(1)} %dynamic-slice_bitcast_fusion.3), channel_id=1, source_target_pairs={{0,4},{1,5},{2,6},{3,7},{4,0},{5,1},{6,2},{7,3},{8,12},{9,13},{10,... | collective-permute-start | bytes 663560 | tf_op jit(solution)/shard_map/ppermute | solution.py:837
  310.9 5.0 %collective-permute-start.18 = (bf16[48,1152]{1,0:T(8,128)(2,1)S(1)}, bf16[48,1152]{1,0:T(8,128)(2,1)S(1)}, u32[]{:S(2)}, u32[]{:S(2)}) collective-permute-start(bf16[48,1152]{1,0:T(8,128)(2,1)S(1)} %dynamic-slice_bitcast_fusion.4), channel_id=1, source_target_pairs={{0,2},{1,3},{2,0},{3,1},{4,6},{5,7},{6,4},{7,5},{8,10},{9,11},{10,... | collective-permute-start | bytes 331784 | tf_op jit(solution)/shard_map/ppermute | solution.py:837
  312.6 6.9 %collective-permute-start.14 = (bf16[48,1152]{1,0:T(8,128)(2,1)S(1)}, bf16[48,1152]{1,0:T(8,128)(2,1)S(1)}, u32[]{:S(2)}, u32[]{:S(2)}) collective-permute-start(bf16[48,1152]{1,0:T(8,128)(2,1)S(1)} %dynamic-slice_bitcast_fusion.5), channel_id=1, source_target_pairs={{0,8},{1,9},{2,10},{3,11},{4,12},{5,13},{6,14},{7,15},{8,0},{9,1},... | collective-permute-start | bytes 331784 | tf_op jit(solution)/shard_map/ppermute | solution.py:837
  319.6 21.6 %copy-start.20 = (bf16[1,432,768]{2,1,0:T(8,128)(2,1)S(1)}, bf16[1,432,768]{2,1,0:T(8,128)(2,1)}, u32[]{:S(2)}) copy-start(bf16[1,432,768]{2,1,0:T(8,128)(2,1)} %reduce-scatter.2.cloned.1.call-done) | copy-start | bytes 1990660
  319.6 14.1 %collective-permute-start.19 = (bf16[48,2304]{1,0:T(8,128)(2,1)S(1)}, bf16[48,2304]{1,0:T(8,128)(2,1)S(1)}, u32[]{:S(2)}, u32[]{:S(2)}) collective-permute-start(bf16[48,2304]{1,0:T(8,128)(2,1)S(1)} %pad_maximum_fusion.3), channel_id=1, source_target_pairs={{0,16},{16,0},{1,17},{17,1},{2,18},{18,2},{3,19},{19,3},{4,20},{20... | collective-permute-start | bytes 663560 | tf_op jit(solution)/shard_map/ppermute | solution.py:814
  321.2 20.0 %collective-permute-start.20 = (bf16[432,768]{1,0:T(8,128)(2,1)}, bf16[432,768]{1,0:T(8,128)(2,1)S(1)}, u32[]{:S(2)}, u32[]{:S(2)}) collective-permute-start(bf16[432,768]{1,0:T(8,128)(2,1)} %bitcast.78), channel_id=1, source_target_pairs={{0,16},{16,0},{1,17},{17,1},{2,18},{18,2},{3,19},{19,3},{4,20},{20... | collective-permute-start | bytes 1990664 | tf_op jit(solution)/shard_map/ppermute | solution.py:814
  343.0 2.7 copy-start.19
Sparse Core Ops, SparseCore 0:
  167.7 129.8 reduce-scatter.1

commit v5 on v4

--- a/solution.py
+++ b/solution.py
@@ -904,12 +904,10 @@
             excess += lax.ppermute(excess, axis, [(i, i ^ bit) for i in range(lax.axis_size(axis))])
         return lax.optimization_barrier((excess, result))
 
-    excess, attended = hop_beside(excess, attended)
 
     out_c, branch_c, dx, early_grads = middle(
         layout, numbers, attended, inverse, x_all, cot, out_weight, up_weight, down_weight, mlp_gain, dp_count
     )
-    excess, dx = hop_beside(excess, dx)
     output = swap_tiles(out_c)
     branch = swap_tiles(branch_c)
     parts_hid = hid // width

time: 359 us -> 357 us (level)
    ppermute x8, waiting for transfers between devices: 40.3 us -> 32.5 us  [scatter_halving(): got = lax.ppermute(send, 'dp', [(i, i ^ 1 << n) for i in range(count)])]
  transfers between devices with their start and end apart: 22 -> 22, of which waited for: 8 -> 9; matrix products, arithmetic and copies ran while one was open for 5% -> 5% of each run, Pallas kernels for 40% -> 41%
where the time goes in v5:
time: 357 us; the launch traced here: 351 us
  Pallas kernels  203 us (57%)
  waiting for transfers between devices  70.4 us (20%)
  starting transfers between devices  26.1 us (7%)
  between operations  22.3 us (6%)
  local copies, waits for them, and re-layouts  19.8 us (6%)
  other arithmetic  9.71 us (3%)
    pallas_call x7, Pallas kernels, kernel_call(): pl.pallas_call(kernel, grid_spec=pltpu.PrefetchScalarGridSpec(num_scalar_...  178 us
    ppermute x8, waiting for transfers between devices, scatter_halving(): got = lax.ppermute(send, 'dp', [(i, i ^ 1 << n) for i in range(count)])  32.5 us
    ppermute x8, waiting for transfers between devices, swap_seq(): return lax.ppermute(array, 'seq', [(0, 1), (1, 0)])  30.8 us
    pallas_call x2, Pallas kernels, project(): pl.pallas_call(project_kernel, grid=(owned,), out_shape=outs, in_specs=[r...  15.7 us
    ppermute x8, starting transfers between devices, swap_seq(): return lax.ppermute(array, 'seq', [(0, 1), (1, 0)])  13.8 us
    ppermute x8, starting transfers between devices, scatter_halving(): got = lax.ppermute(send, 'dp', [(i, i ^ 1 << n) for i in range(count)])  8.29 us
  transfers between devices with their start and end apart: 22, of which 9 were waited for; matrix products, arithmetic and copies ran while one was open for 5% of the time, Pallas kernels for 41%

profile of v5, /device:TPU:0, one launch (start us, length us, event | category | flops | bytes accessed | tf_op | source)
XLA Modules:
  0.0 351.4 jit_solution(8122001733097491565)
XLA Ops:
  7.3 3.1 copy.65
  10.4 3.0 collective-permute-start
  15.2 1.4 fusion.11
  21.1 0.7 fusion.9.numbers
  21.9 1.5 copy-done.11
  23.4 7.3 %shard_map.178 = (bf16[10,256,768]{2,1,0:T(8,128)(2,1)S(1)}, bf16[10,256,768]{2,1,0:T(8,128)(2,1)S(1)}, bf16[10,256,768]{2,1,0:T(8,128)(2,1)}, bf16[10,256,768]{2,1,0:T(8,128)(2,1)}, bf16[10,256,768]{2,1,0:T(8,128)(2,1)}) custom-call(bf16[5,256,768]{2,1,0:T(8,128)(2,1)S(1)} %bitcast.72, bf16[768,2304]{1,0:T(8,128)(2,1)S(1)} %copy-done.7, ...), custom_call_target="tpu_custom_call" | custom-call | flops 4529848320 | bytes 7549747 | tf_op jit(solution)/shard_map/pallas_call | solution.py:615
  30.7 25.7 %collective-permute-done = bf16[1280,768]{1,0:T(8,128)(2,1)} collective-permute-done((bf16[1280,768]{1,0:T(8,128)(2,1)}, bf16[1280,768]{1,0:T(8,128)(2,1)}, u32[]{:S(2)}, u32[]{:S(2)}) %collective-permute-start) | collective-permute-done | bytes 1966112 | tf_op jit(solution)/shard_map/ppermute | solution.py:814
  56.5 1.2 constant_dynamic-slice_fusion.9
  57.7 1.8 collective-permute-start.2
  59.5 8.4 %shard_map.179 = (bf16[10,256,768]{2,1,0:T(8,128)(2,1)S(1)}, bf16[10,256,768]{2,1,0:T(8,128)(2,1)S(1)}, bf16[10,256,768]{2,1,0:T(8,128)(2,1)}, bf16[10,256,768]{2,1,0:T(8,128)(2,1)}, bf16[10,256,768]{2,1,0:T(8,128)(2,1)}) custom-call(bf16[5,256,768]{2,1,0:T(8,128)(2,1)} %bitcast.5.x_ref, ...), custom_call_target="tpu_custom_call", output_to_operand_aliasing={{0}: (3, {}), {1}: (4, {}), {2}: (5, {}), {3}: (6, {}), {4}... | custom-call | flops 4529848320 | bytes 7549747 | tf_op jit(solution)/shard_map/pallas_call | solution.py:615
  67.9 4.6 %shard_map.180 = (f32[10,10,1,256]{3,2,1,0:T(1,128)S(1)}, f32[10,1,256]{2,1,0:T(1,128)S(1)}) custom-call(s32[320]{0:T(512)S(1)} %fusion.9.numbers, bf16[10,256,768]{2,1,0:T(8,128)(2,1)S(1)} %get-tuple-element.56.q_ref, bf16[10,256,768]{2,1,0:T(8,128)(2,1)S(1)} %get-tuple-element.57.k_ref), custom_call_target="tpu_custom_call" | custom-call | flops 838860800 | bytes 1398101 | tf_op jit(solution)/shard_map/pallas_call | solution.py:675
  72.9 30.6 %shard_map.181 = (f32[5,256,768]{2,1,0:T(8,128)}, f32[5,256,768]{2,1,0:T(8,128)}) custom-call(s32[320]{0:T(512)S(1)} %fusion.9.numbers, bf16[10,256,768]{2,1,0:T(8,128)(2,1)S(1)} %get-tuple-element.56.q_ref, bf16[10,256,768]{2,1,0:T(8,128)(2,1)S(1)} %get-tuple-element.57.k_ref, bf16[10,256,768]{2,1,0:T(8,128)(2,1)S(1)} %copy-done.9, ...), custom_call_target="tpu_custom_call" | custom-call | flops 4026531840 | bytes 6710886 | tf_op jit(solution)/shard_map/pallas_call | solution.py:675
  103.5 0.8 slice_dynamic-update-slice_fusion.5
  104.3 0.8 slice_dynamic-update-slice_fusion.4
  105.0 60.5 %shard_map.182 = (bf16[5,256,768]{2,1,0:T(8,128)(2,1)}, bf16[5,256,768]{2,1,0:T(8,128)(2,1)}, bf16[5,256,1536]{2,1,0:T(8,128)(2,1)}, bf16[16,432,768]{2,1,0:T(8,128)(2,1)}) custom-call(s32[320]{0:T(512)} %copy-done.12, f32[5,256,768]{2,1,0:T(8,128)} %get-tuple-element.61.att_ref, f32[5,256,768]{2,1,0:T(8,128)} %get-tuple-element.62.inv_ref, ...), custom_call_target="tpu_custom_call" | custom-call | flops 40768634880 | bytes 67947728 | tf_op jit(solution)/shard_map/pallas_call | solution.py:675
  168.2 1.1 collective-permute-done.1
  170.0 1.4 constant_dynamic-slice_fusion.5
  171.5 1.7 collective-permute-start.3
  173.8 56.3 %shard_map.183 = (bf16[5,256,768]{2,1,0:T(8,128)(2,1)S(1)}, bf16[10,256,768]{2,1,0:T(8,128)(2,1)S(1)}, bf16[10,256,768]{2,1,0:T(8,128)(2,1)S(1)}, f32[5,10,1,256]{3,2,1,0:T(1,128)S(1)}) custom-call(s32[320]{0:T(512)S(1)} %copy-done.13, bf16[10,256,768]{2,1,0:T(8,128)(2,1)} %copy-done, bf16[10,256,768]{2,1,0:T(8,128)(2,1)} %copy-done.2, ...), custom_call_target="tpu_custom_call" | custom-call | flops 12079595520 | bytes 20132660 | tf_op jit(solution)/shard_map/pallas_call | solution.py:675
  230.1 3.3 collective-permute-start.6
  233.4 0.8 slice_dynamic-update-slice_fusion.3
  234.2 0.8 slice_dynamic-update-slice_fusion.2
  235.2 5.3 %shard_map.188 = bf16[768,1152]{1,0:T(8,128)(2,1)S(1)} custom-call(bf16[10,256,768]{2,1,0:T(8,128)(2,1)S(1)} %copy-done.6, bf16[10,256,768]{2,1,0:T(8,128)(2,1)S(1)} %get-tuple-element.76.dk_in_ref.dk_ref, bf16[10,256,768]{2,1,0:T(8,128)(2,1)S(1)} %get-tuple-element.79.dv_ref), custom_call_target="tpu_custom_call" | custom-call | flops 4529848320 | bytes 7549747 | tf_op jit(solution)/shard_map/pallas_call | solution.py:791
  240.6 1.0 copy.48
  242.3 3.2 collective-permute-start.7
  245.5 7.3 %shard_map.184 = (bf16[5,256,768]{2,1,0:T(8,128)(2,1)S(1)}, bf16[10,256,768]{2,1,0:T(8,128)(2,1)S(1)}) custom-call(s32[320]{0:T(512)S(1)} %copy-done.13, bf16[10,256,768]{2,1,0:T(8,128)(2,1)S(1)} %copy-done.1, bf16[10,256,768]{2,1,0:T(8,128)(2,1)S(1)} %copy-done.3, ...), custom_call_target="tpu_custom_call", output_to_operand_aliasing={{0}: (4, {}), {1}: (5, {})} | custom-call | flops 1056964608 | bytes 1761607 | tf_op jit(solution)/shard_map/pallas_call | solution.py:675
  252.9 6.2 %shard_map.185 = bf16[5,256,768]{2,1,0:T(8,128)(2,1)S(1)} custom-call(s32[320]{0:T(512)S(1)} %copy-done.13, bf16[5,256,768]{2,1,0:T(8,128)(2,1)S(1)} %get-tuple-element.81.dq_ref, bf16[10,256,768]{2,1,0:T(8,128)(2,1)S(1)} %get-tuple-element.82.dk_ref, bf16[10,256,768]{2,1,0:T(8,128)(2,1)S(1)} %get-tuple-element.79.dv_ref, bf16[768,2304]{1,0:T(8,128)(2,1)S(1)} %copy-done.8), custom_call_target="tpu_custom_call" | custom-call | flops 4529848320 | bytes 7549747 | tf_op jit(solution)/shard_map/pallas_call | solution.py:675
  259.2 4.4 %shard_map.187 = bf16[768,1152]{1,0:T(8,128)(2,1)S(1)} custom-call(s32[320]{0:T(512)S(1)} %copy-done.13, bf16[10,256,768]{2,1,0:T(8,128)(2,1)S(1)} %copy-done.6, bf16[5,256,768]{2,1,0:T(8,128)(2,1)S(1)} %get-tuple-element.81.dq_ref, bf16[10,256,768]{2,1,0:T(8,128)(2,1)S(1)} %get-tuple-element.82.dk_ref), custom_call_target="tpu_custom_call" | custom-call | flops 3019898880 | bytes 5033164 | tf_op jit(solution)/shard_map/pallas_call | solution.py:803
  263.5 1.2 constant_dynamic-slice_fusion.3
  264.7 1.0 copy.49
  265.7 4.4 %collective-permute-done.19 = f32[1,128]{1,0:T(1,128)S(1)} collective-permute-done((f32[1,128]{1,0:T(1,128)S(1)}, f32[1,128]{1,0:T(1,128)S(1)}, u32[]{:S(2)}, u32[]{:S(2)}) %collective-permute-start.19) | collective-permute-done | bytes 544 | tf_op jit(solution)/shard_map/ppermute | solution.py:904
  270.8 1.5 collective-permute-start.8
  272.2 1.5 collective-permute-done.20
  273.8 1.4 fusion
  275.3 1.4 fusion.1
  276.8 2.9 collective-permute-start.10
  279.7 16.1 %collective-permute-done.14 = bf16[2,2,48,1152]{3,2,1,0:T(8,128)(2,1)S(1)} collective-permute-done((bf16[2,2,48,1152]{3,2,1,0:T(8,128)(2,1)S(1)}, bf16[2,2,48,1152]{3,2,1,0:T(8,128)(2,1)S(1)}, u32[]{:S(2)}, u32[]{:S(2)}) %collective-permute-start.14) | collective-permute-done | bytes 442400 | tf_op jit(solution)/shard_map/ppermute | solution.py:837
  295.9 2.5 collective-permute-start.15
  299.1 9.6 %collective-permute-done.15 = bf16[2,48,1152]{2,1,0:T(8,128)(2,1)S(1)} collective-permute-done((bf16[2,48,1152]{2,1,0:T(8,128)(2,1)S(1)}, bf16[2,48,1152]{2,1,0:T(8,128)(2,1)S(1)}, u32[]{:S(2)}, u32[]{:S(2)}) %collective-permute-start.15) | collective-permute-done | bytes 221216 | tf_op jit(solution)/shard_map/ppermute | solution.py:837
  308.9 1.6 collective-permute-start.16
  310.6 3.3 collective-permute-done.16
  313.9 3.5 %collective-permute-done.12 = bf16[48,1152]{1,0:T(8,128)(2,1)S(1)} collective-permute-done((bf16[48,1152]{1,0:T(8,128)(2,1)S(1)}, bf16[48,1152]{1,0:T(8,128)(2,1)S(1)}, u32[]{:S(2)}, u32[]{:S(2)}) %collective-permute-start.12) | collective-permute-done | bytes 110624 | tf_op jit(solution)/shard_map/ppermute | solution.py:837
  317.5 1.5 collective-permute-start.17
  319.6 12.0 %shard_map.186 = bf16[5,256,768]{2,1,0:T(8,128)(2,1)} custom-call(s32[320]{0:T(512)} %copy-done.12, bf16[5,256,768]{2,1,0:T(8,128)(2,1)} %copy-done.5, bf16[10,256,768]{2,1,0:T(8,128)(2,1)} %copy-done.4, bf16[10,256,768]{2,1,0:T(8,128)(2,1)} %copy-done.10, bf16[768,2304]{1,0:T(8,128)(2,1)} %w_ref.7, bf16[5,256,768]{2,1,0:T(8,128)(2,1)} %collective-permute-done.8.back_ref, ...), custom_call_target="tpu_custom_call" | custom-call | flops 4529848320 | bytes 7549747 | tf_op jit(solution)/shard_map/pallas_call | solution.py:675
  331.7 1.9 multiply_reduce_fusion.1
  334.2 5.0 %collective-permute-done.18 = bf16[432,768]{1,0:T(8,128)(2,1)S(1)} collective-permute-done((bf16[432,768]{1,0:T(8,128)(2,1)}, bf16[432,768]{1,0:T(8,128)(2,1)S(1)}, u32[]{:S(2)}, u32[]{:S(2)}) %collective-permute-start.18) | collective-permute-done | bytes 663584 | tf_op jit(solution)/shard_map/ppermute | solution.py:814
  340.0 0.9 fusion.10
  341.0 1.4 multiply_reduce_fusion
  (115 shorter events, 10.3 us)
Async XLA Ops:
  7.2 6.2 %copy-start.25 = (s32[1,5]{1,0:T(1,128)S(1)}, s32[1,5]{1,0:T(1,128)}, u32[]{:S(2)}) copy-start(s32[1,5]{1,0:T(1,128)} %param.13) | copy-start | bytes 64
  7.2 12.0 %copy-start.23 = (f32[768]{0:T(1024)S(1)}, f32[768]{0:T(1024)}, u32[]{:S(2)}) copy-start(f32[768]{0:T(1024)} %param.15) | copy-start | bytes 9220
  7.2 14.7 %copy-start.7 = (bf16[768,2304]{1,0:T(8,128)(2,1)S(1)}, bf16[768,2304]{1,0:T(8,128)(2,1)}, u32[]{:S(2)}) copy-start(bf16[768,2304]{1,0:T(8,128)(2,1)} %w_ref.7) | copy-start | bytes 10616836
  7.2 12.0 %copy-start.24 = (f32[768]{0:T(1024)S(1)}, f32[768]{0:T(1024)}, u32[]{:S(2)}) copy-start(f32[768]{0:T(1024)} %param.18) | copy-start | bytes 9220
  7.2 310.3 %reduce-scatter.2.cloned.1.call-start = ((), (), s32[]{:S(2)}) async-start(), calls=%async_computation.1 | async-start | bytes 11280384 | tf_op jit(solution)/shard_map/reduce_scatter | solution.py:918
  10.4 46.1 %collective-permute-start = (bf16[1280,768]{1,0:T(8,128)(2,1)}, bf16[1280,768]{1,0:T(8,128)(2,1)}, u32[]{:S(2)}, u32[]{:S(2)}) collective-permute-start(bf16[1280,768]{1,0:T(8,128)(2,1)} %bitcast.70), channel_id=1, source_target_pairs={{0,16},{16,0},{1,17},{17,1},{2,18},{18,2},{3,19},{19,3},{4,20},{20... | collective-permute-start | bytes 5898248 | tf_op jit(solution)/shard_map/ppermute | solution.py:814
  19.2 40.3 %copy-start.14 = (f32[1,768]{1,0:T(1,128)}, f32[1,768]{1,0:T(1,128)S(1)}, u32[]{:S(2)}) copy-start(f32[1,768]{1,0:T(1,128)S(1)} %reshape.180.gain_ref) | copy-start | bytes 9220
  21.8 50.7 %copy-start.12 = (s32[320]{0:T(512)}, s32[320]{0:T(512)S(1)}, u32[]{:S(2)}) copy-start(s32[320]{0:T(512)S(1)} %fusion.9.numbers) | copy-start | bytes 3844
  21.9 1.5 copy-start.11
  57.7 45.8 %collective-permute-start.2 = (bf16[2,256,768]{2,1,0:T(8,128)(2,1)S(1)}, bf16[2,256,768]{2,1,0:T(8,128)(2,1)S(1)}, u32[]{:S(2)}, u32[]{:S(2)}) collective-permute-start(bf16[2,256,768]{2,1,0:T(8,128)(2,1)S(1)} %pad_maximum_fusion), channel_id=1, source_target_pairs={{0,16},{16,0},{1,17},{17,1},{2,18},{18,2},{3,19},{19,3},{4,20},{20... | collective-permute-start | bytes 2359304 | tf_op jit(solution)/shard_map/ppermute | solution.py:814
  67.9 4.7 %copy-start = (bf16[10,256,768]{2,1,0:T(8,128)(2,1)}, bf16[10,256,768]{2,1,0:T(8,128)(2,1)S(1)}, u32[]{:S(2)}) copy-start(bf16[10,256,768]{2,1,0:T(8,128)(2,1)S(1)} %get-tuple-element.56.q_ref) | copy-start | bytes 11796484
  67.9 4.7 %copy-start.2 = (bf16[10,256,768]{2,1,0:T(8,128)(2,1)}, bf16[10,256,768]{2,1,0:T(8,128)(2,1)S(1)}, u32[]{:S(2)}) copy-start(bf16[10,256,768]{2,1,0:T(8,128)(2,1)S(1)} %get-tuple-element.57.k_ref) | copy-start | bytes 11796484
  67.9 5.0 %copy-start.9 = (bf16[10,256,768]{2,1,0:T(8,128)(2,1)S(1)}, bf16[10,256,768]{2,1,0:T(8,128)(2,1)}, u32[]{:S(2)}) copy-start(bf16[10,256,768]{2,1,0:T(8,128)(2,1)} %get-tuple-element.59.v_ref) | copy-start | bytes 11796484
  165.6 4.4 %copy-start.18 = (bf16[5,256,768]{2,1,0:T(8,128)(2,1)S(1)}, bf16[5,256,768]{2,1,0:T(8,128)(2,1)}, u32[]{:S(2)}) copy-start(bf16[5,256,768]{2,1,0:T(8,128)(2,1)} %get-tuple-element.69) | copy-start | bytes 5898244
  168.1 1.2 collective-permute-start.1
  170.0 3.8 %copy-start.17 = (bf16[5,256,1536]{2,1,0:T(8,128)(2,1)S(1)}, bf16[5,256,1536]{2,1,0:T(8,128)(2,1)}, u32[]{:S(2)}) copy-start(bf16[5,256,1536]{2,1,0:T(8,128)(2,1)} %get-tuple-element.65.dx_ref) | copy-start | bytes 11796484
  171.4 2.3 copy-start.13
  171.5 61.9 %collective-permute-start.3 = (bf16[2,256,768]{2,1,0:T(8,128)(2,1)S(1)}, bf16[2,256,768]{2,1,0:T(8,128)(2,1)S(1)}, u32[]{:S(2)}, u32[]{:S(2)}) collective-permute-start(bf16[2,256,768]{2,1,0:T(8,128)(2,1)S(1)} %pad_maximum_fusion.1), channel_id=1, source_target_pairs={{0,16},{16,0},{1,17},{17,1},{2,18},{18,2},{3,19},{19,3},{4,20},{20... | collective-permute-start | bytes 2359304 | tf_op jit(solution)/shard_map/ppermute | solution.py:814
  173.3 61.7 %collective-permute-start.4 = (bf16[2,256,768]{2,1,0:T(8,128)(2,1)S(1)}, bf16[2,256,768]{2,1,0:T(8,128)(2,1)S(1)}, u32[]{:S(2)}, u32[]{:S(2)}) collective-permute-start(bf16[2,256,768]{2,1,0:T(8,128)(2,1)S(1)} %pad_maximum_fusion.2), channel_id=1, source_target_pairs={{0,16},{16,0},{1,17},{17,1},{2,18},{18,2},{3,19},{19,3},{4,20},{20... | collective-permute-start | bytes 2359304 | tf_op jit(solution)/shard_map/ppermute | solution.py:814
  173.8 61.4 %copy-start.6 = (bf16[10,256,768]{2,1,0:T(8,128)(2,1)S(1)}, bf16[10,256,768]{2,1,0:T(8,128)(2,1)}, u32[]{:S(2)}) copy-start(bf16[10,256,768]{2,1,0:T(8,128)(2,1)} %get-tuple-element.84.normed_ref) | copy-start | bytes 11796484
  230.1 22.8 %copy-start.10 = (bf16[10,256,768]{2,1,0:T(8,128)(2,1)}, bf16[10,256,768]{2,1,0:T(8,128)(2,1)S(1)}, u32[]{:S(2)}) copy-start(bf16[10,256,768]{2,1,0:T(8,128)(2,1)S(1)} %get-tuple-element.79.dv_ref) | copy-start | bytes 11796484
  230.1 12.2 %collective-permute-start.6 = (f32[5,10,1,256]{3,2,1,0:T(1,128)S(1)}, f32[5,10,1,256]{3,2,1,0:T(1,128)S(1)}, u32[]{:S(2)}, u32[]{:S(2)}) collective-permute-start(f32[5,10,1,256]{3,2,1,0:T(1,128)S(1)} %get-tuple-element.72), channel_id=1, source_target_pairs={{0,16},{16,0},{1,17},{17,1},{2,18},{18,2},{3,19},{19,3},{4,20},{20... | collective-permute-start | bytes 153608 | tf_op jit(solution)/shard_map/ppermute | solution.py:814
  235.1 5.4 %copy-start.19 = (bf16[5,256,768]{2,1,0:T(8,128)(2,1)}, bf16[5,256,768]{2,1,0:T(8,128)(2,1)S(1)}, u32[]{:S(2)}) copy-start(bf16[5,256,768]{2,1,0:T(8,128)(2,1)S(1)} %slice_dynamic-update-slice_fusion.branch_ref) | copy-start | bytes 5898244
  235.1 7.2 %collective-permute-start.5 = (f32[1,128]{1,0:T(1,128)S(1)}, f32[1,128]{1,0:T(1,128)S(1)}, u32[]{:S(2)}, u32[]{:S(2)}) collective-permute-start(f32[1,128]{1,0:T(1,128)S(1)} %broadcast_add_fusion), channel_id=1, source_target_pairs={{0,2},{1,3},{2,0},{3,1},{4,6},{5,7},{6,4},{7,5},{8,10},{9,11},{10,... | collective-permute-start | bytes 1544 | tf_op jit(solution)/shard_map/ppermute | solution.py:904
  235.2 10.4 %copy-start.3 = (bf16[10,256,768]{2,1,0:T(8,128)(2,1)S(1)}, bf16[10,256,768]{2,1,0:T(8,128)(2,1)}, u32[]{:S(2)}) copy-start(bf16[10,256,768]{2,1,0:T(8,128)(2,1)} %copy-done.2) | copy-start | bytes 11796484
  240.5 5.0 %copy-start.1 = (bf16[10,256,768]{2,1,0:T(8,128)(2,1)S(1)}, bf16[10,256,768]{2,1,0:T(8,128)(2,1)}, u32[]{:S(2)}) copy-start(bf16[10,256,768]{2,1,0:T(8,128)(2,1)} %copy-done) | copy-start | bytes 11796484
  241.6 32.2 %collective-permute-start.13 = (bf16[2,2,2,48,1152]{4,3,2,0,1:T(8,128)(2,1)}, bf16[2,2,2,48,1152]{4,3,2,0,1:T(8,128)(2,1)}, u32[]{:S(2)}, u32[]{:S(2)}) collective-permute-start(bf16[2,2,2,48,1152]{4,3,2,0,1:T(8,128)(2,1)} %bitcast.66), channel_id=1, source_target_pairs={{0,1},{1,0},{2,3},{3,2},{4,5},{5,4},{6,7},{7,6},{8,9},{9,8},{10,11... | collective-permute-start | bytes 2654216 | tf_op jit(solution)/shard_map/ppermute | solution.py:837
  242.3 16.8 %collective-permute-start.7 = (f32[1,128]{1,0:T(1,128)S(1)}, f32[1,128]{1,0:T(1,128)S(1)}, u32[]{:S(2)}, u32[]{:S(2)}) collective-permute-start(f32[1,128]{1,0:T(1,128)S(1)} %add.144), channel_id=1, source_target_pairs={{0,4},{1,5},{2,6},{3,7},{4,0},{5,1},{6,2},{7,3},{8,12},{9,13},{10,... | collective-permute-start | bytes 1544 | tf_op jit(solution)/shard_map/ppermute | solution.py:904
  245.5 7.4 %copy-start.8 = (bf16[768,2304]{1,0:T(8,128)(2,1)S(1)}, bf16[768,2304]{1,0:T(8,128)(2,1)}, u32[]{:S(2)}) copy-start(bf16[768,2304]{1,0:T(8,128)(2,1)} %w_ref.7) | copy-start | bytes 10616836
  252.8 6.3 %copy-start.4 = (bf16[10,256,768]{2,1,0:T(8,128)(2,1)}, bf16[10,256,768]{2,1,0:T(8,128)(2,1)S(1)}, u32[]{:S(2)}) copy-start(bf16[10,256,768]{2,1,0:T(8,128)(2,1)S(1)} %get-tuple-element.82.dk_ref) | copy-start | bytes 11796484
  252.8 6.3 %copy-start.5 = (bf16[5,256,768]{2,1,0:T(8,128)(2,1)}, bf16[5,256,768]{2,1,0:T(8,128)(2,1)S(1)}, u32[]{:S(2)}) copy-start(bf16[5,256,768]{2,1,0:T(8,128)(2,1)S(1)} %get-tuple-element.81.dq_ref) | copy-start | bytes 5898244
  259.1 4.4 %copy-start.15 = (bf16[5,256,768]{2,1,0:T(8,128)(2,1)}, bf16[5,256,768]{2,1,0:T(8,128)(2,1)S(1)}, u32[]{:S(2)}) copy-start(bf16[5,256,768]{2,1,0:T(8,128)(2,1)S(1)} %shard_map.185) | copy-start | bytes 5898244
  263.5 7.2 %copy-start.16 = (bf16[5,256,768]{2,1,0:T(8,128)(2,1)S(1)}, bf16[5,256,768]{2,1,0:T(8,128)(2,1)}, u32[]{:S(2)}) copy-start(bf16[5,256,768]{2,1,0:T(8,128)(2,1)} %copy-done.15) | copy-start | bytes 5898244
  265.7 9.6 %collective-permute-start.9 = (bf16[2,2,2,48,1152]{4,3,0,1,2:T(8,128)(2,1)}, bf16[2,2,2,48,1152]{4,3,0,1,2:T(8,128)(2,1)}, u32[]{:S(2)}, u32[]{:S(2)}) collective-permute-start(bf16[2,2,2,48,1152]{4,3,0,1,2:T(8,128)(2,1)} %bitcast.67), channel_id=1, source_target_pairs={{0,1},{1,0},{2,3},{3,2},{4,5},{5,4},{6,7},{7,6},{8,9},{9,8},{10,11... | collective-permute-start | bytes 2654216 | tf_op jit(solution)/shard_map/ppermute | solution.py:837
  265.7 4.4 %collective-permute-start.19 = (f32[1,128]{1,0:T(1,128)S(1)}, f32[1,128]{1,0:T(1,128)S(1)}, u32[]{:S(2)}, u32[]{:S(2)}) collective-permute-start(f32[1,128]{1,0:T(1,128)S(1)} %add.145), channel_id=1, source_target_pairs={{0,8},{1,9},{2,10},{3,11},{4,12},{5,13},{6,14},{7,15},{8,0},{9,1},... | collective-permute-start | bytes 1544 | tf_op jit(solution)/shard_map/ppermute | solution.py:904
  270.2 3.6 %collective-permute-start.20 = (f32[1,128]{1,0:T(1,128)S(1)}, f32[1,128]{1,0:T(1,128)S(1)}, u32[]{:S(2)}, u32[]{:S(2)}) collective-permute-start(f32[1,128]{1,0:T(1,128)S(1)} %add.165), channel_id=1, source_target_pairs={{0,16},{16,0},{1,17},{17,1},{2,18},{18,2},{3,19},{19,3},{4,20},{20... | collective-permute-start | bytes 1544 | tf_op jit(solution)/shard_map/ppermute | solution.py:904
  270.7 4.6 %copy-start.20 = (bf16[2,2,2,1,48,1152]{5,4,3,2,1,0:T(8,128)(2,1)S(1)}, bf16[2,2,2,1,48,1152]{5,4,3,2,1,0:T(8,128)(2,1)}, u32[]{:S(2)}) copy-start(bf16[2,2,2,1,48,1152]{5,4,3,2,1,0:T(8,128)(2,1)} %get-tuple-element.101) | copy-start | bytes 2654212
  270.8 46.7 %collective-permute-start.8 = (bf16[5,256,768]{2,1,0:T(8,128)(2,1)S(1)}, bf16[5,256,768]{2,1,0:T(8,128)(2,1)}, u32[]{:S(2)}, u32[]{:S(2)}) collective-permute-start(bf16[5,256,768]{2,1,0:T(8,128)(2,1)S(1)} %copy-done.16), channel_id=1, source_target_pairs={{0,16},{16,0},{1,17},{17,1},{2,18},{18,2},{3,19},{19,3},{4,20},{20... | collective-permute-start | bytes 5898248 | tf_op jit(solution)/shard_map/ppermute | solution.py:814
  275.2 20.5 %collective-permute-start.14 = (bf16[2,2,48,1152]{3,2,1,0:T(8,128)(2,1)S(1)}, bf16[2,2,48,1152]{3,2,1,0:T(8,128)(2,1)S(1)}, u32[]{:S(2)}, u32[]{:S(2)}) collective-permute-start(bf16[2,2,48,1152]{3,2,1,0:T(8,128)(2,1)S(1)} %dynamic-slice_bitcast_fusion), channel_id=1, source_target_pairs={{0,4},{1,5},{2,6},{3,7},{4,0},{5,1},{6,2},{7,3},{8,12},{9,13},{10,... | collective-permute-start | bytes 1327112 | tf_op jit(solution)/shard_map/ppermute | solution.py:837
  276.8 21.6 %collective-permute-start.10 = (bf16[2,2,48,1152]{3,2,0,1:T(8,128)(2,1)S(1)}, bf16[2,2,48,1152]{3,2,0,1:T(8,128)(2,1)S(1)}, u32[]{:S(2)}, u32[]{:S(2)}) collective-permute-start(bf16[2,2,48,1152]{3,2,0,1:T(8,128)(2,1)S(1)} %dynamic-slice_bitcast_fusion.1), channel_id=1, source_target_pairs={{0,2},{1,3},{2,0},{3,1},{4,6},{5,7},{6,4},{7,5},{8,10},{9,11},{10,... | collective-permute-start | bytes 1327112 | tf_op jit(solution)/shard_map/ppermute | solution.py:837
  295.9 12.9 %collective-permute-start.15 = (bf16[2,48,1152]{2,1,0:T(8,128)(2,1)S(1)}, bf16[2,48,1152]{2,1,0:T(8,128)(2,1)S(1)}, u32[]{:S(2)}, u32[]{:S(2)}) collective-permute-start(bf16[2,48,1152]{2,1,0:T(8,128)(2,1)S(1)} %dynamic-slice_bitcast_fusion.2), channel_id=1, source_target_pairs={{0,8},{1,9},{2,10},{3,11},{4,12},{5,13},{6,14},{7,15},{8,0},{9,1},... | collective-permute-start | bytes 663560 | tf_op jit(solution)/shard_map/ppermute | solution.py:837
  298.5 11.9 %collective-permute-start.11 = (bf16[2,48,1152]{2,1,0:T(8,128)(2,1)S(1)}, bf16[2,48,1152]{2,1,0:T(8,128)(2,1)S(1)}, u32[]{:S(2)}, u32[]{:S(2)}) collective-permute-start(bf16[2,48,1152]{2,1,0:T(8,128)(2,1)S(1)} %dynamic-slice_bitcast_fusion.3), channel_id=1, source_target_pairs={{0,4},{1,5},{2,6},{3,7},{4,0},{5,1},{6,2},{7,3},{8,12},{9,13},{10,... | collective-permute-start | bytes 663560 | tf_op jit(solution)/shard_map/ppermute | solution.py:837
  308.9 5.0 %collective-permute-start.16 = (bf16[48,1152]{1,0:T(8,128)(2,1)S(1)}, bf16[48,1152]{1,0:T(8,128)(2,1)S(1)}, u32[]{:S(2)}, u32[]{:S(2)}) collective-permute-start(bf16[48,1152]{1,0:T(8,128)(2,1)S(1)} %dynamic-slice_bitcast_fusion.4), channel_id=1, source_target_pairs={{0,2},{1,3},{2,0},{3,1},{4,6},{5,7},{6,4},{7,5},{8,10},{9,11},{10,... | collective-permute-start | bytes 331784 | tf_op jit(solution)/shard_map/ppermute | solution.py:837
  310.5 6.9 %collective-permute-start.12 = (bf16[48,1152]{1,0:T(8,128)(2,1)S(1)}, bf16[48,1152]{1,0:T(8,128)(2,1)S(1)}, u32[]{:S(2)}, u32[]{:S(2)}) collective-permute-start(bf16[48,1152]{1,0:T(8,128)(2,1)S(1)} %dynamic-slice_bitcast_fusion.5), channel_id=1, source_target_pairs={{0,8},{1,9},{2,10},{3,11},{4,12},{5,13},{6,14},{7,15},{8,0},{9,1},... | collective-permute-start | bytes 331784 | tf_op jit(solution)/shard_map/ppermute | solution.py:837
  317.5 21.6 %copy-start.22 = (bf16[1,432,768]{2,1,0:T(8,128)(2,1)S(1)}, bf16[1,432,768]{2,1,0:T(8,128)(2,1)}, u32[]{:S(2)}) copy-start(bf16[1,432,768]{2,1,0:T(8,128)(2,1)} %reduce-scatter.2.cloned.1.call-done) | copy-start | bytes 1990660
  317.5 14.1 %collective-permute-start.17 = (bf16[48,2304]{1,0:T(8,128)(2,1)S(1)}, bf16[48,2304]{1,0:T(8,128)(2,1)S(1)}, u32[]{:S(2)}, u32[]{:S(2)}) collective-permute-start(bf16[48,2304]{1,0:T(8,128)(2,1)S(1)} %pad_maximum_fusion.3), channel_id=1, source_target_pairs={{0,16},{16,0},{1,17},{17,1},{2,18},{18,2},{3,19},{19,3},{4,20},{20... | collective-permute-start | bytes 663560 | tf_op jit(solution)/shard_map/ppermute | solution.py:814
  319.0 20.2 %collective-permute-start.18 = (bf16[432,768]{1,0:T(8,128)(2,1)}, bf16[432,768]{1,0:T(8,128)(2,1)S(1)}, u32[]{:S(2)}, u32[]{:S(2)}) collective-permute-start(bf16[432,768]{1,0:T(8,128)(2,1)} %bitcast.78), channel_id=1, source_target_pairs={{0,16},{16,0},{1,17},{17,1},{2,18},{18,2},{3,19},{19,3},{4,20},{20... | collective-permute-start | bytes 1990664 | tf_op jit(solution)/shard_map/ppermute | solution.py:814
  341.0 2.0 copy-start.21
Sparse Core Ops, SparseCore 0:
  165.7 128.2 reduce-scatter.1
